TPU v7x, 512 devices: a whole 4x8x8 slice. The times are simulated.
512 devices in a mesh: psg: 64 (over z, y), pb: 4 (over x), rep: 2 (over core).
Axes of the slice: x: 4, y: 8, z: 8, core: 2. Of those that a mesh axis runs over, the one named last changes fastest.
Arguments:
- queries: bfloat16 [512, 2048], P(None, ('pb', 'rep'))
- prefixes: bfloat16 [2048, 32, 2048], P('psg', None, ('pb', 'rep')), may hold values from -6 to 6
- owner: int32 [2048], P('psg'), may hold values from 0 to 16, as said below
- key_weight: bfloat16 [2048, 2048], P(None, ('pb', 'rep')), may hold values from -0.125 to 0.125
- value_weight: bfloat16 [2048, 2048], P(None, ('pb', 'rep')), may hold values from -0.125 to 0.125
- cotangent: bfloat16 [512, 2048], P(None, ('pb', 'rep')), may hold values from -6 to 6
Outputs:
- attended: bfloat16 [512, 2048], P(None, ('pb', 'rep'))
- query_grad: bfloat16 [512, 2048], P(None, ('pb', 'rep'))
Inputs may be any that keep to these rules, and one draw needn't show every extreme that they name: owner[j] is the question of slot j; the value 16 marks an empty slot. Slots 0 to 15 hold every question once, the last slot is empty, and the other slots follow a skewed law over the questions.
All inputs are finite; a program needn't handle non-finite values.
Results may differ from a plain program's by a relative error of at most 0.025.
The roundings to bfloat16 on the way count: a program that leaves them out, or rounds other values in their place, can miss the bound.
Values may be sent and summed in bfloat16 or wider, within the bound.
No kernel may reach another device: no remote copies, remote signals or barrier semaphores. Data moves between devices by JAX's collectives and lax.ppermute only.
A program may use at most 64 MiB of HBM per device.

v0:
```python
import jax
import jax.numpy as jnp
from jax import lax
from jax.sharding import PartitionSpec as P

HDIM = 64
TGT = 32


masked_value = -1e30


def slot_lookup(table, owner, fill_value):
    extra = jnp.full((1,) + table.shape[1:], fill_value, table.dtype)
    return jnp.take(jnp.concatenate([table, extra], axis=0), owner, axis=0)


def body(queries, prefixes, owner, key_weight, value_weight, cotangent):
    gathered = lax.all_gather(prefixes, ("pb", "rep"), axis=2, tiled=True)
    slot_count, vector_count, feature_count = gathered.shape
    passage_rows = gathered.reshape(slot_count * vector_count, feature_count)
    key_rows = jnp.dot(passage_rows, key_weight, preferred_element_type=jnp.float32).astype(
        jnp.bfloat16
    )
    value_rows = jnp.dot(passage_rows, value_weight, preferred_element_type=jnp.float32).astype(
        jnp.bfloat16
    )
    row_count, col_count = queries.shape
    head_count = col_count // HDIM
    question_count = row_count // TGT
    key_slots = key_rows.reshape(slot_count, vector_count, head_count, HDIM)
    value_slots = value_rows.reshape(slot_count, vector_count, head_count, HDIM)
    query_slots = slot_lookup(queries.reshape(question_count, TGT, head_count, HDIM), owner, 0.0)
    grad_slots = slot_lookup(cotangent.reshape(question_count, TGT, head_count, HDIM), owner, 0.0)
    grad_heads = cotangent.reshape(row_count, head_count, HDIM)
    slot_live = (owner < question_count)[:, None, None, None]
    matches = owner[:, None] == jnp.arange(question_count, dtype=jnp.int32)[None, :]
    one_hot = matches.astype(jnp.float32)
    scores = jnp.einsum(
        "sthd,sphd->shtp", query_slots, key_slots, preferred_element_type=jnp.float32
    )
    scores = jnp.where(slot_live, scores, masked_value)
    slot_max = jnp.max(scores, axis=3)
    question_max = jnp.max(
        jnp.where(matches[:, :, None, None], slot_max[:, None], masked_value), axis=0
    )
    local_max = jnp.transpose(question_max, (1, 0, 2)).reshape(head_count, row_count)
    row_max = lax.pmax(local_max, "psg")
    max_table = jnp.transpose(row_max.reshape(head_count, question_count, TGT), (1, 0, 2))
    slot_rowmax = slot_lookup(max_table, owner, 0.0)
    exponent = jnp.where(slot_live, jnp.exp(scores - slot_rowmax[:, :, :, None]), jnp.float32(0.0))
    slot_totals = jnp.sum(exponent, axis=3)
    local_totals = jnp.einsum(
        "sq,sht->qth", one_hot, slot_totals, precision=lax.Precision.HIGHEST
    ).reshape(row_count, head_count)
    slot_summed = jnp.einsum(
        "shtp,sphd->sthd",
        exponent.astype(jnp.bfloat16),
        value_slots,
        preferred_element_type=jnp.float32,
    ).reshape(slot_count, TGT * col_count)
    summed = jnp.dot(one_hot.T, slot_summed, precision=lax.Precision.HIGHEST).reshape(
        row_count, col_count
    )
    summed, totals = lax.psum((summed, local_totals), "psg")
    attended = (
        (summed.reshape(row_count, head_count, HDIM) / totals[:, :, None])
        .astype(jnp.bfloat16)
        .reshape(row_count, col_count)
    )
    attended_heads = attended.reshape(row_count, head_count, HDIM).astype(jnp.float32)
    correction = jnp.sum(grad_heads.astype(jnp.float32) * attended_heads, axis=2)
    slot_corr = jnp.transpose(
        slot_lookup(correction.reshape(question_count, TGT, head_count), owner, 0.0), (0, 2, 1)
    )
    slot_tot = jnp.transpose(
        slot_lookup(totals.reshape(question_count, TGT, head_count), owner, 1.0), (0, 2, 1)
    )
    product = jnp.einsum(
        "sthd,sphd->shtp", grad_slots, value_slots, preferred_element_type=jnp.float32
    )
    grad_scores = (
        exponent / slot_tot[:, :, :, None] * (product - slot_corr[:, :, :, None])
    ).astype(jnp.bfloat16)
    slot_grad = jnp.einsum(
        "shtp,sphd->sthd", grad_scores, key_slots, preferred_element_type=jnp.float32
    ).reshape(slot_count, TGT * col_count)
    local_grad = jnp.dot(one_hot.T, slot_grad, precision=lax.Precision.HIGHEST).reshape(
        row_count, col_count
    )
    query_grad = lax.psum(local_grad, "psg").astype(jnp.bfloat16)
    return (attended, query_grad)


def solution(mesh):
    placed = (
        P(None, ("pb", "rep")),
        P("psg", None, ("pb", "rep")),
        P("psg"),
        P(None, ("pb", "rep")),
        P(None, ("pb", "rep")),
        P(None, ("pb", "rep")),
    )
    return jax.shard_map(
        body,
        mesh=mesh,
        in_specs=placed,
        out_specs=(P(None, ("pb", "rep")), P(None, ("pb", "rep"))),
        check_vma=False,
    )
```

profile of v0, /device:TPU:6, one launch (start us, length us, event | category | flops | bytes accessed | tf_op | source)
XLA Modules:
  0.0 818.3 jit_solution(11769542194474999594)
XLA Ops:
  7.2 0.7 all-gather.2.cloned.1.call-update
  8.0 1.2 reshape.99
  9.6 1.7 gather_fusion.1
  11.3 44.2 %all-gather.2.cloned.1.call-done = bf16[32,32,2048]{2,1,0:T(8,128)(2,1)} async-done(((bf16[32,32,256]{2,1,0:T(8,128)(2,1)}), bf16[32,32,2048]{2,1,0:T(8,128)(2,1)}) %all-gather.2.cloned.1.call-update) | async-done | bytes 4194320 | tf_op jit(solution)/shard_map/all_gather | solution.py:19
  55.5 3.4 convolution_convert_fusion
  59.0 1.4 reshape.100
  60.3 2.3 select_reduce_fusion
  62.9 280.4 %pmax.7 = f32[16,4,32]{2,1,0:T(4,128)S(1)} all-reduce(f32[16,4,32]{2,1,0:T(4,128)S(1)} %copy.115), channel_id=1, replica_groups=mesh['psg'=64,'pb'=4,'rep'=2] {'psg'}, use_global_device_ids=true, to_apply=%region_2.4 | all-reduce | flops 2048 | bytes 16384 | tf_op jit(solution)/shard_map/pmax | solution.py:48
  343.3 0.6 gather_fusion
  344.0 4.6 convolution_convert_fusion.1
  348.6 2.8 reshape.98
  351.3 2.0 convolution_bitcast_fusion.1
  353.4 3.1 copy.118
  356.5 3.5 reshape.103
  360.1 2.5 fusion.33
  362.6 1.9 reshape.104
  364.5 2.0 copy.119
  366.6 0.8 copy.124
  367.4 1.0 reshape.107
  368.5 1.2 copy.122
  369.7 0.9 concatenate.18
  370.6 2.7 gather_fusion.3
  373.3 0.8 fusion
  374.4 140.4 %psum.22 = f32[512,4]{0,1:T(4,128)S(1)} all-reduce(f32[512,4]{0,1:T(4,128)S(1)} %reshape.105), channel_id=1, replica_groups=mesh['psg'=64,'pb'=4,'rep'=2] {'psg'}, use_global_device_ids=true, to_apply=%region_5.7 | all-reduce | flops 2048 | bytes 16384 | tf_op jit(solution)/shard_map/psum | solution.py:65
  514.9 0.6 gather_fusion.2
  515.9 1.2 fusion.25
  517.9 4.5 convolution_bitcast_fusion
  522.4 3.4 copy.129
  525.7 2.5 reshape.110
  528.2 1.8 fusion.32
  530.1 280.5 %all-reduce.9 = bf16[512,256]{1,0:T(8,128)(2,1)} all-reduce(f32[512,256]{1,0:T(8,128)S(1)} %reshape.111), channel_id=1, replica_groups=mesh['psg'=64,'pb'=4,'rep'=2] {'psg'}, use_global_device_ids=true, to_apply=%region_7.10 | all-reduce | flops 131072 | bytes 786432 | tf_op jit(solution)/shard_map/psum | solution.py:91
  810.6 0.8 copy.130
  (41 shorter events, 2.5 us)
Async XLA Ops:
  7.2 48.4 %copy-start = (bf16[2048,256]{1,0:T(8,128)(2,1)S(1)}, bf16[2048,256]{1,0:T(8,128)(2,1)}, u32[]{:S(2)}) copy-start(bf16[2048,256]{1,0:T(8,128)(2,1)} %param.13) | copy-start | bytes 3145732
  7.2 2.1 copy-start.6
  7.2 48.3 %all-gather.2.cloned.1.call-start = ((), (), s32[]{:S(2)}) async-start(), calls=%async_computation | async-start | bytes 4718592 | tf_op jit(solution)/shard_map/all_gather | solution.py:19
  7.9 508.0 %all-reduce.8.cloned.1.call-start = ((), (), s32[]{:S(2)}) async-start(), calls=%async_computation.1 | async-start | bytes 1048576 | tf_op jit(solution)/shard_map/psum | solution.py:65
  344.0 7.3 copy-start.4
  360.1 6.5 copy-start.2
  368.5 4.8 copy-start.5
  373.3 142.6 %copy-start.3 = (bf16[512,256]{0,1:T(8,128)(2,1)S(1)}, bf16[512,256]{0,1:T(8,128)(2,1)}, u32[]{:S(2)}) copy-start(bf16[512,256]{0,1:T(8,128)(2,1)} %copy.124) | copy-start | bytes 786436
  528.2 282.3 %copy-start.1 = (f32[512,256]{0,1:T(8,128)S(1)}, f32[512,256]{0,1:T(8,128)}, u32[]{:S(2)}) copy-start(f32[512,256]{0,1:T(8,128)} %all-reduce.8.cloned.1.call-done) | copy-start | bytes 1572868
Sparse Core Ops, SparseCore 0:
  10.1 45.3 all-gather.1
  366.7 149.1 all-reduce.7
where the time goes:
time: 819 us; the launch traced here: 818 us
  blocking collectives  701 us (86%)
  waiting for transfers between devices  45.3 us (6%)
  local copies, waits for them, and re-layouts  33.7 us (4%)
  matrix products  21.2 us (3%)
  between operations  14.3 us (2%)
    psum x1, blocking collectives, body(): query_grad = lax.psum(local_grad, 'psg').astype(jnp.bfloat16)  280 us
    pmax x1, blocking collectives, body(): row_max = lax.pmax(local_max, 'psg')  280 us
    psum x1, blocking collectives, body(): summed, totals = lax.psum((summed, local_totals), 'psg')  140 us
    all_gather x1, waiting for transfers between devices, body(): gathered = lax.all_gather(prefixes, ('pb', 'rep'), axis=2, tiled=True)  44.2 us
  transfers between devices with their start and end apart: 2, of which 2 were waited for; matrix products, arithmetic and copies ran while one was open for 1% of the time, Pallas kernels for 0%

commit v1 on v0

v1 whole, which is shorter than its diff:
```python
import jax
import jax.numpy as jnp
from jax import lax
from jax.experimental import pallas as pl
from jax.experimental.pallas import tpu as pltpu
from jax.sharding import PartitionSpec as P

HDIM = 64
TGT = 32
PL = 32
QUESTIONS = 16
PARTS = 3

masked_value = -1e30

f32 = jnp.float32
bf16 = jnp.bfloat16
NT = (((1,), (1,)), ((), ()))


def split_parts(x):
    first = x.astype(bf16)
    rest = x - first.astype(f32)
    second = rest.astype(bf16)
    third = (rest - second.astype(f32)).astype(bf16)
    return first.astype(f32), second.astype(f32), third.astype(f32)


def per_head(x, width, reduce, fill):
    lane_head = lax.broadcasted_iota(jnp.int32, x.shape, x.ndim - 1) // width
    out = jnp.zeros_like(x)
    for head in range(x.shape[-1] // width):
        one = reduce(jnp.where(lane_head == head, x, fill), axis=-1, keepdims=True)
        out = jnp.where(lane_head == head, one, out)
    return out


def local_kernel(pieces, *refs):
    block_ref, owner_ref = refs[:2]
    x_refs = refs[2 : 2 + pieces]
    (wk_ref, wv_ref, q_ref, c_ref, out_ref, kblk, vblk, score, product, top, total, dots, corr, acc_v, acc_k) = refs[
        2 + pieces :
    ]
    slots = owner_ref.shape[0]
    half = slots // 2
    heads = q_ref.shape[1] // HDIM
    keys = heads * PL

    top[...] = jnp.full_like(top, masked_value)
    total[...] = jnp.zeros_like(total)
    dots[...] = jnp.zeros_like(dots)
    acc_v[...] = jnp.zeros_like(acc_v)
    acc_k[...] = jnp.zeros_like(acc_k)

    blocks = 8
    wide = wk_ref.shape[0] // blocks

    def weight(ref):
        rows = [ref[pl.ds(pl.multiple_of(block_ref[j] * wide, wide), wide), :] for j in range(blocks)]
        return jnp.concatenate(rows, axis=0)

    on_diagonal = (
        lax.broadcasted_iota(jnp.int32, (keys, heads * HDIM), 0) // PL
        == lax.broadcasted_iota(jnp.int32, (keys, heads * HDIM), 1) // HDIM
    ).astype(f32).astype(bf16)

    group = 8
    for start in range(0, slots, group):
        side = 0 if start < half else 1
        low = (start - side * half) * PL
        rows = jnp.concatenate([x_refs[j * 2 + side][low : low + group * PL, :] for j in range(blocks)], axis=1)
        key_rows = jnp.dot(rows, weight(wk_ref), preferred_element_type=f32).astype(bf16)
        value_rows = jnp.dot(rows, weight(wv_ref), preferred_element_type=f32).astype(bf16)
        for i in range(group):
            slot = start + i
            kb = jnp.concatenate([key_rows[i * PL : (i + 1) * PL]] * heads, axis=0) * on_diagonal
            vb = jnp.concatenate([value_rows[i * PL : (i + 1) * PL]] * heads, axis=0) * on_diagonal
            kblk[slot] = kb
            vblk[slot] = vb
            o = owner_ref[slot]
            at = pl.ds(pl.multiple_of(jnp.minimum(o, QUESTIONS - 1) * TGT, TGT), TGT)
            s = lax.dot_general(q_ref[at, :], kb, NT, preferred_element_type=f32)
            score[slot] = s
            product[slot] = lax.dot_general(c_ref[at, :], vb, NT, preferred_element_type=f32)
            top[o] = jnp.maximum(top[o], s)

    for q in range(QUESTIONS):
        top[q] = per_head(top[q], PL, jnp.max, masked_value)

    for slot in range(slots):
        o = owner_ref[slot]
        e = jnp.exp(score[slot] - top[o])
        score[slot] = e
        total[o] = total[o] + e
        dots[o] = dots[o] + e * product[slot]

    for q in range(QUESTIONS):
        t = per_head(total[q], PL, jnp.sum, 0.0)
        d = per_head(dots[q], PL, jnp.sum, 0.0)
        total[q] = t
        corr[q] = jnp.where(t > 0.0, d / jnp.where(t > 0.0, t, 1.0), 0.0)
    corr[QUESTIONS] = jnp.zeros_like(corr[QUESTIONS])

    for slot in range(slots):
        o = owner_ref[slot]
        e = score[slot]
        g = e * (product[slot] - corr[o])
        both = jnp.concatenate([e, g], axis=0).astype(bf16)
        acc_v[o] = acc_v[o] + jnp.dot(both[:TGT], vblk[slot], preferred_element_type=f32)
        acc_k[o] = acc_k[o] + jnp.dot(both, kblk[slot], preferred_element_type=f32)

    cols = heads * HDIM
    part = lax.broadcasted_iota(jnp.int32, (TGT, keys), 1) % PL
    for q in range(QUESTIONS):
        at = slice(q * TGT, (q + 1) * TGT)
        out_ref[at, 0:cols] = acc_v[q].astype(bf16)
        out_ref[at, cols : 2 * cols] = acc_k[q, TGT:, :].astype(bf16)
        out_ref[at, 2 * cols : 3 * cols] = acc_k[q, :TGT, :].astype(bf16)
        extra = jnp.zeros((TGT, keys), f32)
        pieces_of = split_parts(top[q]) + split_parts(total[q]) + split_parts(corr[q])
        for n, piece in enumerate(pieces_of):
            extra = jnp.where(part == n, piece, extra)
        out_ref[at, 3 * cols :] = extra.astype(bf16)


def final_kernel(r_ref, c_ref, out_ref):
    rows, cols = c_ref.shape
    heads = cols // HDIM
    keys = heads * PL
    devices = r_ref.shape[0] // rows
    lane = lax.broadcasted_iota(jnp.int32, (keys, 3 * cols), 0)
    spot = lax.broadcasted_iota(jnp.int32, (keys, 3 * cols), 1)
    pick = (lane // PL == (spot % cols) // HDIM) & ((lane % PL) // PARTS == spot // cols)
    pick = pick.astype(f32).astype(bf16)
    wide = jnp.dot(r_ref[:, 3 * cols :], pick, preferred_element_type=f32).reshape(devices, rows, 3 * cols)
    top = wide[:, :, 0:cols]
    weight = jnp.exp(top - jnp.max(top, axis=0, keepdims=True))
    total = jnp.sum(weight * wide[:, :, cols : 2 * cols], axis=0)

    def read(n):
        return r_ref[:, n * cols : (n + 1) * cols].astype(f32).reshape(devices, rows, cols)

    summed = jnp.sum(weight * read(0), axis=0)
    attended = (summed / total).astype(bf16).astype(f32)
    corr = per_head(c_ref[...] * attended, HDIM, jnp.sum, 0.0)
    shift = wide[:, :, 2 * cols :] - corr[None]
    grad = jnp.sum(weight * (read(1) + shift * read(2)), axis=0) / total
    both = jnp.concatenate([attended, grad], axis=1)
    two = jnp.concatenate([both, both], axis=0).astype(bf16)
    for n in range(devices // 2):
        out_ref[2 * rows * n : 2 * rows * (n + 1), :] = two


def gather(x):
    n = lax.axis_size("pb")
    right = [(i, (i + 1) % n) for i in range(n)]
    left = [(i, (i - 1) % n) for i in range(n)]
    swap = [(0, 1), (1, 0)]
    half = x.shape[0] // 2
    a, b = x[:half], x[half:]
    left_a = lax.ppermute(a, "pb", right)
    right_b = lax.ppermute(b, "pb", left)
    left_b = lax.ppermute(b, "pb", right)
    right_a = lax.ppermute(a, "pb", left)
    far_a = lax.ppermute(left_a, "pb", right)
    far_b = lax.ppermute(right_b, "pb", left)
    pb, rep = lax.axis_index("pb"), lax.axis_index("rep")
    out = []
    for shift, first, second in ((0, a, b), (n - 1, left_a, left_b), (1, right_a, right_b), (2, far_a, far_b)):
        place = (pb + shift) % n
        out.append((place * 2 + rep, first, second))
        out.append((place * 2 + 1 - rep, lax.ppermute(first, "rep", swap), lax.ppermute(second, "rep", swap)))
    return out


def body(queries, prefixes, owner, key_weight, value_weight, cotangent):
    slots, vectors, features = prefixes.shape
    rows, cols = queries.shape
    heads = cols // HDIM
    keys = heads * PL
    devices = lax.axis_size("psg")
    own = rows // devices

    parts = gather(prefixes.reshape(slots * vectors, features))
    block = jnp.stack([p[0] for p in parts]).astype(jnp.int32)
    pieces = [p for part in parts for p in part[1:]]
    smem = pl.BlockSpec(memory_space=pltpu.SMEM)
    vmem = pl.BlockSpec(memory_space=pltpu.VMEM)
    payload = pl.pallas_call(
        lambda *refs: local_kernel(len(pieces), *refs),
        out_shape=jax.ShapeDtypeStruct((rows, 3 * cols + keys), bf16),
        in_specs=[smem, smem] + [vmem] * (len(pieces) + 4),
        out_specs=vmem,
        scratch_shapes=[
            pltpu.VMEM((slots, keys, cols), bf16),
            pltpu.VMEM((slots, keys, cols), bf16),
            pltpu.VMEM((slots, TGT, keys), f32),
            pltpu.VMEM((slots, TGT, keys), f32),
            pltpu.VMEM((QUESTIONS + 1, TGT, keys), f32),
            pltpu.VMEM((QUESTIONS + 1, TGT, keys), f32),
            pltpu.VMEM((QUESTIONS + 1, TGT, keys), f32),
            pltpu.VMEM((QUESTIONS + 1, TGT, keys), f32),
            pltpu.VMEM((QUESTIONS + 1, TGT, cols), f32),
            pltpu.VMEM((QUESTIONS + 1, 2 * TGT, cols), f32),
        ],
        compiler_params=pltpu.CompilerParams(vmem_limit_bytes=48 * 1024 * 1024),
        name="local_sums",
    )(block, owner, *pieces, key_weight, value_weight, queries, cotangent)

    received = lax.all_to_all(payload, "psg", 0, 0, tiled=True)
    own_cotangent = lax.dynamic_slice_in_dim(cotangent, lax.axis_index("psg") * own, own, 0).astype(f32)
    finished = pl.pallas_call(
        final_kernel,
        out_shape=jax.ShapeDtypeStruct((rows, 2 * cols), bf16),
        in_specs=[vmem, vmem],
        out_specs=vmem,
        compiler_params=pltpu.CompilerParams(vmem_limit_bytes=48 * 1024 * 1024),
        name="final_sums",
    )(received, own_cotangent)
    outputs = lax.all_to_all(finished, "psg", 0, 0, tiled=True)
    return outputs[:, :cols], outputs[:, cols:]


def solution(mesh):
    placed = (
        P(None, ("pb", "rep")),
        P("psg", None, ("pb", "rep")),
        P("psg"),
        P(None, ("pb", "rep")),
        P(None, ("pb", "rep")),
        P(None, ("pb", "rep")),
    )
    return jax.shard_map(
        body,
        mesh=mesh,
        in_specs=placed,
        out_specs=(P(None, ("pb", "rep")), P(None, ("pb", "rep"))),
        check_vma=False,
    )
```

time: 819 us -> 122 us (0.15)
  the two profiles are of different devices: /device:TPU:6 before, /device:TPU:8 now
where the time goes in v1:
time: 122 us; the launch traced here: 121 us
  starting transfers between devices  55.1 us (45%)
  waiting for transfers between devices  28.2 us (23%)
  blocking collectives  25.4 us (21%)
  Pallas kernels  9.77 us (8%)
  local copies, waits for them, and re-layouts  2.04 us (2%)
    all_to_all x1, waiting for transfers between devices, body(): received = lax.all_to_all(payload, 'psg', 0, 0, tiled=True)  27 us
    all_to_all x1, blocking collectives, body(): outputs = lax.all_to_all(finished, 'psg', 0, 0, tiled=True)  25.4 us
    all_to_all x1, starting transfers between devices, body(): received = lax.all_to_all(payload, 'psg', 0, 0, tiled=True)  16.6 us
    ppermute x4, starting transfers between devices, gather(): lax.ppermute(second, 'rep', swap)  9.14 us
    pallas_call x1, Pallas kernels, body(): pl.pallas_call(lambda *refs: local_kernel(len(pieces), *refs), out_shape=...  9.1 us
    ppermute x4, starting transfers between devices, gather(): lax.ppermute(first, 'rep', swap)  8.17 us
    ppermute x1, starting transfers between devices, gather(): far_b = lax.ppermute(right_b, 'pb', left)  5.13 us
    ppermute x1, starting transfers between devices, gather(): right_a = lax.ppermute(a, 'pb', left)  4.86 us
  transfers between devices with their start and end apart: 15, of which 2 were waited for; matrix products, arithmetic and copies ran while one was open for 0% of the time, Pallas kernels for 0%

profile of v1, /device:TPU:8, one launch (start us, length us, event | category | flops | bytes accessed | tf_op | source)
XLA Modules:
  0.0 121.4 jit_solution(656686774145205040)
XLA Ops:
  0.6 1.1 fusion.1
  1.8 3.4 %collective-permute-start.2 = (bf16[512,256]{1,0:T(8,128)(2,1)S(1)}, bf16[512,256]{1,0:T(8,128)(2,1)S(1)}, u32[]{:S(2)}, u32[]{:S(2)}) collective-permute-start(bf16[512,256]{1,0:T(8,128)(2,1)S(1)} %bitcast.20), channel_id=1, source_target_pairs={{0,2},{2,4},{4,6},{6,0},{1,3},{3,5},{5,7},{7,1},{8,10},{10,12},{12... | collective-permute-start | bytes 786440 | tf_op jit(solution)/shard_map/ppermute | solution.py:161
  5.2 3.7 %collective-permute-start.7 = (bf16[512,256]{1,0:T(8,128)(2,1)S(1)}, bf16[512,256]{1,0:T(8,128)(2,1)S(1)}, u32[]{:S(2)}, u32[]{:S(2)}) collective-permute-start(bf16[512,256]{1,0:T(8,128)(2,1)S(1)} %bitcast.16), channel_id=1, source_target_pairs={{0,6},{2,0},{4,2},{6,4},{1,7},{3,1},{5,3},{7,5},{8,14},{10,8},{12,... | collective-permute-start | bytes 786440 | tf_op jit(solution)/shard_map/ppermute | solution.py:162
  8.8 2.2 %collective-permute-start.3 = (bf16[512,256]{1,0:T(8,128)(2,1)S(1)}, bf16[512,256]{1,0:T(8,128)(2,1)S(1)}, u32[]{:S(2)}, u32[]{:S(2)}) collective-permute-start(bf16[512,256]{1,0:T(8,128)(2,1)S(1)} %bitcast.17), channel_id=1, source_target_pairs={{0,2},{2,4},{4,6},{6,0},{1,3},{3,5},{5,7},{7,1},{8,10},{10,12},{12... | collective-permute-start | bytes 786440 | tf_op jit(solution)/shard_map/ppermute | solution.py:163
  11.0 4.9 %collective-permute-start.6 = (bf16[512,256]{1,0:T(8,128)(2,1)S(1)}, bf16[512,256]{1,0:T(8,128)(2,1)S(1)}, u32[]{:S(2)}, u32[]{:S(2)}) collective-permute-start(bf16[512,256]{1,0:T(8,128)(2,1)S(1)} %bitcast.21), channel_id=1, source_target_pairs={{0,6},{2,0},{4,2},{6,4},{1,7},{3,1},{5,3},{7,5},{8,14},{10,8},{12,... | collective-permute-start | bytes 786440 | tf_op jit(solution)/shard_map/ppermute | solution.py:164
  15.9 1.9 %collective-permute-start = (bf16[512,256]{1,0:T(8,128)(2,1)S(1)}, bf16[512,256]{1,0:T(8,128)(2,1)S(1)}, u32[]{:S(2)}, u32[]{:S(2)}) collective-permute-start(bf16[512,256]{1,0:T(8,128)(2,1)S(1)} %bitcast.22), channel_id=1, source_target_pairs={{0,1},{1,0},{2,3},{3,2},{4,5},{5,4},{6,7},{7,6},{8,9},{9,8},{10,11... | collective-permute-start | bytes 786440 | tf_op jit(solution)/shard_map/ppermute | solution.py:172
  17.8 0.0 collective-permute-done.2.refs_6_
  17.8 2.4 %collective-permute-start.1 = (bf16[512,256]{1,0:T(8,128)(2,1)S(1)}, bf16[512,256]{1,0:T(8,128)(2,1)S(1)}, u32[]{:S(2)}, u32[]{:S(2)}) collective-permute-start(bf16[512,256]{1,0:T(8,128)(2,1)S(1)} %bitcast.18), channel_id=1, source_target_pairs={{0,1},{1,0},{2,3},{3,2},{4,5},{5,4},{6,7},{7,6},{8,9},{9,8},{10,11... | collective-permute-start | bytes 786440 | tf_op jit(solution)/shard_map/ppermute | solution.py:172
  20.3 0.0 collective-permute-done.7.refs_11_
  20.3 1.9 %collective-permute-start.10 = (bf16[512,256]{1,0:T(8,128)(2,1)S(1)}, bf16[512,256]{1,0:T(8,128)(2,1)S(1)}, u32[]{:S(2)}, u32[]{:S(2)}) collective-permute-start(bf16[512,256]{1,0:T(8,128)(2,1)S(1)} %collective-permute-done.2.refs_6_), channel_id=1, source_target_pairs={{0,2},{2,4},{4,6},{6,0},{1,3},{3,5},{5,7},{7,1},{8,10},{10,12},{12... | collective-permute-start | bytes 786440 | tf_op jit(solution)/shard_map/ppermute | solution.py:165
  22.2 5.1 %collective-permute-start.11 = (bf16[512,256]{1,0:T(8,128)(2,1)S(1)}, bf16[512,256]{1,0:T(8,128)(2,1)S(1)}, u32[]{:S(2)}, u32[]{:S(2)}) collective-permute-start(bf16[512,256]{1,0:T(8,128)(2,1)S(1)} %collective-permute-done.7.refs_11_), channel_id=1, source_target_pairs={{0,6},{2,0},{4,2},{6,4},{1,7},{3,1},{5,3},{7,5},{8,14},{10,8},{12,... | collective-permute-start | bytes 786440 | tf_op jit(solution)/shard_map/ppermute | solution.py:166
  27.4 0.0 collective-permute-done.6.refs_10_
  27.4 1.9 %collective-permute-start.4 = (bf16[512,256]{1,0:T(8,128)(2,1)S(1)}, bf16[512,256]{1,0:T(8,128)(2,1)S(1)}, u32[]{:S(2)}, u32[]{:S(2)}) collective-permute-start(bf16[512,256]{1,0:T(8,128)(2,1)S(1)} %collective-permute-done.2.refs_6_), channel_id=1, source_target_pairs={{0,1},{1,0},{2,3},{3,2},{4,5},{5,4},{6,7},{7,6},{8,9},{9,8},{10,11... | collective-permute-start | bytes 786440 | tf_op jit(solution)/shard_map/ppermute | solution.py:172
  29.3 2.4 %collective-permute-start.9 = (bf16[512,256]{1,0:T(8,128)(2,1)S(1)}, bf16[512,256]{1,0:T(8,128)(2,1)}, u32[]{:S(2)}, u32[]{:S(2)}) collective-permute-start(bf16[512,256]{1,0:T(8,128)(2,1)S(1)} %collective-permute-done.7.refs_11_), channel_id=1, source_target_pairs={{0,1},{1,0},{2,3},{3,2},{4,5},{5,4},{6,7},{7,6},{8,9},{9,8},{10,11... | collective-permute-start | bytes 786440 | tf_op jit(solution)/shard_map/ppermute | solution.py:172
  31.7 0.0 collective-permute-done.1.refs_5_
  31.7 1.9 %collective-permute-start.5 = (bf16[512,256]{1,0:T(8,128)(2,1)S(1)}, bf16[512,256]{1,0:T(8,128)(2,1)}, u32[]{:S(2)}, u32[]{:S(2)}) collective-permute-start(bf16[512,256]{1,0:T(8,128)(2,1)S(1)} %collective-permute-done.3.refs_7_), channel_id=1, source_target_pairs={{0,1},{1,0},{2,3},{3,2},{4,5},{5,4},{6,7},{7,6},{8,9},{9,8},{10,11... | collective-permute-start | bytes 786440 | tf_op jit(solution)/shard_map/ppermute | solution.py:172
  33.7 0.0 collective-permute-done.10.refs_14_
  33.7 2.4 %collective-permute-start.8 = (bf16[512,256]{1,0:T(8,128)(2,1)S(1)}, bf16[512,256]{1,0:T(8,128)(2,1)}, u32[]{:S(2)}, u32[]{:S(2)}) collective-permute-start(bf16[512,256]{1,0:T(8,128)(2,1)S(1)} %collective-permute-done.6.refs_10_), channel_id=1, source_target_pairs={{0,1},{1,0},{2,3},{3,2},{4,5},{5,4},{6,7},{7,6},{8,9},{9,8},{10,11... | collective-permute-start | bytes 786440 | tf_op jit(solution)/shard_map/ppermute | solution.py:172
  36.1 1.9 %collective-permute-start.12 = (bf16[512,256]{1,0:T(8,128)(2,1)S(1)}, bf16[512,256]{1,0:T(8,128)(2,1)}, u32[]{:S(2)}, u32[]{:S(2)}) collective-permute-start(bf16[512,256]{1,0:T(8,128)(2,1)S(1)} %collective-permute-done.10.refs_14_), channel_id=1, source_target_pairs={{0,1},{1,0},{2,3},{3,2},{4,5},{5,4},{6,7},{7,6},{8,9},{9,8},{10,11... | collective-permute-start | bytes 786440 | tf_op jit(solution)/shard_map/ppermute | solution.py:172
  38.0 2.4 %collective-permute-start.13 = (bf16[512,256]{1,0:T(8,128)(2,1)S(1)}, bf16[512,256]{1,0:T(8,128)(2,1)}, u32[]{:S(2)}, u32[]{:S(2)}) collective-permute-start(bf16[512,256]{1,0:T(8,128)(2,1)S(1)} %collective-permute-done.11.refs_15_), channel_id=1, source_target_pairs={{0,1},{1,0},{2,3},{3,2},{4,5},{5,4},{6,7},{7,6},{8,9},{9,8},{10,11... | collective-permute-start | bytes 786440 | tf_op jit(solution)/shard_map/ppermute | solution.py:172
  40.5 0.0 copy-start.2
  40.5 0.1 stack.35.refs_0_
  40.6 0.0 collective-permute-done.9.refs_13_
  40.6 0.0 collective-permute-done.5.refs_9_
  40.6 0.0 collective-permute-done.8.refs_12_
  40.6 1.1 collective-permute-done.13.refs_17_
  41.7 9.1 %local_sums.1 = bf16[512,896]{1,0:T(8,128)(2,1)} custom-call(s32[8]{0:T(128)S(1)} %stack.35.refs_0_, s32[32]{0:T(128)S(1)} %copy-done.2, bf16[512,256]{1,0:T(8,128)(2,1)S(1)} %bitcast.23, bf16[512,256]{1,0:T(8,128)(2,1)S(1)} %bitcast.19, bf16[512,256]{1,0:T(8,128)(2,1)S(1)} %collective-permute-done.refs_4_, ...), custom_call_target="tpu_custom_call" | custom-call | tf_op jit(solution)/shard_map/local_sums/pallas_call | solution.py:189
  50.8 16.6 %all-to-all-start = ((bf16[64,8,896]{2,1,0:T(8,128)(2,1)}), bf16[64,8,896]{2,1,0:T(8,128)(2,1)S(1)}, u32[]{:S(2)}, u32[]{:S(2)}) async-start(bf16[64,8,896]{2,1,0:T(8,128)(2,1)} %bitcast.10), calls=%async_computation | async-start | bytes 1835008 | tf_op jit(solution)/shard_map/all_to_all | solution.py:210
  67.5 27.0 %all-to-all-done = bf16[64,8,896]{2,1,0:T(8,128)(2,1)S(1)} async-done(((bf16[64,8,896]{2,1,0:T(8,128)(2,1)}), bf16[64,8,896]{2,1,0:T(8,128)(2,1)S(1)}, u32[]{:S(2)}, u32[]{:S(2)}) %all-to-all-start) | async-done | bytes 917536 | tf_op jit(solution)/shard_map/all_to_all | solution.py:210
  94.5 0.7 final_sums.1
  95.2 25.4 %all_to_all.23 = bf16[64,8,512]{2,1,0:T(8,128)(2,1)S(1)} all-to-all(bf16[64,8,512]{2,1,0:T(8,128)(2,1)S(1)} %bitcast.15), channel_id=1, replica_groups=mesh['psg'=64,'pb'=4,'rep'=2] {'psg'}, dimensions={0} | all-to-all | bytes 1048576 | tf_op jit(solution)/shard_map/all_to_all | solution.py:220
  120.6 0.8 fusion
  (11 shorter events, 0.0 us)
Async XLA Ops:
  0.6 41.1 %copy-start = (bf16[512,256]{1,0:T(8,128)(2,1)S(1)}, bf16[512,256]{1,0:T(8,128)(2,1)}, u32[]{:S(2)}) copy-start(bf16[512,256]{1,0:T(8,128)(2,1)} %refs_21_.1) | copy-start | bytes 786436
  0.6 41.1 %copy-start.1 = (bf16[512,256]{1,0:T(8,128)(2,1)S(1)}, bf16[512,256]{1,0:T(8,128)(2,1)}, u32[]{:S(2)}) copy-start(bf16[512,256]{1,0:T(8,128)(2,1)} %refs_20_.1) | copy-start | bytes 786436
  1.8 16.1 %collective-permute-start.2 = (bf16[512,256]{1,0:T(8,128)(2,1)S(1)}, bf16[512,256]{1,0:T(8,128)(2,1)S(1)}, u32[]{:S(2)}, u32[]{:S(2)}) collective-permute-start(bf16[512,256]{1,0:T(8,128)(2,1)S(1)} %bitcast.20), channel_id=1, source_target_pairs={{0,2},{2,4},{4,6},{6,0},{1,3},{3,5},{5,7},{7,1},{8,10},{10,12},{12... | collective-permute-start | bytes 786440 | tf_op jit(solution)/shard_map/ppermute | solution.py:161
  5.2 15.1 %collective-permute-start.7 = (bf16[512,256]{1,0:T(8,128)(2,1)S(1)}, bf16[512,256]{1,0:T(8,128)(2,1)S(1)}, u32[]{:S(2)}, u32[]{:S(2)}) collective-permute-start(bf16[512,256]{1,0:T(8,128)(2,1)S(1)} %bitcast.16), channel_id=1, source_target_pairs={{0,6},{2,0},{4,2},{6,4},{1,7},{3,1},{5,3},{7,5},{8,14},{10,8},{12,... | collective-permute-start | bytes 786440 | tf_op jit(solution)/shard_map/ppermute | solution.py:162
  8.8 13.4 %collective-permute-start.3 = (bf16[512,256]{1,0:T(8,128)(2,1)S(1)}, bf16[512,256]{1,0:T(8,128)(2,1)S(1)}, u32[]{:S(2)}, u32[]{:S(2)}) collective-permute-start(bf16[512,256]{1,0:T(8,128)(2,1)S(1)} %bitcast.17), channel_id=1, source_target_pairs={{0,2},{2,4},{4,6},{6,0},{1,3},{3,5},{5,7},{7,1},{8,10},{10,12},{12... | collective-permute-start | bytes 786440 | tf_op jit(solution)/shard_map/ppermute | solution.py:163
  11.0 16.3 %collective-permute-start.6 = (bf16[512,256]{1,0:T(8,128)(2,1)S(1)}, bf16[512,256]{1,0:T(8,128)(2,1)S(1)}, u32[]{:S(2)}, u32[]{:S(2)}) collective-permute-start(bf16[512,256]{1,0:T(8,128)(2,1)S(1)} %bitcast.21), channel_id=1, source_target_pairs={{0,6},{2,0},{4,2},{6,4},{1,7},{3,1},{5,3},{7,5},{8,14},{10,8},{12,... | collective-permute-start | bytes 786440 | tf_op jit(solution)/shard_map/ppermute | solution.py:164
  15.9 13.4 %collective-permute-start = (bf16[512,256]{1,0:T(8,128)(2,1)S(1)}, bf16[512,256]{1,0:T(8,128)(2,1)S(1)}, u32[]{:S(2)}, u32[]{:S(2)}) collective-permute-start(bf16[512,256]{1,0:T(8,128)(2,1)S(1)} %bitcast.22), channel_id=1, source_target_pairs={{0,1},{1,0},{2,3},{3,2},{4,5},{5,4},{6,7},{7,6},{8,9},{9,8},{10,11... | collective-permute-start | bytes 786440 | tf_op jit(solution)/shard_map/ppermute | solution.py:172
  17.8 13.9 %collective-permute-start.1 = (bf16[512,256]{1,0:T(8,128)(2,1)S(1)}, bf16[512,256]{1,0:T(8,128)(2,1)S(1)}, u32[]{:S(2)}, u32[]{:S(2)}) collective-permute-start(bf16[512,256]{1,0:T(8,128)(2,1)S(1)} %bitcast.18), channel_id=1, source_target_pairs={{0,1},{1,0},{2,3},{3,2},{4,5},{5,4},{6,7},{7,6},{8,9},{9,8},{10,11... | collective-permute-start | bytes 786440 | tf_op jit(solution)/shard_map/ppermute | solution.py:172
  20.3 13.4 %collective-permute-start.10 = (bf16[512,256]{1,0:T(8,128)(2,1)S(1)}, bf16[512,256]{1,0:T(8,128)(2,1)S(1)}, u32[]{:S(2)}, u32[]{:S(2)}) collective-permute-start(bf16[512,256]{1,0:T(8,128)(2,1)S(1)} %collective-permute-done.2.refs_6_), channel_id=1, source_target_pairs={{0,2},{2,4},{4,6},{6,0},{1,3},{3,5},{5,7},{7,1},{8,10},{10,12},{12... | collective-permute-start | bytes 786440 | tf_op jit(solution)/shard_map/ppermute | solution.py:165
  22.2 13.9 %collective-permute-start.11 = (bf16[512,256]{1,0:T(8,128)(2,1)S(1)}, bf16[512,256]{1,0:T(8,128)(2,1)S(1)}, u32[]{:S(2)}, u32[]{:S(2)}) collective-permute-start(bf16[512,256]{1,0:T(8,128)(2,1)S(1)} %collective-permute-done.7.refs_11_), channel_id=1, source_target_pairs={{0,6},{2,0},{4,2},{6,4},{1,7},{3,1},{5,3},{7,5},{8,14},{10,8},{12,... | collective-permute-start | bytes 786440 | tf_op jit(solution)/shard_map/ppermute | solution.py:166
  27.4 10.7 %collective-permute-start.4 = (bf16[512,256]{1,0:T(8,128)(2,1)S(1)}, bf16[512,256]{1,0:T(8,128)(2,1)S(1)}, u32[]{:S(2)}, u32[]{:S(2)}) collective-permute-start(bf16[512,256]{1,0:T(8,128)(2,1)S(1)} %collective-permute-done.2.refs_6_), channel_id=1, source_target_pairs={{0,1},{1,0},{2,3},{3,2},{4,5},{5,4},{6,7},{7,6},{8,9},{9,8},{10,11... | collective-permute-start | bytes 786440 | tf_op jit(solution)/shard_map/ppermute | solution.py:172
  29.3 11.3 %collective-permute-start.9 = (bf16[512,256]{1,0:T(8,128)(2,1)S(1)}, bf16[512,256]{1,0:T(8,128)(2,1)}, u32[]{:S(2)}, u32[]{:S(2)}) collective-permute-start(bf16[512,256]{1,0:T(8,128)(2,1)S(1)} %collective-permute-done.7.refs_11_), channel_id=1, source_target_pairs={{0,1},{1,0},{2,3},{3,2},{4,5},{5,4},{6,7},{7,6},{8,9},{9,8},{10,11... | collective-permute-start | bytes 786440 | tf_op jit(solution)/shard_map/ppermute | solution.py:172
  31.7 8.9 %collective-permute-start.5 = (bf16[512,256]{1,0:T(8,128)(2,1)S(1)}, bf16[512,256]{1,0:T(8,128)(2,1)}, u32[]{:S(2)}, u32[]{:S(2)}) collective-permute-start(bf16[512,256]{1,0:T(8,128)(2,1)S(1)} %collective-permute-done.3.refs_7_), channel_id=1, source_target_pairs={{0,1},{1,0},{2,3},{3,2},{4,5},{5,4},{6,7},{7,6},{8,9},{9,8},{10,11... | collective-permute-start | bytes 786440 | tf_op jit(solution)/shard_map/ppermute | solution.py:172
  33.7 6.9 %collective-permute-start.8 = (bf16[512,256]{1,0:T(8,128)(2,1)S(1)}, bf16[512,256]{1,0:T(8,128)(2,1)}, u32[]{:S(2)}, u32[]{:S(2)}) collective-permute-start(bf16[512,256]{1,0:T(8,128)(2,1)S(1)} %collective-permute-done.6.refs_10_), channel_id=1, source_target_pairs={{0,1},{1,0},{2,3},{3,2},{4,5},{5,4},{6,7},{7,6},{8,9},{9,8},{10,11... | collective-permute-start | bytes 786440 | tf_op jit(solution)/shard_map/ppermute | solution.py:172
  36.1 4.5 %collective-permute-start.12 = (bf16[512,256]{1,0:T(8,128)(2,1)S(1)}, bf16[512,256]{1,0:T(8,128)(2,1)}, u32[]{:S(2)}, u32[]{:S(2)}) collective-permute-start(bf16[512,256]{1,0:T(8,128)(2,1)S(1)} %collective-permute-done.10.refs_14_), channel_id=1, source_target_pairs={{0,1},{1,0},{2,3},{3,2},{4,5},{5,4},{6,7},{7,6},{8,9},{9,8},{10,11... | collective-permute-start | bytes 786440 | tf_op jit(solution)/shard_map/ppermute | solution.py:172
  38.0 3.7 %collective-permute-start.13 = (bf16[512,256]{1,0:T(8,128)(2,1)S(1)}, bf16[512,256]{1,0:T(8,128)(2,1)}, u32[]{:S(2)}, u32[]{:S(2)}) collective-permute-start(bf16[512,256]{1,0:T(8,128)(2,1)S(1)} %collective-permute-done.11.refs_15_), channel_id=1, source_target_pairs={{0,1},{1,0},{2,3},{3,2},{4,5},{5,4},{6,7},{7,6},{8,9},{9,8},{10,11... | collective-permute-start | bytes 786440 | tf_op jit(solution)/shard_map/ppermute | solution.py:172
  40.5 1.2 %copy-start.2 = (s32[32]{0:T(128)S(1)}, s32[32]{0:T(128)}, u32[]{:S(2)}) copy-start(s32[32]{0:T(128)} %refs_1_.1) | copy-start | bytes 388
  50.8 43.7 %all-to-all-start = ((bf16[64,8,896]{2,1,0:T(8,128)(2,1)}), bf16[64,8,896]{2,1,0:T(8,128)(2,1)S(1)}, u32[]{:S(2)}, u32[]{:S(2)}) async-start(bf16[64,8,896]{2,1,0:T(8,128)(2,1)} %bitcast.10), calls=%async_computation | async-start | bytes 1835008 | tf_op jit(solution)/shard_map/all_to_all | solution.py:210

commit v2 on v1

--- a/solution.py
+++ b/solution.py
@@ -35,15 +35,36 @@
     return out
 
 
-def local_kernel(pieces, *refs):
-    block_ref, owner_ref = refs[:2]
-    x_refs = refs[2 : 2 + pieces]
-    (wk_ref, wv_ref, q_ref, c_ref, out_ref, kblk, vblk, score, product, top, total, dots, corr, acc_v, acc_k) = refs[
-        2 + pieces :
-    ]
+def own_kernel(block_ref, x_ref, wk_ref, wv_ref, acc_ref, rest_ref):
+    wide = x_ref.shape[1]
+    cols = wk_ref.shape[1]
+    for n in range(wk_ref.shape[0] // wide):
+        at = pl.ds(pl.multiple_of(block_ref[n] * wide, wide), wide)
+        for side, ref in enumerate((wk_ref, wv_ref)):
+            columns = slice(side * cols, (side + 1) * cols)
+            if n == 0:
+                acc_ref[:, columns] = jnp.dot(x_ref[...], ref[at, :], preferred_element_type=f32)
+            else:
+                rest_ref[(n - 1) * wide : n * wide, columns] = ref[at, :]
+
+
+def near_kernel(acc_ref, rest_ref, *refs):
+    x_refs, out_ref = refs[:-1], refs[-1]
+    weight = rest_ref[0 : len(x_refs) * x_refs[0].shape[1], :]
+    chunk = 512
+    for low in range(0, acc_ref.shape[0], chunk):
+        rows = jnp.concatenate([x[low : low + chunk, :] for x in x_refs], axis=1)
+        out_ref[low : low + chunk, :] = acc_ref[low : low + chunk, :] + jnp.dot(
+            rows, weight, preferred_element_type=f32
+        )
+
+
+def local_kernel(owner_ref, acc_ref, *refs):
+    (far_ref, rest_ref, q_ref, c_ref, out_ref, kblk, vblk, score, product, top, total, dots, corr, acc_v, acc_k) = refs
     slots = owner_ref.shape[0]
     half = slots // 2
-    heads = q_ref.shape[1] // HDIM
+    cols = q_ref.shape[1]
+    heads = cols // HDIM
     keys = heads * PL
 
     top[...] = jnp.full_like(top, masked_value)
@@ -52,29 +73,23 @@
     acc_v[...] = jnp.zeros_like(acc_v)
     acc_k[...] = jnp.zeros_like(acc_k)
 
-    blocks = 8
-    wide = wk_ref.shape[0] // blocks
-
-    def weight(ref):
-        rows = [ref[pl.ds(pl.multiple_of(block_ref[j] * wide, wide), wide), :] for j in range(blocks)]
-        return jnp.concatenate(rows, axis=0)
-
     on_diagonal = (
-        lax.broadcasted_iota(jnp.int32, (keys, heads * HDIM), 0) // PL
-        == lax.broadcasted_iota(jnp.int32, (keys, heads * HDIM), 1) // HDIM
+        lax.broadcasted_iota(jnp.int32, (keys, cols), 0) // PL
+        == lax.broadcasted_iota(jnp.int32, (keys, cols), 1) // HDIM
     ).astype(f32).astype(bf16)
 
-    group = 8
-    for start in range(0, slots, group):
-        side = 0 if start < half else 1
-        low = (start - side * half) * PL
-        rows = jnp.concatenate([x_refs[j * 2 + side][low : low + group * PL, :] for j in range(blocks)], axis=1)
-        key_rows = jnp.dot(rows, weight(wk_ref), preferred_element_type=f32).astype(bf16)
-        value_rows = jnp.dot(rows, weight(wv_ref), preferred_element_type=f32).astype(bf16)
-        for i in range(group):
-            slot = start + i
-            kb = jnp.concatenate([key_rows[i * PL : (i + 1) * PL]] * heads, axis=0) * on_diagonal
-            vb = jnp.concatenate([value_rows[i * PL : (i + 1) * PL]] * heads, axis=0) * on_diagonal
+    for side in range(2):
+        low = side * half * PL
+        rows = far_ref[low : low + half * PL, :]
+        projected = acc_ref[low : low + half * PL, :] + jnp.dot(
+            rows, rest_ref[-rows.shape[1] :, :], preferred_element_type=f32
+        )
+        projected = projected.astype(bf16)
+        for i in range(half):
+            slot = side * half + i
+            own = projected[i * PL : (i + 1) * PL]
+            kb = jnp.concatenate([own[:, :cols]] * heads, axis=0) * on_diagonal
+            vb = jnp.concatenate([own[:, cols:]] * heads, axis=0) * on_diagonal
             kblk[slot] = kb
             vblk[slot] = vb
             o = owner_ref[slot]
@@ -109,7 +124,6 @@
         acc_v[o] = acc_v[o] + jnp.dot(both[:TGT], vblk[slot], preferred_element_type=f32)
         acc_k[o] = acc_k[o] + jnp.dot(both, kblk[slot], preferred_element_type=f32)
 
-    cols = heads * HDIM
     part = lax.broadcasted_iota(jnp.int32, (TGT, keys), 1) % PL
     for q in range(QUESTIONS):
         at = slice(q * TGT, (q + 1) * TGT)
@@ -151,26 +165,16 @@
         out_ref[2 * rows * n : 2 * rows * (n + 1), :] = two
 
 
-def gather(x):
+def swap(block):
+    return lax.ppermute(block, "rep", [(0, 1), (1, 0)])
+
+
+def block_numbers():
     n = lax.axis_size("pb")
-    right = [(i, (i + 1) % n) for i in range(n)]
-    left = [(i, (i - 1) % n) for i in range(n)]
-    swap = [(0, 1), (1, 0)]
-    half = x.shape[0] // 2
-    a, b = x[:half], x[half:]
-    left_a = lax.ppermute(a, "pb", right)
-    right_b = lax.ppermute(b, "pb", left)
-    left_b = lax.ppermute(b, "pb", right)
-    right_a = lax.ppermute(a, "pb", left)
-    far_a = lax.ppermute(left_a, "pb", right)
-    far_b = lax.ppermute(right_b, "pb", left)
     pb, rep = lax.axis_index("pb"), lax.axis_index("rep")
-    out = []
-    for shift, first, second in ((0, a, b), (n - 1, left_a, left_b), (1, right_a, right_b), (2, far_a, far_b)):
-        place = (pb + shift) % n
-        out.append((place * 2 + rep, first, second))
-        out.append((place * 2 + 1 - rep, lax.ppermute(first, "rep", swap), lax.ppermute(second, "rep", swap)))
-    return out
+    places = [(pb + shift) % n for shift in (0, n - 1, 1, 2)]
+    numbers = [number for place in places for number in (place * 2 + rep, place * 2 + 1 - rep)]
+    return jnp.stack(numbers).astype(jnp.int32)
 
 
 def body(queries, prefixes, owner, key_weight, value_weight, cotangent):
@@ -181,15 +185,38 @@
     devices = lax.axis_size("psg")
     own = rows // devices
 
-    parts = gather(prefixes.reshape(slots * vectors, features))
-    block = jnp.stack([p[0] for p in parts]).astype(jnp.int32)
-    pieces = [p for part in parts for p in part[1:]]
+    passages = prefixes.reshape(slots * vectors, features)
+    n = lax.axis_size("pb")
+    left, right, far = (
+        lax.ppermute(passages, "pb", [(i, (i + shift) % n) for i in range(n)]) for shift in (1, n - 1, 2)
+    )
+    other = swap(passages)
     smem = pl.BlockSpec(memory_space=pltpu.SMEM)
     vmem = pl.BlockSpec(memory_space=pltpu.VMEM)
+    sums = jax.ShapeDtypeStruct((slots * vectors, 2 * cols), f32)
+    projected, rest = pl.pallas_call(
+        own_kernel,
+        out_shape=(sums, jax.ShapeDtypeStruct((key_weight.shape[0] - features, 2 * cols), bf16)),
+        in_specs=[smem] + [vmem] * 3,
+        out_specs=(vmem, vmem),
+        compiler_params=pltpu.CompilerParams(vmem_limit_bytes=16 * 1024 * 1024),
+        name="own_projection",
+    )(block_numbers(), passages, key_weight, value_weight)
+    left, projected, rest = lax.optimization_barrier((left, projected, rest))
+    near = [other, left, swap(left), right, swap(right), far]
+    far = swap(far)
+    projected = pl.pallas_call(
+        near_kernel,
+        out_shape=sums,
+        in_specs=[vmem] * (2 + len(near)),
+        out_specs=vmem,
+        compiler_params=pltpu.CompilerParams(vmem_limit_bytes=16 * 1024 * 1024),
+        name="near_projection",
+    )(projected, rest, *near)
     payload = pl.pallas_call(
-        lambda *refs: local_kernel(len(pieces), *refs),
+        local_kernel,
         out_shape=jax.ShapeDtypeStruct((rows, 3 * cols + keys), bf16),
-        in_specs=[smem, smem] + [vmem] * (len(pieces) + 4),
+        in_specs=[smem] + [vmem] * 5,
         out_specs=vmem,
         scratch_shapes=[
             pltpu.VMEM((slots, keys, cols), bf16),
@@ -203,9 +230,9 @@
             pltpu.VMEM((QUESTIONS + 1, TGT, cols), f32),
             pltpu.VMEM((QUESTIONS + 1, 2 * TGT, cols), f32),
         ],
-        compiler_params=pltpu.CompilerParams(vmem_limit_bytes=48 * 1024 * 1024),
+        compiler_params=pltpu.CompilerParams(vmem_limit_bytes=24 * 1024 * 1024),
         name="local_sums",
-    )(block, owner, *pieces, key_weight, value_weight, queries, cotangent)
+    )(owner, projected, far, rest, queries, cotangent)
 
     received = lax.all_to_all(payload, "psg", 0, 0, tiled=True)
     own_cotangent = lax.dynamic_slice_in_dim(cotangent, lax.axis_index("psg") * own, own, 0).astype(f32)
@@ -214,7 +241,7 @@
         out_shape=jax.ShapeDtypeStruct((rows, 2 * cols), bf16),
         in_specs=[vmem, vmem],
         out_specs=vmem,
-        compiler_params=pltpu.CompilerParams(vmem_limit_bytes=48 * 1024 * 1024),
+        compiler_params=pltpu.CompilerParams(vmem_limit_bytes=24 * 1024 * 1024),
         name="final_sums",
     )(received, own_cotangent)
     outputs = lax.all_to_all(finished, "psg", 0, 0, tiled=True)

time: 122 us -> 113 us (0.926)
  the two profiles are of different devices: /device:TPU:8 before, /device:TPU:6 now
where the time goes in v2:
time: 113 us
  starting transfers between devices  37.8 us (33%)
  waiting for transfers between devices  35.6 us (32%)
  blocking collectives  25.1 us (22%)
  Pallas kernels  8.96 us (8%)
  local copies, waits for them, and re-layouts  4.42 us (4%)
    all_to_all x1, waiting for transfers between devices, body(): received = lax.all_to_all(payload, 'psg', 0, 0, tiled=True)  27 us
    all_to_all x1, blocking collectives, body(): outputs = lax.all_to_all(finished, 'psg', 0, 0, tiled=True)  25.1 us
    all_to_all x1, starting transfers between devices, body(): received = lax.all_to_all(payload, 'psg', 0, 0, tiled=True)  16 us
    ppermute x3, starting transfers between devices, body(): lax.ppermute(passages, 'pb', [(i, (i + shift) % n) for i in range(n)])  13.1 us
    ppermute x4, starting transfers between devices, swap(): return lax.ppermute(block, 'rep', [(0, 1), (1, 0)])  8.77 us
    ppermute x3, waiting for transfers between devices, body(): lax.ppermute(passages, 'pb', [(i, (i + shift) % n) for i in range(n)])  8.62 us
    pallas_call x1, Pallas kernels, body(): pl.pallas_call(local_kernel, out_shape=jax.ShapeDtypeStruct((rows, 3 * co...  5.45 us
    unnamed x12, local copies, waits for them, and re-layouts  3.51 us
  transfers between devices with their start and end apart: 8, of which 2 were waited for; matrix products, arithmetic and copies ran while one was open for 0% of the time, Pallas kernels for 3%

profile of v2, /device:TPU:6, one launch (start us, length us, event | category | flops | bytes accessed | tf_op | source)
XLA Modules:
  0.0 112.9 jit_solution(10532785443095604242)
XLA Ops:
  0.6 7.8 %collective-permute-start = (bf16[1024,256]{1,0:T(8,128)(2,1)}, bf16[1024,256]{1,0:T(8,128)(2,1)S(1)}, u32[]{:S(2)}, u32[]{:S(2)}) collective-permute-start(bf16[1024,256]{1,0:T(8,128)(2,1)} %bitcast.15), channel_id=1, source_target_pairs={{0,2},{2,4},{4,6},{6,0},{1,3},{3,5},{5,7},{7,1},{8,10},{10,12},{12... | collective-permute-start | bytes 1572872 | tf_op jit(solution)/shard_map/ppermute | solution.py:191
  8.4 1.9 %collective-permute-start.3 = (bf16[1024,256]{1,0:T(8,128)(2,1)}, bf16[1024,256]{1,0:T(8,128)(2,1)S(1)}, u32[]{:S(2)}, u32[]{:S(2)}) collective-permute-start(bf16[1024,256]{1,0:T(8,128)(2,1)} %bitcast.16), channel_id=1, source_target_pairs={{0,6},{2,0},{4,2},{6,4},{1,7},{3,1},{5,3},{7,5},{8,14},{10,8},{12,... | collective-permute-start | bytes 1572872 | tf_op jit(solution)/shard_map/ppermute | solution.py:191
  10.3 3.4 %collective-permute-start.5 = (bf16[1024,256]{1,0:T(8,128)(2,1)}, bf16[1024,256]{1,0:T(8,128)(2,1)S(1)}, u32[]{:S(2)}, u32[]{:S(2)}) collective-permute-start(bf16[1024,256]{1,0:T(8,128)(2,1)} %bitcast.17), channel_id=1, source_target_pairs={{0,4},{2,6},{4,0},{6,2},{1,5},{3,7},{5,1},{7,3},{8,12},{10,14},{12... | collective-permute-start | bytes 1572872 | tf_op jit(solution)/shard_map/ppermute | solution.py:191
  13.7 1.9 %collective-permute-start.1 = (bf16[1024,256]{1,0:T(8,128)(2,1)}, bf16[1024,256]{1,0:T(8,128)(2,1)S(1)}, u32[]{:S(2)}, u32[]{:S(2)}) collective-permute-start(bf16[1024,256]{1,0:T(8,128)(2,1)} %bitcast.18), channel_id=1, source_target_pairs={{0,1},{1,0},{2,3},{3,2},{4,5},{5,4},{6,7},{7,6},{8,9},{9,8},{10,11... | collective-permute-start | bytes 1572872 | tf_op jit(solution)/shard_map/ppermute | solution.py:169
  15.7 0.1 stack.35.block_ref
  15.8 1.2 %copy-done = bf16[2048,256]{1,0:T(8,128)(2,1)S(1)} copy-done((bf16[2048,256]{1,0:T(8,128)(2,1)S(1)}, bf16[2048,256]{1,0:T(8,128)(2,1)}, u32[]{:S(2)}) %copy-start) | copy-done | bytes 1048600
  17.0 1.2 %copy-done.1 = bf16[2048,256]{1,0:T(8,128)(2,1)S(1)} copy-done((bf16[2048,256]{1,0:T(8,128)(2,1)S(1)}, bf16[2048,256]{1,0:T(8,128)(2,1)}, u32[]{:S(2)}) %copy-start.1) | copy-done | bytes 1048600
  18.2 1.0 copy-done.2
  19.3 1.0 own_projection.1
  20.3 0.0 collective-permute-done.refs_1_
  20.3 0.0 copy-start.3
  20.3 0.0 copy-start.4
  20.4 0.0 copy-start.5
  20.4 2.5 %collective-permute-start.2 = (bf16[1024,256]{1,0:T(8,128)(2,1)S(1)}, bf16[1024,256]{1,0:T(8,128)(2,1)S(1)}, u32[]{:S(2)}, u32[]{:S(2)}) collective-permute-start(bf16[1024,256]{1,0:T(8,128)(2,1)S(1)} %collective-permute-done.refs_1_), channel_id=1, source_target_pairs={{0,1},{1,0},{2,3},{3,2},{4,5},{5,4},{6,7},{7,6},{8,9},{9,8},{10,11... | collective-permute-start | bytes 1572872 | tf_op jit(solution)/shard_map/ppermute | solution.py:169
  22.9 8.6 %collective-permute-done.3.refs_3_ = bf16[1024,256]{1,0:T(8,128)(2,1)S(1)} collective-permute-done((bf16[1024,256]{1,0:T(8,128)(2,1)}, bf16[1024,256]{1,0:T(8,128)(2,1)S(1)}, u32[]{:S(2)}, u32[]{:S(2)}) %collective-permute-start.3) | collective-permute-done | bytes 524320 | tf_op jit(solution)/shard_map/ppermute | solution.py:191
  31.5 1.9 %collective-permute-start.4 = (bf16[1024,256]{1,0:T(8,128)(2,1)S(1)}, bf16[1024,256]{1,0:T(8,128)(2,1)S(1)}, u32[]{:S(2)}, u32[]{:S(2)}) collective-permute-start(bf16[1024,256]{1,0:T(8,128)(2,1)S(1)} %collective-permute-done.3.refs_3_), channel_id=1, source_target_pairs={{0,1},{1,0},{2,3},{3,2},{4,5},{5,4},{6,7},{7,6},{8,9},{9,8},{10,11... | collective-permute-start | bytes 1572872 | tf_op jit(solution)/shard_map/ppermute | solution.py:169
  33.4 0.0 collective-permute-done.5.refs_5_
  33.5 2.4 %collective-permute-start.6 = (bf16[1024,256]{1,0:T(8,128)(2,1)S(1)}, bf16[1024,256]{1,0:T(8,128)(2,1)S(1)}, u32[]{:S(2)}, u32[]{:S(2)}) collective-permute-start(bf16[1024,256]{1,0:T(8,128)(2,1)S(1)} %collective-permute-done.5.refs_5_), channel_id=1, source_target_pairs={{0,1},{1,0},{2,3},{3,2},{4,5},{5,4},{6,7},{7,6},{8,9},{9,8},{10,11... | collective-permute-start | bytes 1572872 | tf_op jit(solution)/shard_map/ppermute | solution.py:169
  35.9 0.0 collective-permute-done.1.refs_0_
  35.9 0.0 collective-permute-done.2.refs_2_
  35.9 0.0 collective-permute-done.4.refs_4_
  35.9 1.8 %near_projection.1.acc_ref = f32[1024,512]{1,0:T(8,128)S(1)} custom-call(f32[1024,512]{1,0:T(8,128)S(1)} %get-tuple-element.9.acc_ref, bf16[1792,512]{1,0:T(8,128)(2,1)S(1)} %get-tuple-element.10.rest_ref.refs_1_, bf16[1024,256]{1,0:T(8,128)(2,1)S(1)} %collective-permute-done.1.refs_0_, bf16[1024,256]{1,0:T(8,128)(2,1)S(1)} %collective-permute-done.refs_1_, ...), custom_call_target="tpu_custom_call" | custom-call | tf_op jit(solution)/shard_map/near_projection/pallas_call | solution.py:208
  37.7 0.0 collective-permute-done.6.refs_0_
  37.7 0.0 copy-done.3
  37.7 0.0 copy-done.4
  37.7 0.0 copy-done.5
  37.7 5.4 %local_sums.1 = bf16[512,896]{1,0:T(8,128)(2,1)} custom-call(s32[32]{0:T(128)S(1)} %copy-done.5, f32[1024,512]{1,0:T(8,128)S(1)} %near_projection.1.acc_ref, bf16[1024,256]{1,0:T(8,128)(2,1)S(1)} %collective-permute-done.6.refs_0_, bf16[1792,512]{1,0:T(8,128)(2,1)S(1)} %get-tuple-element.10.rest_ref.refs_1_, bf16[512,256]{1,0:T(8,128)(2,1)S(1)} %copy-done.4, ...), custom_call_target="tpu_custom_call" | custom-call | tf_op jit(solution)/shard_map/local_sums/pallas_call | solution.py:216
  43.2 16.0 %all-to-all-start = ((bf16[64,8,896]{2,1,0:T(8,128)(2,1)}), bf16[64,8,896]{2,1,0:T(8,128)(2,1)S(1)}, u32[]{:S(2)}, u32[]{:S(2)}) async-start(bf16[64,8,896]{2,1,0:T(8,128)(2,1)} %bitcast.9), calls=%async_computation | async-start | bytes 1835008 | tf_op jit(solution)/shard_map/all_to_all | solution.py:237
  59.2 27.0 %all-to-all-done = bf16[64,8,896]{2,1,0:T(8,128)(2,1)S(1)} async-done(((bf16[64,8,896]{2,1,0:T(8,128)(2,1)}), bf16[64,8,896]{2,1,0:T(8,128)(2,1)S(1)}, u32[]{:S(2)}, u32[]{:S(2)}) %all-to-all-start) | async-done | bytes 917536 | tf_op jit(solution)/shard_map/all_to_all | solution.py:237
  86.2 0.7 final_sums.1
  86.9 25.1 %all_to_all.23 = bf16[64,8,512]{2,1,0:T(8,128)(2,1)S(1)} all-to-all(bf16[64,8,512]{2,1,0:T(8,128)(2,1)S(1)} %bitcast.14), channel_id=1, replica_groups=mesh['psg'=64,'pb'=4,'rep'=2] {'psg'}, dimensions={0} | all-to-all | bytes 1048576 | tf_op jit(solution)/shard_map/all_to_all | solution.py:247
  112.0 0.8 fusion
  (4 shorter events, 0.0 us)
Async XLA Ops:
  0.6 19.7 %collective-permute-start = (bf16[1024,256]{1,0:T(8,128)(2,1)}, bf16[1024,256]{1,0:T(8,128)(2,1)S(1)}, u32[]{:S(2)}, u32[]{:S(2)}) collective-permute-start(bf16[1024,256]{1,0:T(8,128)(2,1)} %bitcast.15), channel_id=1, source_target_pairs={{0,2},{2,4},{4,6},{6,0},{1,3},{3,5},{5,7},{7,1},{8,10},{10,12},{12... | collective-permute-start | bytes 1572872 | tf_op jit(solution)/shard_map/ppermute | solution.py:191
  8.4 23.1 %collective-permute-start.3 = (bf16[1024,256]{1,0:T(8,128)(2,1)}, bf16[1024,256]{1,0:T(8,128)(2,1)S(1)}, u32[]{:S(2)}, u32[]{:S(2)}) collective-permute-start(bf16[1024,256]{1,0:T(8,128)(2,1)} %bitcast.16), channel_id=1, source_target_pairs={{0,6},{2,0},{4,2},{6,4},{1,7},{3,1},{5,3},{7,5},{8,14},{10,8},{12,... | collective-permute-start | bytes 1572872 | tf_op jit(solution)/shard_map/ppermute | solution.py:191
  10.3 23.1 %collective-permute-start.5 = (bf16[1024,256]{1,0:T(8,128)(2,1)}, bf16[1024,256]{1,0:T(8,128)(2,1)S(1)}, u32[]{:S(2)}, u32[]{:S(2)}) collective-permute-start(bf16[1024,256]{1,0:T(8,128)(2,1)} %bitcast.17), channel_id=1, source_target_pairs={{0,4},{2,6},{4,0},{6,2},{1,5},{3,7},{5,1},{7,3},{8,12},{10,14},{12... | collective-permute-start | bytes 1572872 | tf_op jit(solution)/shard_map/ppermute | solution.py:191
  13.7 22.2 %collective-permute-start.1 = (bf16[1024,256]{1,0:T(8,128)(2,1)}, bf16[1024,256]{1,0:T(8,128)(2,1)S(1)}, u32[]{:S(2)}, u32[]{:S(2)}) collective-permute-start(bf16[1024,256]{1,0:T(8,128)(2,1)} %bitcast.18), channel_id=1, source_target_pairs={{0,1},{1,0},{2,3},{3,2},{4,5},{5,4},{6,7},{7,6},{8,9},{9,8},{10,11... | collective-permute-start | bytes 1572872 | tf_op jit(solution)/shard_map/ppermute | solution.py:169
  15.8 1.2 %copy-start = (bf16[2048,256]{1,0:T(8,128)(2,1)S(1)}, bf16[2048,256]{1,0:T(8,128)(2,1)}, u32[]{:S(2)}) copy-start(bf16[2048,256]{1,0:T(8,128)(2,1)} %wk_ref.1) | copy-start | bytes 3145732
  17.0 1.2 %copy-start.1 = (bf16[2048,256]{1,0:T(8,128)(2,1)S(1)}, bf16[2048,256]{1,0:T(8,128)(2,1)}, u32[]{:S(2)}) copy-start(bf16[2048,256]{1,0:T(8,128)(2,1)} %wv_ref.1) | copy-start | bytes 3145732
  18.2 1.0 copy-start.2
  20.3 17.4 %copy-start.3 = (bf16[512,256]{1,0:T(8,128)(2,1)S(1)}, bf16[512,256]{1,0:T(8,128)(2,1)}, u32[]{:S(2)}) copy-start(bf16[512,256]{1,0:T(8,128)(2,1)} %refs_3_.1) | copy-start | bytes 786436
  20.3 17.4 %copy-start.4 = (bf16[512,256]{1,0:T(8,128)(2,1)S(1)}, bf16[512,256]{1,0:T(8,128)(2,1)}, u32[]{:S(2)}) copy-start(bf16[512,256]{1,0:T(8,128)(2,1)} %refs_2_.1) | copy-start | bytes 786436
  20.4 17.4 %copy-start.5 = (s32[32]{0:T(128)S(1)}, s32[32]{0:T(128)}, u32[]{:S(2)}) copy-start(s32[32]{0:T(128)} %owner_ref.1) | copy-start | bytes 388
  20.4 15.5 %collective-permute-start.2 = (bf16[1024,256]{1,0:T(8,128)(2,1)S(1)}, bf16[1024,256]{1,0:T(8,128)(2,1)S(1)}, u32[]{:S(2)}, u32[]{:S(2)}) collective-permute-start(bf16[1024,256]{1,0:T(8,128)(2,1)S(1)} %collective-permute-done.refs_1_), channel_id=1, source_target_pairs={{0,1},{1,0},{2,3},{3,2},{4,5},{5,4},{6,7},{7,6},{8,9},{9,8},{10,11... | collective-permute-start | bytes 1572872 | tf_op jit(solution)/shard_map/ppermute | solution.py:169
  31.5 4.4 %collective-permute-start.4 = (bf16[1024,256]{1,0:T(8,128)(2,1)S(1)}, bf16[1024,256]{1,0:T(8,128)(2,1)S(1)}, u32[]{:S(2)}, u32[]{:S(2)}) collective-permute-start(bf16[1024,256]{1,0:T(8,128)(2,1)S(1)} %collective-permute-done.3.refs_3_), channel_id=1, source_target_pairs={{0,1},{1,0},{2,3},{3,2},{4,5},{5,4},{6,7},{7,6},{8,9},{9,8},{10,11... | collective-permute-start | bytes 1572872 | tf_op jit(solution)/shard_map/ppermute | solution.py:169
  33.5 4.3 %collective-permute-start.6 = (bf16[1024,256]{1,0:T(8,128)(2,1)S(1)}, bf16[1024,256]{1,0:T(8,128)(2,1)S(1)}, u32[]{:S(2)}, u32[]{:S(2)}) collective-permute-start(bf16[1024,256]{1,0:T(8,128)(2,1)S(1)} %collective-permute-done.5.refs_5_), channel_id=1, source_target_pairs={{0,1},{1,0},{2,3},{3,2},{4,5},{5,4},{6,7},{7,6},{8,9},{9,8},{10,11... | collective-permute-start | bytes 1572872 | tf_op jit(solution)/shard_map/ppermute | solution.py:169
  43.2 43.1 %all-to-all-start = ((bf16[64,8,896]{2,1,0:T(8,128)(2,1)}), bf16[64,8,896]{2,1,0:T(8,128)(2,1)S(1)}, u32[]{:S(2)}, u32[]{:S(2)}) async-start(bf16[64,8,896]{2,1,0:T(8,128)(2,1)} %bitcast.9), calls=%async_computation | async-start | bytes 1835008 | tf_op jit(solution)/shard_map/all_to_all | solution.py:237

commit v3 on v2

--- a/solution.py
+++ b/solution.py
@@ -1,5 +1,6 @@
 import jax
 import jax.numpy as jnp
+import numpy as np
 from jax import lax
 from jax.experimental import pallas as pl
 from jax.experimental.pallas import tpu as pltpu
@@ -10,6 +11,7 @@
 PL = 32
 QUESTIONS = 16
 PARTS = 3
+SIDE = 8
 
 masked_value = -1e30
 
@@ -124,44 +126,74 @@
         acc_v[o] = acc_v[o] + jnp.dot(both[:TGT], vblk[slot], preferred_element_type=f32)
         acc_k[o] = acc_k[o] + jnp.dot(both, kblk[slot], preferred_element_type=f32)
 
-    part = lax.broadcasted_iota(jnp.int32, (TGT, keys), 1) % PL
     for q in range(QUESTIONS):
         at = slice(q * TGT, (q + 1) * TGT)
         out_ref[at, 0:cols] = acc_v[q].astype(bf16)
         out_ref[at, cols : 2 * cols] = acc_k[q, TGT:, :].astype(bf16)
         out_ref[at, 2 * cols : 3 * cols] = acc_k[q, :TGT, :].astype(bf16)
-        extra = jnp.zeros((TGT, keys), f32)
-        pieces_of = split_parts(top[q]) + split_parts(total[q]) + split_parts(corr[q])
-        for n, piece in enumerate(pieces_of):
-            extra = jnp.where(part == n, piece, extra)
-        out_ref[at, 3 * cols :] = extra.astype(bf16)
+        out_ref[at, 3 * cols :] = pack((top[q], total[q], corr[q]))
+
+
+def spread(extra, cols):
+    keys = extra.shape[1]
+    heads = keys // PL
+    lane = lax.broadcasted_iota(jnp.int32, (keys, 3 * cols), 0)
+    spot = lax.broadcasted_iota(jnp.int32, (keys, 3 * cols), 1)
+    pick = (lane // PL == (spot % cols) // (cols // heads)) & ((lane % PL) // PARTS == spot // cols)
+    wide = jnp.dot(extra, pick.astype(f32).astype(bf16), preferred_element_type=f32)
+    return [wide[:, n * cols : (n + 1) * cols] for n in range(3)]
+
+
+def pack(values):
+    part = lax.broadcasted_iota(jnp.int32, values[0].shape, 1) % PL
+    out = jnp.zeros_like(values[0])
+    for n, piece in enumerate([piece for value in values for piece in split_parts(value)]):
+        out = jnp.where(part == n, piece, out)
+    return out.astype(bf16)
+
+
+def merge(extra, cols, rows):
+    top, total, corr = [x.reshape(-1, rows, cols) for x in spread(extra, cols)]
+    high = jnp.max(top, axis=0)
+    scale = jnp.exp(top - high[None])
+    sums = jnp.sum(scale * total, axis=0)
+    dots = jnp.sum(scale * total * corr, axis=0)
+    mean = jnp.where(sums > 0.0, dots / jnp.where(sums > 0.0, sums, 1.0), 0.0)
+    return scale, corr, high, sums, mean
+
+
+def merge_kernel(r_ref, out_ref):
+    rows = out_ref.shape[0]
+    keys = r_ref.shape[1] % 256
+    cols = (r_ref.shape[1] - keys) // 3
+    extra = r_ref[:, 3 * cols :]
+
+    def read(n):
+        return r_ref[:, n * cols : (n + 1) * cols].astype(f32).reshape(-1, rows, cols)
+
+    scale, corr, _, _, mean = merge(extra, cols, rows)
+    out_ref[:, 0:cols] = jnp.sum(scale * read(0), axis=0).astype(bf16)
+    low = scale * read(2)
+    grad = jnp.sum(scale * read(1) + (corr - mean[None]) * low, axis=0)
+    out_ref[:, cols : 2 * cols] = grad.astype(bf16)
+    out_ref[:, 2 * cols : 3 * cols] = jnp.sum(low, axis=0).astype(bf16)
+    out_ref[:, 3 * cols :] = pack(merge(extra, keys, rows)[2:])
 
 
 def final_kernel(r_ref, c_ref, out_ref):
     rows, cols = c_ref.shape
-    heads = cols // HDIM
-    keys = heads * PL
-    devices = r_ref.shape[0] // rows
-    lane = lax.broadcasted_iota(jnp.int32, (keys, 3 * cols), 0)
-    spot = lax.broadcasted_iota(jnp.int32, (keys, 3 * cols), 1)
-    pick = (lane // PL == (spot % cols) // HDIM) & ((lane % PL) // PARTS == spot // cols)
-    pick = pick.astype(f32).astype(bf16)
-    wide = jnp.dot(r_ref[:, 3 * cols :], pick, preferred_element_type=f32).reshape(devices, rows, 3 * cols)
-    top = wide[:, :, 0:cols]
-    weight = jnp.exp(top - jnp.max(top, axis=0, keepdims=True))
-    total = jnp.sum(weight * wide[:, :, cols : 2 * cols], axis=0)
+    scale, own, _, total, _ = merge(r_ref[:, 3 * cols :], cols, rows)
 
     def read(n):
-        return r_ref[:, n * cols : (n + 1) * cols].astype(f32).reshape(devices, rows, cols)
-
-    summed = jnp.sum(weight * read(0), axis=0)
+        return r_ref[:, n * cols : (n + 1) * cols].astype(f32).reshape(-1, rows, cols)
+
+    summed = jnp.sum(scale * read(0), axis=0)
     attended = (summed / total).astype(bf16).astype(f32)
     corr = per_head(c_ref[...] * attended, HDIM, jnp.sum, 0.0)
-    shift = wide[:, :, 2 * cols :] - corr[None]
-    grad = jnp.sum(weight * (read(1) + shift * read(2)), axis=0) / total
+    grad = jnp.sum(scale * (read(1) + (own - corr[None]) * read(2)), axis=0) / total
     both = jnp.concatenate([attended, grad], axis=1)
     two = jnp.concatenate([both, both], axis=0).astype(bf16)
-    for n in range(devices // 2):
+    for n in range(out_ref.shape[0] // (2 * rows)):
         out_ref[2 * rows * n : 2 * rows * (n + 1), :] = two
 
 
@@ -177,13 +209,30 @@
     return jnp.stack(numbers).astype(jnp.int32)
 
 
+AXES = ("psg", "pb", "rep")
+
+
+def line_groups(mesh_shape, turn):
+    side = SIDE
+    assert side * side == mesh_shape[0]
+    ids = np.arange(np.prod(mesh_shape)).reshape((side, side) + tuple(mesh_shape[1:]))
+    groups = []
+    for core in range(mesh_shape[2]):
+        along = (core + turn + 1) % 2
+        lines = np.moveaxis(ids[:, :, :, core], along, -1)
+        groups += lines.reshape(-1, side).tolist()
+    return groups
+
+
+def exchange(x, groups):
+    return lax.all_to_all(x, AXES, 0, 0, axis_index_groups=groups, tiled=True)
+
+
 def body(queries, prefixes, owner, key_weight, value_weight, cotangent):
     slots, vectors, features = prefixes.shape
     rows, cols = queries.shape
     heads = cols // HDIM
     keys = heads * PL
-    devices = lax.axis_size("psg")
-    own = rows // devices
 
     passages = prefixes.reshape(slots * vectors, features)
     n = lax.axis_size("pb")
@@ -234,17 +283,36 @@
         name="local_sums",
     )(owner, projected, far, rest, queries, cotangent)
 
-    received = lax.all_to_all(payload, "psg", 0, 0, tiled=True)
-    own_cotangent = lax.dynamic_slice_in_dim(cotangent, lax.axis_index("psg") * own, own, 0).astype(f32)
+    shape = tuple(lax.axis_size(name) for name in AXES)
+    first_lines, second_lines = line_groups(shape, 0), line_groups(shape, 1)
+    block_rows = rows // SIDE
+    merged = pl.pallas_call(
+        merge_kernel,
+        out_shape=jax.ShapeDtypeStruct((block_rows, payload.shape[1]), bf16),
+        in_specs=[vmem],
+        out_specs=vmem,
+        compiler_params=pltpu.CompilerParams(vmem_limit_bytes=24 * 1024 * 1024),
+        name="line_sums",
+    )(exchange(payload, first_lines))
+    received = exchange(merged, second_lines)
+
+    own = block_rows // SIDE
+    place = lax.axis_index("psg")
+    z, y = place // SIDE, place % SIDE
+    core = lax.axis_index("rep")
+    start = jnp.where(core == 0, y, z) * block_rows + jnp.where(core == 0, z, y) * own
+    own_cotangent = lax.dynamic_slice_in_dim(cotangent, start, own, 0).astype(f32)
     finished = pl.pallas_call(
         final_kernel,
-        out_shape=jax.ShapeDtypeStruct((rows, 2 * cols), bf16),
+        out_shape=jax.ShapeDtypeStruct((block_rows, 2 * cols), bf16),
         in_specs=[vmem, vmem],
         out_specs=vmem,
         compiler_params=pltpu.CompilerParams(vmem_limit_bytes=24 * 1024 * 1024),
         name="final_sums",
     )(received, own_cotangent)
-    outputs = lax.all_to_all(finished, "psg", 0, 0, tiled=True)
+    block_out = exchange(finished, second_lines)
+    copies = jnp.broadcast_to(block_out[None], (SIDE,) + block_out.shape).reshape(rows, 2 * cols)
+    outputs = exchange(copies, first_lines)
     return outputs[:, :cols], outputs[:, cols:]
 
 

time: 113 us -> 115 us (1.018)
  blocking collectives: 25.1 us -> 50.3 us
  waiting for transfers between devices: 35.6 us -> 17.5 us
  starting transfers between devices: 37.8 us -> 32.1 us
    all_to_all x1 -> x3, blocking collectives: 25.1 us -> 50.3 us  [exchange(): return lax.all_to_all(x, AXES, 0, 0, axis_index_groups=groups, tiled=True)]
    all_to_all x1, waiting for transfers between devices: 27 us -> 8.9 us  [exchange(): return lax.all_to_all(x, AXES, 0, 0, axis_index_groups=groups, tiled=True)]
    all_to_all x1, starting transfers between devices: 16 us -> 10.3 us  [exchange(): return lax.all_to_all(x, AXES, 0, 0, axis_index_groups=groups, tiled=True)]
  transfers between devices with their start and end apart: 8 -> 8, of which waited for: 2 -> 2; matrix products, arithmetic and copies ran while one was open for 0% -> 0% of each run, Pallas kernels for 3% -> 2%
where the time goes in v3:
time: 115 us; the launch traced here: 114 us
  blocking collectives  50.3 us (44%)
  starting transfers between devices  32.1 us (28%)
  waiting for transfers between devices  17.5 us (15%)
  Pallas kernels  9.07 us (8%)
  local copies, waits for them, and re-layouts  4.46 us (4%)
    all_to_all x3, blocking collectives, exchange(): return lax.all_to_all(x, AXES, 0, 0, axis_index_groups=groups, tiled=True)  50.3 us
    ppermute x3, starting transfers between devices, body(): lax.ppermute(passages, 'pb', [(i, (i + shift) % n) for i in range(n)])  13.1 us
    all_to_all x1, starting transfers between devices, exchange(): return lax.all_to_all(x, AXES, 0, 0, axis_index_groups=groups, tiled=True)  10.3 us
    all_to_all x1, waiting for transfers between devices, exchange(): return lax.all_to_all(x, AXES, 0, 0, axis_index_groups=groups, tiled=True)  8.9 us
    ppermute x4, starting transfers between devices, swap(): return lax.ppermute(block, 'rep', [(0, 1), (1, 0)])  8.77 us
    ppermute x3, waiting for transfers between devices, body(): lax.ppermute(passages, 'pb', [(i, (i + shift) % n) for i in range(n)])  8.62 us
    pallas_call x1, Pallas kernels, body(): pl.pallas_call(local_kernel, out_shape=jax.ShapeDtypeStruct((rows, 3 * co...  4.53 us
    unnamed x12, local copies, waits for them, and re-layouts  3.51 us
  transfers between devices with their start and end apart: 8, of which 2 were waited for; matrix products, arithmetic and copies ran while one was open for 0% of the time, Pallas kernels for 2%

profile of v3, /device:TPU:6, one launch (start us, length us, event | category | flops | bytes accessed | tf_op | source)
XLA Modules:
  0.0 114.4 jit_solution(16405686053650523698)
XLA Ops:
  0.6 7.8 %collective-permute-start = (bf16[1024,256]{1,0:T(8,128)(2,1)}, bf16[1024,256]{1,0:T(8,128)(2,1)S(1)}, u32[]{:S(2)}, u32[]{:S(2)}) collective-permute-start(bf16[1024,256]{1,0:T(8,128)(2,1)} %bitcast.18), channel_id=1, source_target_pairs={{0,2},{2,4},{4,6},{6,0},{1,3},{3,5},{5,7},{7,1},{8,10},{10,12},{12... | collective-permute-start | bytes 1572872 | tf_op jit(solution)/shard_map/ppermute | solution.py:240
  8.4 1.9 %collective-permute-start.3 = (bf16[1024,256]{1,0:T(8,128)(2,1)}, bf16[1024,256]{1,0:T(8,128)(2,1)S(1)}, u32[]{:S(2)}, u32[]{:S(2)}) collective-permute-start(bf16[1024,256]{1,0:T(8,128)(2,1)} %bitcast.19), channel_id=1, source_target_pairs={{0,6},{2,0},{4,2},{6,4},{1,7},{3,1},{5,3},{7,5},{8,14},{10,8},{12,... | collective-permute-start | bytes 1572872 | tf_op jit(solution)/shard_map/ppermute | solution.py:240
  10.3 3.4 %collective-permute-start.5 = (bf16[1024,256]{1,0:T(8,128)(2,1)}, bf16[1024,256]{1,0:T(8,128)(2,1)S(1)}, u32[]{:S(2)}, u32[]{:S(2)}) collective-permute-start(bf16[1024,256]{1,0:T(8,128)(2,1)} %bitcast.20), channel_id=1, source_target_pairs={{0,4},{2,6},{4,0},{6,2},{1,5},{3,7},{5,1},{7,3},{8,12},{10,14},{12... | collective-permute-start | bytes 1572872 | tf_op jit(solution)/shard_map/ppermute | solution.py:240
  13.7 1.9 %collective-permute-start.1 = (bf16[1024,256]{1,0:T(8,128)(2,1)}, bf16[1024,256]{1,0:T(8,128)(2,1)S(1)}, u32[]{:S(2)}, u32[]{:S(2)}) collective-permute-start(bf16[1024,256]{1,0:T(8,128)(2,1)} %bitcast.21), channel_id=1, source_target_pairs={{0,1},{1,0},{2,3},{3,2},{4,5},{5,4},{6,7},{7,6},{8,9},{9,8},{10,11... | collective-permute-start | bytes 1572872 | tf_op jit(solution)/shard_map/ppermute | solution.py:201
  15.7 0.1 stack.35.block_ref
  15.8 1.2 %copy-done = bf16[2048,256]{1,0:T(8,128)(2,1)S(1)} copy-done((bf16[2048,256]{1,0:T(8,128)(2,1)S(1)}, bf16[2048,256]{1,0:T(8,128)(2,1)}, u32[]{:S(2)}) %copy-start) | copy-done | bytes 1048600
  17.0 1.2 %copy-done.1 = bf16[2048,256]{1,0:T(8,128)(2,1)S(1)} copy-done((bf16[2048,256]{1,0:T(8,128)(2,1)S(1)}, bf16[2048,256]{1,0:T(8,128)(2,1)}, u32[]{:S(2)}) %copy-start.1) | copy-done | bytes 1048600
  18.2 1.0 copy-done.2
  19.3 1.0 own_projection.1
  20.3 0.0 collective-permute-done.refs_1_
  20.3 0.0 copy-start.3
  20.3 0.0 copy-start.4
  20.4 0.0 copy-start.5
  20.4 2.5 %collective-permute-start.2 = (bf16[1024,256]{1,0:T(8,128)(2,1)S(1)}, bf16[1024,256]{1,0:T(8,128)(2,1)S(1)}, u32[]{:S(2)}, u32[]{:S(2)}) collective-permute-start(bf16[1024,256]{1,0:T(8,128)(2,1)S(1)} %collective-permute-done.refs_1_), channel_id=1, source_target_pairs={{0,1},{1,0},{2,3},{3,2},{4,5},{5,4},{6,7},{7,6},{8,9},{9,8},{10,11... | collective-permute-start | bytes 1572872 | tf_op jit(solution)/shard_map/ppermute | solution.py:201
  22.9 8.6 %collective-permute-done.3.refs_3_ = bf16[1024,256]{1,0:T(8,128)(2,1)S(1)} collective-permute-done((bf16[1024,256]{1,0:T(8,128)(2,1)}, bf16[1024,256]{1,0:T(8,128)(2,1)S(1)}, u32[]{:S(2)}, u32[]{:S(2)}) %collective-permute-start.3) | collective-permute-done | bytes 524320 | tf_op jit(solution)/shard_map/ppermute | solution.py:240
  31.5 1.9 %collective-permute-start.4 = (bf16[1024,256]{1,0:T(8,128)(2,1)S(1)}, bf16[1024,256]{1,0:T(8,128)(2,1)S(1)}, u32[]{:S(2)}, u32[]{:S(2)}) collective-permute-start(bf16[1024,256]{1,0:T(8,128)(2,1)S(1)} %collective-permute-done.3.refs_3_), channel_id=1, source_target_pairs={{0,1},{1,0},{2,3},{3,2},{4,5},{5,4},{6,7},{7,6},{8,9},{9,8},{10,11... | collective-permute-start | bytes 1572872 | tf_op jit(solution)/shard_map/ppermute | solution.py:201
  33.4 0.0 collective-permute-done.5.refs_5_
  33.5 2.4 %collective-permute-start.6 = (bf16[1024,256]{1,0:T(8,128)(2,1)S(1)}, bf16[1024,256]{1,0:T(8,128)(2,1)S(1)}, u32[]{:S(2)}, u32[]{:S(2)}) collective-permute-start(bf16[1024,256]{1,0:T(8,128)(2,1)S(1)} %collective-permute-done.5.refs_5_), channel_id=1, source_target_pairs={{0,1},{1,0},{2,3},{3,2},{4,5},{5,4},{6,7},{7,6},{8,9},{9,8},{10,11... | collective-permute-start | bytes 1572872 | tf_op jit(solution)/shard_map/ppermute | solution.py:201
  35.9 0.0 collective-permute-done.1.refs_0_
  35.9 0.0 collective-permute-done.2.refs_2_
  35.9 0.0 collective-permute-done.4.refs_4_
  35.9 1.8 %near_projection.1.acc_ref = f32[1024,512]{1,0:T(8,128)S(1)} custom-call(f32[1024,512]{1,0:T(8,128)S(1)} %get-tuple-element.9.acc_ref, bf16[1792,512]{1,0:T(8,128)(2,1)S(1)} %get-tuple-element.10.rest_ref.refs_1_, bf16[1024,256]{1,0:T(8,128)(2,1)S(1)} %collective-permute-done.1.refs_0_, bf16[1024,256]{1,0:T(8,128)(2,1)S(1)} %collective-permute-done.refs_1_, ...), custom_call_target="tpu_custom_call" | custom-call | tf_op jit(solution)/shard_map/near_projection/pallas_call | solution.py:257
  37.7 0.0 collective-permute-done.6.refs_0_
  37.7 4.5 %local_sums.1 = bf16[512,896]{1,0:T(8,128)(2,1)S(1)} custom-call(s32[32]{0:T(128)S(1)} %copy-done.5, f32[1024,512]{1,0:T(8,128)S(1)} %near_projection.1.acc_ref, bf16[1024,256]{1,0:T(8,128)(2,1)S(1)} %collective-permute-done.6.refs_0_, bf16[1792,512]{1,0:T(8,128)(2,1)S(1)} %get-tuple-element.10.rest_ref.refs_1_, bf16[512,256]{1,0:T(8,128)(2,1)S(1)} %copy-done.4, ...), custom_call_target="tpu_custom_call" | custom-call | tf_op jit(solution)/shard_map/local_sums/pallas_call | solution.py:265
  42.3 23.8 %all_to_all.40 = bf16[8,64,896]{2,1,0:T(8,128)(2,1)S(1)} all-to-all(bf16[8,64,896]{2,1,0:T(8,128)(2,1)S(1)} %bitcast.17), channel_id=1, replica_groups={{0,8,16,24,32,40,48,56},{2,10,18,26,34,42,50,58},{4,12,20,28,36,44,52,6..., dimensions={0} | all-to-all | bytes 1835008 | tf_op jit(solution)/shard_map/all_to_all | solution.py:228
  66.1 1.4 %line_sums.1 = bf16[64,896]{1,0:T(8,128)(2,1)} custom-call(bf16[512,896]{1,0:T(8,128)(2,1)S(1)} %bitcast.16), custom_call_target="tpu_custom_call" | custom-call | tf_op jit(solution)/shard_map/line_sums/pallas_call | solution.py:289
  67.5 10.3 %all-to-all-start.1 = ((bf16[8,8,896]{2,1,0:T(8,128)(2,1)}), bf16[8,8,896]{2,1,0:T(8,128)(2,1)S(1)}, u32[]{:S(2)}, u32[]{:S(2)}) async-start(bf16[8,8,896]{2,1,0:T(8,128)(2,1)} %bitcast.11), calls=%async_computation.1 | async-start | bytes 229376 | tf_op jit(solution)/shard_map/all_to_all | solution.py:228
  77.8 8.9 %all-to-all-done.1 = bf16[8,8,896]{2,1,0:T(8,128)(2,1)S(1)} async-done(((bf16[8,8,896]{2,1,0:T(8,128)(2,1)}), bf16[8,8,896]{2,1,0:T(8,128)(2,1)S(1)}, u32[]{:S(2)}, u32[]{:S(2)}) %all-to-all-start.1) | async-done | bytes 114720 | tf_op jit(solution)/shard_map/all_to_all | solution.py:228
  86.7 0.3 final_sums.1
  87.0 10.8 %all_to_all.41 = bf16[8,8,512]{2,1,0:T(8,128)(2,1)S(1)} all-to-all(bf16[8,8,512]{2,1,0:T(8,128)(2,1)S(1)} %bitcast.24), channel_id=1, replica_groups={{0,64,128,192,256,320,384,448},{2,66,130,194,258,322,386,450},{4,68,132..., dimensions={0} | all-to-all | bytes 131072 | tf_op jit(solution)/shard_map/all_to_all | solution.py:228
  97.8 15.7 %all_to_all.42 = bf16[8,64,512]{2,1,0:T(8,128)(2,1)S(1)} all-to-all(bf16[8,64,512]{2,1,0:T(8,128)(2,1)S(1)} %broadcast_in_dim.9), channel_id=1, replica_groups={{0,8,16,24,32,40,48,56},{2,10,18,26,34,42,50,58},{4,12,20,28,36,44,52,6..., dimensions={0} | all-to-all | bytes 1048576 | tf_op jit(solution)/shard_map/all_to_all | solution.py:228
  113.5 0.8 fusion
  (8 shorter events, 0.1 us)
Async XLA Ops:
  0.6 19.7 %collective-permute-start = (bf16[1024,256]{1,0:T(8,128)(2,1)}, bf16[1024,256]{1,0:T(8,128)(2,1)S(1)}, u32[]{:S(2)}, u32[]{:S(2)}) collective-permute-start(bf16[1024,256]{1,0:T(8,128)(2,1)} %bitcast.18), channel_id=1, source_target_pairs={{0,2},{2,4},{4,6},{6,0},{1,3},{3,5},{5,7},{7,1},{8,10},{10,12},{12... | collective-permute-start | bytes 1572872 | tf_op jit(solution)/shard_map/ppermute | solution.py:240
  8.4 23.1 %collective-permute-start.3 = (bf16[1024,256]{1,0:T(8,128)(2,1)}, bf16[1024,256]{1,0:T(8,128)(2,1)S(1)}, u32[]{:S(2)}, u32[]{:S(2)}) collective-permute-start(bf16[1024,256]{1,0:T(8,128)(2,1)} %bitcast.19), channel_id=1, source_target_pairs={{0,6},{2,0},{4,2},{6,4},{1,7},{3,1},{5,3},{7,5},{8,14},{10,8},{12,... | collective-permute-start | bytes 1572872 | tf_op jit(solution)/shard_map/ppermute | solution.py:240
  10.3 23.1 %collective-permute-start.5 = (bf16[1024,256]{1,0:T(8,128)(2,1)}, bf16[1024,256]{1,0:T(8,128)(2,1)S(1)}, u32[]{:S(2)}, u32[]{:S(2)}) collective-permute-start(bf16[1024,256]{1,0:T(8,128)(2,1)} %bitcast.20), channel_id=1, source_target_pairs={{0,4},{2,6},{4,0},{6,2},{1,5},{3,7},{5,1},{7,3},{8,12},{10,14},{12... | collective-permute-start | bytes 1572872 | tf_op jit(solution)/shard_map/ppermute | solution.py:240
  13.7 22.2 %collective-permute-start.1 = (bf16[1024,256]{1,0:T(8,128)(2,1)}, bf16[1024,256]{1,0:T(8,128)(2,1)S(1)}, u32[]{:S(2)}, u32[]{:S(2)}) collective-permute-start(bf16[1024,256]{1,0:T(8,128)(2,1)} %bitcast.21), channel_id=1, source_target_pairs={{0,1},{1,0},{2,3},{3,2},{4,5},{5,4},{6,7},{7,6},{8,9},{9,8},{10,11... | collective-permute-start | bytes 1572872 | tf_op jit(solution)/shard_map/ppermute | solution.py:201
  15.8 1.2 %copy-start = (bf16[2048,256]{1,0:T(8,128)(2,1)S(1)}, bf16[2048,256]{1,0:T(8,128)(2,1)}, u32[]{:S(2)}) copy-start(bf16[2048,256]{1,0:T(8,128)(2,1)} %wk_ref.1) | copy-start | bytes 3145732
  17.0 1.2 %copy-start.1 = (bf16[2048,256]{1,0:T(8,128)(2,1)S(1)}, bf16[2048,256]{1,0:T(8,128)(2,1)}, u32[]{:S(2)}) copy-start(bf16[2048,256]{1,0:T(8,128)(2,1)} %wv_ref.1) | copy-start | bytes 3145732
  18.2 1.0 copy-start.2
  20.3 17.4 %copy-start.3 = (bf16[512,256]{1,0:T(8,128)(2,1)S(1)}, bf16[512,256]{1,0:T(8,128)(2,1)}, u32[]{:S(2)}) copy-start(bf16[512,256]{1,0:T(8,128)(2,1)} %refs_3_.1) | copy-start | bytes 786436
  20.3 17.4 %copy-start.4 = (bf16[512,256]{1,0:T(8,128)(2,1)S(1)}, bf16[512,256]{1,0:T(8,128)(2,1)}, u32[]{:S(2)}) copy-start(bf16[512,256]{1,0:T(8,128)(2,1)} %refs_2_.1) | copy-start | bytes 786436
  20.4 17.4 %copy-start.5 = (s32[32]{0:T(128)S(1)}, s32[32]{0:T(128)}, u32[]{:S(2)}) copy-start(s32[32]{0:T(128)} %owner_ref.1) | copy-start | bytes 388
  20.4 15.5 %collective-permute-start.2 = (bf16[1024,256]{1,0:T(8,128)(2,1)S(1)}, bf16[1024,256]{1,0:T(8,128)(2,1)S(1)}, u32[]{:S(2)}, u32[]{:S(2)}) collective-permute-start(bf16[1024,256]{1,0:T(8,128)(2,1)S(1)} %collective-permute-done.refs_1_), channel_id=1, source_target_pairs={{0,1},{1,0},{2,3},{3,2},{4,5},{5,4},{6,7},{7,6},{8,9},{9,8},{10,11... | collective-permute-start | bytes 1572872 | tf_op jit(solution)/shard_map/ppermute | solution.py:201
  31.5 4.4 %collective-permute-start.4 = (bf16[1024,256]{1,0:T(8,128)(2,1)S(1)}, bf16[1024,256]{1,0:T(8,128)(2,1)S(1)}, u32[]{:S(2)}, u32[]{:S(2)}) collective-permute-start(bf16[1024,256]{1,0:T(8,128)(2,1)S(1)} %collective-permute-done.3.refs_3_), channel_id=1, source_target_pairs={{0,1},{1,0},{2,3},{3,2},{4,5},{5,4},{6,7},{7,6},{8,9},{9,8},{10,11... | collective-permute-start | bytes 1572872 | tf_op jit(solution)/shard_map/ppermute | solution.py:201
  33.5 4.3 %collective-permute-start.6 = (bf16[1024,256]{1,0:T(8,128)(2,1)S(1)}, bf16[1024,256]{1,0:T(8,128)(2,1)S(1)}, u32[]{:S(2)}, u32[]{:S(2)}) collective-permute-start(bf16[1024,256]{1,0:T(8,128)(2,1)S(1)} %collective-permute-done.5.refs_5_), channel_id=1, source_target_pairs={{0,1},{1,0},{2,3},{3,2},{4,5},{5,4},{6,7},{7,6},{8,9},{9,8},{10,11... | collective-permute-start | bytes 1572872 | tf_op jit(solution)/shard_map/ppermute | solution.py:201
  67.5 19.2 %all-to-all-start.1 = ((bf16[8,8,896]{2,1,0:T(8,128)(2,1)}), bf16[8,8,896]{2,1,0:T(8,128)(2,1)S(1)}, u32[]{:S(2)}, u32[]{:S(2)}) async-start(bf16[8,8,896]{2,1,0:T(8,128)(2,1)} %bitcast.11), calls=%async_computation.1 | async-start | bytes 229376 | tf_op jit(solution)/shard_map/all_to_all | solution.py:228

commit v4 on v2

--- a/solution.py
+++ b/solution.py
@@ -187,9 +187,9 @@
 
     passages = prefixes.reshape(slots * vectors, features)
     n = lax.axis_size("pb")
-    left, right, far = (
-        lax.ppermute(passages, "pb", [(i, (i + shift) % n) for i in range(n)]) for shift in (1, n - 1, 2)
-    )
+    to_right = [(i, (i + 1) % n) for i in range(n)]
+    left = lax.ppermute(passages, "pb", to_right)
+    right = lax.ppermute(passages, "pb", [(i, (i - 1) % n) for i in range(n)])
     other = swap(passages)
     smem = pl.BlockSpec(memory_space=pltpu.SMEM)
     vmem = pl.BlockSpec(memory_space=pltpu.VMEM)
@@ -203,6 +203,7 @@
         name="own_projection",
     )(block_numbers(), passages, key_weight, value_weight)
     left, projected, rest = lax.optimization_barrier((left, projected, rest))
+    far = lax.ppermute(left, "pb", to_right)
     near = [other, left, swap(left), right, swap(right), far]
     far = swap(far)
     projected = pl.pallas_call(

time: 113 us -> 114 us (level)
  the two profiles are of different devices: /device:TPU:6 before, /device:TPU:8 now
where the time goes in v4:
time: 114 us
  waiting for transfers between devices  39.8 us (35%)
  starting transfers between devices  34.1 us (30%)
  blocking collectives  25.8 us (23%)
  Pallas kernels  8.95 us (8%)
  local copies, waits for them, and re-layouts  4.41 us (4%)
    all_to_all x1, waiting for transfers between devices, body(): received = lax.all_to_all(payload, 'psg', 0, 0, tiled=True)  27.1 us
    all_to_all x1, blocking collectives, body(): outputs = lax.all_to_all(finished, 'psg', 0, 0, tiled=True)  25.8 us
    all_to_all x1, starting transfers between devices, body(): received = lax.all_to_all(payload, 'psg', 0, 0, tiled=True)  16.6 us
    ppermute x4, starting transfers between devices, swap(): return lax.ppermute(block, 'rep', [(0, 1), (1, 0)])  8.16 us
    ppermute x1, waiting for transfers between devices, body(): far = lax.ppermute(left, 'pb', to_right)  7.42 us
    pallas_call x1, Pallas kernels, body(): pl.pallas_call(local_kernel, out_shape=jax.ShapeDtypeStruct((rows, 3 * co...  5.44 us
    ppermute x1, waiting for transfers between devices, body(): left = lax.ppermute(passages, 'pb', to_right)  5.22 us
    ppermute x1, starting transfers between devices, body(): right = lax.ppermute(passages, 'pb', [(i, (i - 1) % n) for i in range(n)])  3.66 us
  transfers between devices with their start and end apart: 8, of which 3 were waited for; matrix products, arithmetic and copies ran while one was open for 0% of the time, Pallas kernels for 2%

profile of v4, /device:TPU:8, one launch (start us, length us, event | category | flops | bytes accessed | tf_op | source)
XLA Modules:
  0.0 113.9 jit_solution(3923383367970634266)
XLA Ops:
  0.6 3.4 %collective-permute-start = (bf16[1024,256]{1,0:T(8,128)(2,1)}, bf16[1024,256]{1,0:T(8,128)(2,1)S(1)}, u32[]{:S(2)}, u32[]{:S(2)}) collective-permute-start(bf16[1024,256]{1,0:T(8,128)(2,1)} %bitcast.15), channel_id=1, source_target_pairs={{0,2},{2,4},{4,6},{6,0},{1,3},{3,5},{5,7},{7,1},{8,10},{10,12},{12... | collective-permute-start | bytes 1572872 | tf_op jit(solution)/shard_map/ppermute | solution.py:191
  4.0 3.7 %collective-permute-start.3 = (bf16[1024,256]{1,0:T(8,128)(2,1)}, bf16[1024,256]{1,0:T(8,128)(2,1)S(1)}, u32[]{:S(2)}, u32[]{:S(2)}) collective-permute-start(bf16[1024,256]{1,0:T(8,128)(2,1)} %bitcast.16), channel_id=1, source_target_pairs={{0,6},{2,0},{4,2},{6,4},{1,7},{3,1},{5,3},{7,5},{8,14},{10,8},{12,... | collective-permute-start | bytes 1572872 | tf_op jit(solution)/shard_map/ppermute | solution.py:192
  7.7 0.1 stack.35.block_ref
  7.8 0.0 copy-start
  7.8 1.2 %copy-done = bf16[2048,256]{1,0:T(8,128)(2,1)S(1)} copy-done((bf16[2048,256]{1,0:T(8,128)(2,1)S(1)}, bf16[2048,256]{1,0:T(8,128)(2,1)}, u32[]{:S(2)}) %copy-start) | copy-done | bytes 1048600
  9.1 0.0 copy-start.1
  9.1 1.2 %copy-done.1 = bf16[2048,256]{1,0:T(8,128)(2,1)S(1)} copy-done((bf16[2048,256]{1,0:T(8,128)(2,1)S(1)}, bf16[2048,256]{1,0:T(8,128)(2,1)}, u32[]{:S(2)}) %copy-start.1) | copy-done | bytes 1048600
  10.3 0.0 copy-start.2
  10.3 1.0 copy-done.2
  11.3 1.0 own_projection.1
  12.4 5.2 %collective-permute-done.refs_1_ = bf16[1024,256]{1,0:T(8,128)(2,1)S(1)} collective-permute-done((bf16[1024,256]{1,0:T(8,128)(2,1)}, bf16[1024,256]{1,0:T(8,128)(2,1)S(1)}, u32[]{:S(2)}, u32[]{:S(2)}) %collective-permute-start) | collective-permute-done | bytes 524320 | tf_op jit(solution)/shard_map/ppermute | solution.py:191
  17.6 2.3 %collective-permute-start.5 = (bf16[1024,256]{1,0:T(8,128)(2,1)S(1)}, bf16[1024,256]{1,0:T(8,128)(2,1)S(1)}, u32[]{:S(2)}, u32[]{:S(2)}) collective-permute-start(bf16[1024,256]{1,0:T(8,128)(2,1)S(1)} %collective-permute-done.refs_1_), channel_id=1, source_target_pairs={{0,2},{2,4},{4,6},{6,0},{1,3},{3,5},{5,7},{7,1},{8,10},{10,12},{12... | collective-permute-start | bytes 1572872 | tf_op jit(solution)/shard_map/ppermute | solution.py:206
  19.9 1.9 %collective-permute-start.1 = (bf16[1024,256]{1,0:T(8,128)(2,1)S(1)}, bf16[1024,256]{1,0:T(8,128)(2,1)S(1)}, u32[]{:S(2)}, u32[]{:S(2)}) collective-permute-start(bf16[1024,256]{1,0:T(8,128)(2,1)S(1)} %bitcast.18), channel_id=1, source_target_pairs={{0,1},{1,0},{2,3},{3,2},{4,5},{5,4},{6,7},{7,6},{8,9},{9,8},{10,11... | collective-permute-start | bytes 1572872 | tf_op jit(solution)/shard_map/ppermute | solution.py:169
  21.9 2.4 %collective-permute-start.2 = (bf16[1024,256]{1,0:T(8,128)(2,1)S(1)}, bf16[1024,256]{1,0:T(8,128)(2,1)S(1)}, u32[]{:S(2)}, u32[]{:S(2)}) collective-permute-start(bf16[1024,256]{1,0:T(8,128)(2,1)S(1)} %collective-permute-done.refs_1_), channel_id=1, source_target_pairs={{0,1},{1,0},{2,3},{3,2},{4,5},{5,4},{6,7},{7,6},{8,9},{9,8},{10,11... | collective-permute-start | bytes 1572872 | tf_op jit(solution)/shard_map/ppermute | solution.py:169
  24.3 0.0 collective-permute-done.3.refs_3_
  24.3 1.9 %collective-permute-start.4 = (bf16[1024,256]{1,0:T(8,128)(2,1)S(1)}, bf16[1024,256]{1,0:T(8,128)(2,1)S(1)}, u32[]{:S(2)}, u32[]{:S(2)}) collective-permute-start(bf16[1024,256]{1,0:T(8,128)(2,1)S(1)} %collective-permute-done.3.refs_3_), channel_id=1, source_target_pairs={{0,1},{1,0},{2,3},{3,2},{4,5},{5,4},{6,7},{7,6},{8,9},{9,8},{10,11... | collective-permute-start | bytes 1572872 | tf_op jit(solution)/shard_map/ppermute | solution.py:169
  26.2 7.4 %collective-permute-done.5.refs_5_ = bf16[1024,256]{1,0:T(8,128)(2,1)S(1)} collective-permute-done((bf16[1024,256]{1,0:T(8,128)(2,1)S(1)}, bf16[1024,256]{1,0:T(8,128)(2,1)S(1)}, u32[]{:S(2)}, u32[]{:S(2)}) %collective-permute-start.5) | collective-permute-done | bytes 524320 | tf_op jit(solution)/shard_map/ppermute | solution.py:206
  33.6 1.9 %collective-permute-start.6 = (bf16[1024,256]{1,0:T(8,128)(2,1)S(1)}, bf16[1024,256]{1,0:T(8,128)(2,1)S(1)}, u32[]{:S(2)}, u32[]{:S(2)}) collective-permute-start(bf16[1024,256]{1,0:T(8,128)(2,1)S(1)} %collective-permute-done.5.refs_5_), channel_id=1, source_target_pairs={{0,1},{1,0},{2,3},{3,2},{4,5},{5,4},{6,7},{7,6},{8,9},{9,8},{10,11... | collective-permute-start | bytes 1572872 | tf_op jit(solution)/shard_map/ppermute | solution.py:169
  35.5 0.0 collective-permute-done.1.refs_0_
  35.6 0.0 collective-permute-done.2.refs_2_
  35.6 0.0 collective-permute-done.4.refs_4_
  35.6 1.8 %near_projection.1.acc_ref = f32[1024,512]{1,0:T(8,128)S(1)} custom-call(f32[1024,512]{1,0:T(8,128)S(1)} %get-tuple-element.9.acc_ref, bf16[1792,512]{1,0:T(8,128)(2,1)S(1)} %get-tuple-element.10.rest_ref.refs_1_, bf16[1024,256]{1,0:T(8,128)(2,1)S(1)} %collective-permute-done.1.refs_0_, bf16[1024,256]{1,0:T(8,128)(2,1)S(1)} %collective-permute-done.refs_1_, ...), custom_call_target="tpu_custom_call" | custom-call | tf_op jit(solution)/shard_map/near_projection/pallas_call | solution.py:209
  37.4 0.0 collective-permute-done.6.refs_0_
  37.4 0.0 copy-done.3
  37.4 0.0 copy-done.4
  37.4 0.0 copy-done.5
  37.4 5.4 %local_sums.1 = bf16[512,896]{1,0:T(8,128)(2,1)} custom-call(s32[32]{0:T(128)S(1)} %copy-done.5, f32[1024,512]{1,0:T(8,128)S(1)} %near_projection.1.acc_ref, bf16[1024,256]{1,0:T(8,128)(2,1)S(1)} %collective-permute-done.6.refs_0_, bf16[1792,512]{1,0:T(8,128)(2,1)S(1)} %get-tuple-element.10.rest_ref.refs_1_, bf16[512,256]{1,0:T(8,128)(2,1)S(1)} %copy-done.4, ...), custom_call_target="tpu_custom_call" | custom-call | tf_op jit(solution)/shard_map/local_sums/pallas_call | solution.py:217
  42.9 16.6 %all-to-all-start = ((bf16[64,8,896]{2,1,0:T(8,128)(2,1)}), bf16[64,8,896]{2,1,0:T(8,128)(2,1)S(1)}, u32[]{:S(2)}, u32[]{:S(2)}) async-start(bf16[64,8,896]{2,1,0:T(8,128)(2,1)} %bitcast.9), calls=%async_computation | async-start | bytes 1835008 | tf_op jit(solution)/shard_map/all_to_all | solution.py:238
  59.5 27.1 %all-to-all-done = bf16[64,8,896]{2,1,0:T(8,128)(2,1)S(1)} async-done(((bf16[64,8,896]{2,1,0:T(8,128)(2,1)}), bf16[64,8,896]{2,1,0:T(8,128)(2,1)S(1)}, u32[]{:S(2)}, u32[]{:S(2)}) %all-to-all-start) | async-done | bytes 917536 | tf_op jit(solution)/shard_map/all_to_all | solution.py:238
  86.6 0.7 final_sums.1
  87.2 25.8 %all_to_all.23 = bf16[64,8,512]{2,1,0:T(8,128)(2,1)S(1)} all-to-all(bf16[64,8,512]{2,1,0:T(8,128)(2,1)S(1)} %bitcast.14), channel_id=1, replica_groups=mesh['psg'=64,'pb'=4,'rep'=2] {'psg'}, dimensions={0} | all-to-all | bytes 1048576 | tf_op jit(solution)/shard_map/all_to_all | solution.py:248
  113.1 0.8 fusion
  (4 shorter events, 0.0 us)
Async XLA Ops:
  0.6 17.0 %collective-permute-start = (bf16[1024,256]{1,0:T(8,128)(2,1)}, bf16[1024,256]{1,0:T(8,128)(2,1)S(1)}, u32[]{:S(2)}, u32[]{:S(2)}) collective-permute-start(bf16[1024,256]{1,0:T(8,128)(2,1)} %bitcast.15), channel_id=1, source_target_pairs={{0,2},{2,4},{4,6},{6,0},{1,3},{3,5},{5,7},{7,1},{8,10},{10,12},{12... | collective-permute-start | bytes 1572872 | tf_op jit(solution)/shard_map/ppermute | solution.py:191
  4.0 20.2 %collective-permute-start.3 = (bf16[1024,256]{1,0:T(8,128)(2,1)}, bf16[1024,256]{1,0:T(8,128)(2,1)S(1)}, u32[]{:S(2)}, u32[]{:S(2)}) collective-permute-start(bf16[1024,256]{1,0:T(8,128)(2,1)} %bitcast.16), channel_id=1, source_target_pairs={{0,6},{2,0},{4,2},{6,4},{1,7},{3,1},{5,3},{7,5},{8,14},{10,8},{12,... | collective-permute-start | bytes 1572872 | tf_op jit(solution)/shard_map/ppermute | solution.py:192
  7.8 1.2 %copy-start = (bf16[2048,256]{1,0:T(8,128)(2,1)S(1)}, bf16[2048,256]{1,0:T(8,128)(2,1)}, u32[]{:S(2)}) copy-start(bf16[2048,256]{1,0:T(8,128)(2,1)} %wk_ref.1) | copy-start | bytes 3145732
  9.1 1.2 %copy-start.1 = (bf16[2048,256]{1,0:T(8,128)(2,1)S(1)}, bf16[2048,256]{1,0:T(8,128)(2,1)}, u32[]{:S(2)}) copy-start(bf16[2048,256]{1,0:T(8,128)(2,1)} %wv_ref.1) | copy-start | bytes 3145732
  10.3 1.0 copy-start.2
  17.6 19.8 %copy-start.3 = (bf16[512,256]{1,0:T(8,128)(2,1)S(1)}, bf16[512,256]{1,0:T(8,128)(2,1)}, u32[]{:S(2)}) copy-start(bf16[512,256]{1,0:T(8,128)(2,1)} %refs_3_.1) | copy-start | bytes 786436
  17.6 19.8 %copy-start.4 = (bf16[512,256]{1,0:T(8,128)(2,1)S(1)}, bf16[512,256]{1,0:T(8,128)(2,1)}, u32[]{:S(2)}) copy-start(bf16[512,256]{1,0:T(8,128)(2,1)} %refs_2_.1) | copy-start | bytes 786436
  17.6 19.8 %copy-start.5 = (s32[32]{0:T(128)S(1)}, s32[32]{0:T(128)}, u32[]{:S(2)}) copy-start(s32[32]{0:T(128)} %owner_ref.1) | copy-start | bytes 388
  17.6 16.0 %collective-permute-start.5 = (bf16[1024,256]{1,0:T(8,128)(2,1)S(1)}, bf16[1024,256]{1,0:T(8,128)(2,1)S(1)}, u32[]{:S(2)}, u32[]{:S(2)}) collective-permute-start(bf16[1024,256]{1,0:T(8,128)(2,1)S(1)} %collective-permute-done.refs_1_), channel_id=1, source_target_pairs={{0,2},{2,4},{4,6},{6,0},{1,3},{3,5},{5,7},{7,1},{8,10},{10,12},{12... | collective-permute-start | bytes 1572872 | tf_op jit(solution)/shard_map/ppermute | solution.py:206
  19.9 15.6 %collective-permute-start.1 = (bf16[1024,256]{1,0:T(8,128)(2,1)S(1)}, bf16[1024,256]{1,0:T(8,128)(2,1)S(1)}, u32[]{:S(2)}, u32[]{:S(2)}) collective-permute-start(bf16[1024,256]{1,0:T(8,128)(2,1)S(1)} %bitcast.18), channel_id=1, source_target_pairs={{0,1},{1,0},{2,3},{3,2},{4,5},{5,4},{6,7},{7,6},{8,9},{9,8},{10,11... | collective-permute-start | bytes 1572872 | tf_op jit(solution)/shard_map/ppermute | solution.py:169
  21.9 13.7 %collective-permute-start.2 = (bf16[1024,256]{1,0:T(8,128)(2,1)S(1)}, bf16[1024,256]{1,0:T(8,128)(2,1)S(1)}, u32[]{:S(2)}, u32[]{:S(2)}) collective-permute-start(bf16[1024,256]{1,0:T(8,128)(2,1)S(1)} %collective-permute-done.refs_1_), channel_id=1, source_target_pairs={{0,1},{1,0},{2,3},{3,2},{4,5},{5,4},{6,7},{7,6},{8,9},{9,8},{10,11... | collective-permute-start | bytes 1572872 | tf_op jit(solution)/shard_map/ppermute | solution.py:169
  24.3 11.3 %collective-permute-start.4 = (bf16[1024,256]{1,0:T(8,128)(2,1)S(1)}, bf16[1024,256]{1,0:T(8,128)(2,1)S(1)}, u32[]{:S(2)}, u32[]{:S(2)}) collective-permute-start(bf16[1024,256]{1,0:T(8,128)(2,1)S(1)} %collective-permute-done.3.refs_3_), channel_id=1, source_target_pairs={{0,1},{1,0},{2,3},{3,2},{4,5},{5,4},{6,7},{7,6},{8,9},{9,8},{10,11... | collective-permute-start | bytes 1572872 | tf_op jit(solution)/shard_map/ppermute | solution.py:169
  33.6 3.8 %collective-permute-start.6 = (bf16[1024,256]{1,0:T(8,128)(2,1)S(1)}, bf16[1024,256]{1,0:T(8,128)(2,1)S(1)}, u32[]{:S(2)}, u32[]{:S(2)}) collective-permute-start(bf16[1024,256]{1,0:T(8,128)(2,1)S(1)} %collective-permute-done.5.refs_5_), channel_id=1, source_target_pairs={{0,1},{1,0},{2,3},{3,2},{4,5},{5,4},{6,7},{7,6},{8,9},{9,8},{10,11... | collective-permute-start | bytes 1572872 | tf_op jit(solution)/shard_map/ppermute | solution.py:169
  42.9 43.7 %all-to-all-start = ((bf16[64,8,896]{2,1,0:T(8,128)(2,1)}), bf16[64,8,896]{2,1,0:T(8,128)(2,1)S(1)}, u32[]{:S(2)}, u32[]{:S(2)}) async-start(bf16[64,8,896]{2,1,0:T(8,128)(2,1)} %bitcast.9), calls=%async_computation | async-start | bytes 1835008 | tf_op jit(solution)/shard_map/all_to_all | solution.py:238

commit v5 on v2

--- a/solution.py
+++ b/solution.py
@@ -172,9 +172,20 @@
 def block_numbers():
     n = lax.axis_size("pb")
     pb, rep = lax.axis_index("pb"), lax.axis_index("rep")
-    places = [(pb + shift) % n for shift in (0, n - 1, 1, 2)]
-    numbers = [number for place in places for number in (place * 2 + rep, place * 2 + 1 - rep)]
+    step = 1 - 2 * rep
+    own = [(pb + shift) % n for shift in (0, n - step, n + step, 2)]
+    other = [(pb + shift) % n for shift in (0, n + step, n - step, 2)]
+    numbers = [number for pair in zip(own, other) for number in (pair[0] * 2 + rep, pair[1] * 2 + 1 - rep)]
     return jnp.stack(numbers).astype(jnp.int32)
+
+
+def along(block, way):
+    n = lax.axis_size("pb")
+    pairs = []
+    for chip in range(n):
+        pairs.append((chip * 2, (chip + way) % n * 2))
+        pairs.append((chip * 2 + 1, (chip - way) % n * 2 + 1))
+    return lax.ppermute(block, ("pb", "rep"), pairs)
 
 
 def body(queries, prefixes, owner, key_weight, value_weight, cotangent):
@@ -186,10 +197,7 @@
     own = rows // devices
 
     passages = prefixes.reshape(slots * vectors, features)
-    n = lax.axis_size("pb")
-    left, right, far = (
-        lax.ppermute(passages, "pb", [(i, (i + shift) % n) for i in range(n)]) for shift in (1, n - 1, 2)
-    )
+    ahead, behind = along(passages, 1), along(passages, -1)
     other = swap(passages)
     smem = pl.BlockSpec(memory_space=pltpu.SMEM)
     vmem = pl.BlockSpec(memory_space=pltpu.VMEM)
@@ -202,8 +210,9 @@
         compiler_params=pltpu.CompilerParams(vmem_limit_bytes=16 * 1024 * 1024),
         name="own_projection",
     )(block_numbers(), passages, key_weight, value_weight)
-    left, projected, rest = lax.optimization_barrier((left, projected, rest))
-    near = [other, left, swap(left), right, swap(right), far]
+    ahead, projected, rest = lax.optimization_barrier((ahead, projected, rest))
+    far = along(ahead, 1)
+    near = [other, ahead, swap(ahead), behind, swap(behind), far]
     far = swap(far)
     projected = pl.pallas_call(
         near_kernel,

time: 113 us -> 109 us (0.965)
  waiting for transfers between devices: 35.6 us -> 31.6 us
  starting transfers between devices: 37.8 us -> 36.2 us
    ppermute x3, waiting for transfers between devices: 8.62 us -> 4.28 us  [along(): return lax.ppermute(block, ('pb', 'rep'), pairs)]
    all_to_all x1, starting transfers between devices: 16 us -> 12.6 us  [body(): received = lax.all_to_all(payload, 'psg', 0, 0, tiled=True)]
    ppermute x3, starting transfers between devices: 13.1 us -> 15.3 us  [along(): return lax.ppermute(block, ('pb', 'rep'), pairs)]
  transfers between devices with their start and end apart: 8 -> 8, of which waited for: 2 -> 3; matrix products, arithmetic and copies ran while one was open for 0% -> 0% of each run, Pallas kernels for 3% -> 3%
where the time goes in v5:
time: 109 us; the launch traced here: 108 us
  starting transfers between devices  36.2 us (33%)
  waiting for transfers between devices  31.6 us (29%)
  blocking collectives  25.8 us (24%)
  Pallas kernels  8.95 us (8%)
  local copies, waits for them, and re-layouts  4.41 us (4%)
    all_to_all x1, waiting for transfers between devices, body(): received = lax.all_to_all(payload, 'psg', 0, 0, tiled=True)  27.3 us
    all_to_all x1, blocking collectives, body(): outputs = lax.all_to_all(finished, 'psg', 0, 0, tiled=True)  25.8 us
    ppermute x3, starting transfers between devices, along(): return lax.ppermute(block, ('pb', 'rep'), pairs)  15.3 us
    all_to_all x1, starting transfers between devices, body(): received = lax.all_to_all(payload, 'psg', 0, 0, tiled=True)  12.6 us
    ppermute x4, starting transfers between devices, swap(): return lax.ppermute(block, 'rep', [(0, 1), (1, 0)])  8.27 us
    pallas_call x1, Pallas kernels, body(): pl.pallas_call(local_kernel, out_shape=jax.ShapeDtypeStruct((rows, 3 * co...  5.45 us
    ppermute x3, waiting for transfers between devices, along(): return lax.ppermute(block, ('pb', 'rep'), pairs)  4.28 us
    unnamed x12, local copies, waits for them, and re-layouts  3.5 us
  transfers between devices with their start and end apart: 8, of which 3 were waited for; matrix products, arithmetic and copies ran while one was open for 0% of the time, Pallas kernels for 3%

profile of v5, /device:TPU:6, one launch (start us, length us, event | category | flops | bytes accessed | tf_op | source)
XLA Modules:
  0.0 107.8 jit_solution(10063832695301540306)
XLA Ops:
  0.6 7.8 %collective-permute-start = (bf16[1024,256]{1,0:T(8,128)(2,1)}, bf16[1024,256]{1,0:T(8,128)(2,1)S(1)}, u32[]{:S(2)}, u32[]{:S(2)}) collective-permute-start(bf16[1024,256]{1,0:T(8,128)(2,1)} %bitcast.15), channel_id=1, source_target_pairs={{0,2},{1,7},{2,4},{3,1},{4,6},{5,3},{6,0},{7,5},{8,10},{9,15},{10,... | collective-permute-start | bytes 1572872 | tf_op jit(solution)/shard_map/ppermute | solution.py:188
  8.4 1.9 %collective-permute-start.3 = (bf16[1024,256]{1,0:T(8,128)(2,1)}, bf16[1024,256]{1,0:T(8,128)(2,1)S(1)}, u32[]{:S(2)}, u32[]{:S(2)}) collective-permute-start(bf16[1024,256]{1,0:T(8,128)(2,1)} %bitcast.16), channel_id=1, source_target_pairs={{0,6},{1,3},{2,0},{3,5},{4,2},{5,7},{6,4},{7,1},{8,14},{9,11},{10,... | collective-permute-start | bytes 1572872 | tf_op jit(solution)/shard_map/ppermute | solution.py:188
  10.4 0.1 stack.35.block_ref
  10.5 0.0 copy-start
  10.5 1.2 %copy-done = bf16[2048,256]{1,0:T(8,128)(2,1)S(1)} copy-done((bf16[2048,256]{1,0:T(8,128)(2,1)S(1)}, bf16[2048,256]{1,0:T(8,128)(2,1)}, u32[]{:S(2)}) %copy-start) | copy-done | bytes 1048600
  11.7 0.0 copy-start.1
  11.7 1.2 %copy-done.1 = bf16[2048,256]{1,0:T(8,128)(2,1)S(1)} copy-done((bf16[2048,256]{1,0:T(8,128)(2,1)S(1)}, bf16[2048,256]{1,0:T(8,128)(2,1)}, u32[]{:S(2)}) %copy-start.1) | copy-done | bytes 1048600
  12.9 1.0 copy-done.2
  14.0 1.0 own_projection.1
  15.0 3.9 %collective-permute-done.refs_1_ = bf16[1024,256]{1,0:T(8,128)(2,1)S(1)} collective-permute-done((bf16[1024,256]{1,0:T(8,128)(2,1)}, bf16[1024,256]{1,0:T(8,128)(2,1)S(1)}, u32[]{:S(2)}, u32[]{:S(2)}) %collective-permute-start) | collective-permute-done | bytes 524320 | tf_op jit(solution)/shard_map/ppermute | solution.py:188
  18.9 0.0 copy-start.3
  18.9 5.6 %collective-permute-start.5 = (bf16[1024,256]{1,0:T(8,128)(2,1)S(1)}, bf16[1024,256]{1,0:T(8,128)(2,1)S(1)}, u32[]{:S(2)}, u32[]{:S(2)}) collective-permute-start(bf16[1024,256]{1,0:T(8,128)(2,1)S(1)} %collective-permute-done.refs_1_), channel_id=1, source_target_pairs={{0,2},{1,7},{2,4},{3,1},{4,6},{5,3},{6,0},{7,5},{8,10},{9,15},{10,... | collective-permute-start | bytes 1572872 | tf_op jit(solution)/shard_map/ppermute | solution.py:188
  24.5 1.9 %collective-permute-start.1 = (bf16[1024,256]{1,0:T(8,128)(2,1)S(1)}, bf16[1024,256]{1,0:T(8,128)(2,1)S(1)}, u32[]{:S(2)}, u32[]{:S(2)}) collective-permute-start(bf16[1024,256]{1,0:T(8,128)(2,1)S(1)} %bitcast.18), channel_id=1, source_target_pairs={{0,1},{1,0},{2,3},{3,2},{4,5},{5,4},{6,7},{7,6},{8,9},{9,8},{10,11... | collective-permute-start | bytes 1572872 | tf_op jit(solution)/shard_map/ppermute | solution.py:169
  26.5 2.4 %collective-permute-start.2 = (bf16[1024,256]{1,0:T(8,128)(2,1)S(1)}, bf16[1024,256]{1,0:T(8,128)(2,1)S(1)}, u32[]{:S(2)}, u32[]{:S(2)}) collective-permute-start(bf16[1024,256]{1,0:T(8,128)(2,1)S(1)} %collective-permute-done.refs_1_), channel_id=1, source_target_pairs={{0,1},{1,0},{2,3},{3,2},{4,5},{5,4},{6,7},{7,6},{8,9},{9,8},{10,11... | collective-permute-start | bytes 1572872 | tf_op jit(solution)/shard_map/ppermute | solution.py:169
  28.9 0.0 collective-permute-done.3.refs_3_
  28.9 1.9 %collective-permute-start.4 = (bf16[1024,256]{1,0:T(8,128)(2,1)S(1)}, bf16[1024,256]{1,0:T(8,128)(2,1)S(1)}, u32[]{:S(2)}, u32[]{:S(2)}) collective-permute-start(bf16[1024,256]{1,0:T(8,128)(2,1)S(1)} %collective-permute-done.3.refs_3_), channel_id=1, source_target_pairs={{0,1},{1,0},{2,3},{3,2},{4,5},{5,4},{6,7},{7,6},{8,9},{9,8},{10,11... | collective-permute-start | bytes 1572872 | tf_op jit(solution)/shard_map/ppermute | solution.py:169
  30.8 0.4 collective-permute-done.5.refs_5_
  31.2 2.0 %collective-permute-start.6 = (bf16[1024,256]{1,0:T(8,128)(2,1)S(1)}, bf16[1024,256]{1,0:T(8,128)(2,1)S(1)}, u32[]{:S(2)}, u32[]{:S(2)}) collective-permute-start(bf16[1024,256]{1,0:T(8,128)(2,1)S(1)} %collective-permute-done.5.refs_5_), channel_id=1, source_target_pairs={{0,1},{1,0},{2,3},{3,2},{4,5},{5,4},{6,7},{7,6},{8,9},{9,8},{10,11... | collective-permute-start | bytes 1572872 | tf_op jit(solution)/shard_map/ppermute | solution.py:169
  33.2 0.0 collective-permute-done.1.refs_0_
  33.2 0.0 collective-permute-done.2.refs_2_
  33.3 0.0 collective-permute-done.4.refs_4_
  33.3 1.8 %near_projection.1.acc_ref = f32[1024,512]{1,0:T(8,128)S(1)} custom-call(f32[1024,512]{1,0:T(8,128)S(1)} %get-tuple-element.9.acc_ref, bf16[1792,512]{1,0:T(8,128)(2,1)S(1)} %get-tuple-element.10.rest_ref.refs_1_, bf16[1024,256]{1,0:T(8,128)(2,1)S(1)} %collective-permute-done.1.refs_0_, bf16[1024,256]{1,0:T(8,128)(2,1)S(1)} %collective-permute-done.refs_1_, ...), custom_call_target="tpu_custom_call" | custom-call | tf_op jit(solution)/shard_map/near_projection/pallas_call | solution.py:217
  35.1 0.0 collective-permute-done.6.refs_0_
  35.1 0.0 copy-done.3
  35.1 0.0 copy-done.4
  35.1 0.0 copy-done.5
  35.1 5.5 %local_sums.1 = bf16[512,896]{1,0:T(8,128)(2,1)} custom-call(s32[32]{0:T(128)S(1)} %copy-done.5, f32[1024,512]{1,0:T(8,128)S(1)} %near_projection.1.acc_ref, bf16[1024,256]{1,0:T(8,128)(2,1)S(1)} %collective-permute-done.6.refs_0_, bf16[1792,512]{1,0:T(8,128)(2,1)S(1)} %get-tuple-element.10.rest_ref.refs_1_, bf16[512,256]{1,0:T(8,128)(2,1)S(1)} %copy-done.4, ...), custom_call_target="tpu_custom_call" | custom-call | tf_op jit(solution)/shard_map/local_sums/pallas_call | solution.py:225
  40.6 12.6 %all-to-all-start = ((bf16[64,8,896]{2,1,0:T(8,128)(2,1)}), bf16[64,8,896]{2,1,0:T(8,128)(2,1)S(1)}, u32[]{:S(2)}, u32[]{:S(2)}) async-start(bf16[64,8,896]{2,1,0:T(8,128)(2,1)} %bitcast.9), calls=%async_computation | async-start | bytes 1835008 | tf_op jit(solution)/shard_map/all_to_all | solution.py:246
  53.2 27.3 %all-to-all-done = bf16[64,8,896]{2,1,0:T(8,128)(2,1)S(1)} async-done(((bf16[64,8,896]{2,1,0:T(8,128)(2,1)}), bf16[64,8,896]{2,1,0:T(8,128)(2,1)S(1)}, u32[]{:S(2)}, u32[]{:S(2)}) %all-to-all-start) | async-done | bytes 917536 | tf_op jit(solution)/shard_map/all_to_all | solution.py:246
  80.5 0.7 final_sums.1
  81.2 25.8 %all_to_all.23 = bf16[64,8,512]{2,1,0:T(8,128)(2,1)S(1)} all-to-all(bf16[64,8,512]{2,1,0:T(8,128)(2,1)S(1)} %bitcast.14), channel_id=1, replica_groups=mesh['psg'=64,'pb'=4,'rep'=2] {'psg'}, dimensions={0} | all-to-all | bytes 1048576 | tf_op jit(solution)/shard_map/all_to_all | solution.py:256
  107.0 0.8 fusion
  (4 shorter events, 0.0 us)
Async XLA Ops:
  0.6 18.3 %collective-permute-start = (bf16[1024,256]{1,0:T(8,128)(2,1)}, bf16[1024,256]{1,0:T(8,128)(2,1)S(1)}, u32[]{:S(2)}, u32[]{:S(2)}) collective-permute-start(bf16[1024,256]{1,0:T(8,128)(2,1)} %bitcast.15), channel_id=1, source_target_pairs={{0,2},{1,7},{2,4},{3,1},{4,6},{5,3},{6,0},{7,5},{8,10},{9,15},{10,... | collective-permute-start | bytes 1572872 | tf_op jit(solution)/shard_map/ppermute | solution.py:188
  8.4 20.5 %collective-permute-start.3 = (bf16[1024,256]{1,0:T(8,128)(2,1)}, bf16[1024,256]{1,0:T(8,128)(2,1)S(1)}, u32[]{:S(2)}, u32[]{:S(2)}) collective-permute-start(bf16[1024,256]{1,0:T(8,128)(2,1)} %bitcast.16), channel_id=1, source_target_pairs={{0,6},{1,3},{2,0},{3,5},{4,2},{5,7},{6,4},{7,1},{8,14},{9,11},{10,... | collective-permute-start | bytes 1572872 | tf_op jit(solution)/shard_map/ppermute | solution.py:188
  10.5 1.2 %copy-start = (bf16[2048,256]{1,0:T(8,128)(2,1)S(1)}, bf16[2048,256]{1,0:T(8,128)(2,1)}, u32[]{:S(2)}) copy-start(bf16[2048,256]{1,0:T(8,128)(2,1)} %wk_ref.1) | copy-start | bytes 3145732
  11.7 1.2 %copy-start.1 = (bf16[2048,256]{1,0:T(8,128)(2,1)S(1)}, bf16[2048,256]{1,0:T(8,128)(2,1)}, u32[]{:S(2)}) copy-start(bf16[2048,256]{1,0:T(8,128)(2,1)} %wv_ref.1) | copy-start | bytes 3145732
  12.9 1.0 copy-start.2
  18.9 16.2 %copy-start.3 = (bf16[512,256]{1,0:T(8,128)(2,1)S(1)}, bf16[512,256]{1,0:T(8,128)(2,1)}, u32[]{:S(2)}) copy-start(bf16[512,256]{1,0:T(8,128)(2,1)} %refs_3_.1) | copy-start | bytes 786436
  18.9 16.2 %copy-start.4 = (bf16[512,256]{1,0:T(8,128)(2,1)S(1)}, bf16[512,256]{1,0:T(8,128)(2,1)}, u32[]{:S(2)}) copy-start(bf16[512,256]{1,0:T(8,128)(2,1)} %refs_2_.1) | copy-start | bytes 786436
  18.9 16.2 %copy-start.5 = (s32[32]{0:T(128)S(1)}, s32[32]{0:T(128)}, u32[]{:S(2)}) copy-start(s32[32]{0:T(128)} %owner_ref.1) | copy-start | bytes 388
  18.9 12.3 %collective-permute-start.5 = (bf16[1024,256]{1,0:T(8,128)(2,1)S(1)}, bf16[1024,256]{1,0:T(8,128)(2,1)S(1)}, u32[]{:S(2)}, u32[]{:S(2)}) collective-permute-start(bf16[1024,256]{1,0:T(8,128)(2,1)S(1)} %collective-permute-done.refs_1_), channel_id=1, source_target_pairs={{0,2},{1,7},{2,4},{3,1},{4,6},{5,3},{6,0},{7,5},{8,10},{9,15},{10,... | collective-permute-start | bytes 1572872 | tf_op jit(solution)/shard_map/ppermute | solution.py:188
  24.5 8.7 %collective-permute-start.1 = (bf16[1024,256]{1,0:T(8,128)(2,1)S(1)}, bf16[1024,256]{1,0:T(8,128)(2,1)S(1)}, u32[]{:S(2)}, u32[]{:S(2)}) collective-permute-start(bf16[1024,256]{1,0:T(8,128)(2,1)S(1)} %bitcast.18), channel_id=1, source_target_pairs={{0,1},{1,0},{2,3},{3,2},{4,5},{5,4},{6,7},{7,6},{8,9},{9,8},{10,11... | collective-permute-start | bytes 1572872 | tf_op jit(solution)/shard_map/ppermute | solution.py:169
  26.5 6.8 %collective-permute-start.2 = (bf16[1024,256]{1,0:T(8,128)(2,1)S(1)}, bf16[1024,256]{1,0:T(8,128)(2,1)S(1)}, u32[]{:S(2)}, u32[]{:S(2)}) collective-permute-start(bf16[1024,256]{1,0:T(8,128)(2,1)S(1)} %collective-permute-done.refs_1_), channel_id=1, source_target_pairs={{0,1},{1,0},{2,3},{3,2},{4,5},{5,4},{6,7},{7,6},{8,9},{9,8},{10,11... | collective-permute-start | bytes 1572872 | tf_op jit(solution)/shard_map/ppermute | solution.py:169
  28.9 4.4 %collective-permute-start.4 = (bf16[1024,256]{1,0:T(8,128)(2,1)S(1)}, bf16[1024,256]{1,0:T(8,128)(2,1)S(1)}, u32[]{:S(2)}, u32[]{:S(2)}) collective-permute-start(bf16[1024,256]{1,0:T(8,128)(2,1)S(1)} %collective-permute-done.3.refs_3_), channel_id=1, source_target_pairs={{0,1},{1,0},{2,3},{3,2},{4,5},{5,4},{6,7},{7,6},{8,9},{9,8},{10,11... | collective-permute-start | bytes 1572872 | tf_op jit(solution)/shard_map/ppermute | solution.py:169
  31.2 3.9 %collective-permute-start.6 = (bf16[1024,256]{1,0:T(8,128)(2,1)S(1)}, bf16[1024,256]{1,0:T(8,128)(2,1)S(1)}, u32[]{:S(2)}, u32[]{:S(2)}) collective-permute-start(bf16[1024,256]{1,0:T(8,128)(2,1)S(1)} %collective-permute-done.5.refs_5_), channel_id=1, source_target_pairs={{0,1},{1,0},{2,3},{3,2},{4,5},{5,4},{6,7},{7,6},{8,9},{9,8},{10,11... | collective-permute-start | bytes 1572872 | tf_op jit(solution)/shard_map/ppermute | solution.py:169
  40.6 40.0 %all-to-all-start = ((bf16[64,8,896]{2,1,0:T(8,128)(2,1)}), bf16[64,8,896]{2,1,0:T(8,128)(2,1)S(1)}, u32[]{:S(2)}, u32[]{:S(2)}) async-start(bf16[64,8,896]{2,1,0:T(8,128)(2,1)} %bitcast.9), calls=%async_computation | async-start | bytes 1835008 | tf_op jit(solution)/shard_map/all_to_all | solution.py:246

commit v6 on v5

--- a/solution.py
+++ b/solution.py
@@ -197,8 +197,7 @@
     own = rows // devices
 
     passages = prefixes.reshape(slots * vectors, features)
-    ahead, behind = along(passages, 1), along(passages, -1)
-    other = swap(passages)
+    ahead = along(passages, 1)
     smem = pl.BlockSpec(memory_space=pltpu.SMEM)
     vmem = pl.BlockSpec(memory_space=pltpu.VMEM)
     sums = jax.ShapeDtypeStruct((slots * vectors, 2 * cols), f32)
@@ -210,7 +209,8 @@
         compiler_params=pltpu.CompilerParams(vmem_limit_bytes=16 * 1024 * 1024),
         name="own_projection",
     )(block_numbers(), passages, key_weight, value_weight)
-    ahead, projected, rest = lax.optimization_barrier((ahead, projected, rest))
+    held, projected, rest = lax.optimization_barrier((passages, projected, rest))
+    behind, other = along(held, -1), swap(held)
     far = along(ahead, 1)
     near = [other, ahead, swap(ahead), behind, swap(behind), far]
     far = swap(far)

time: 109 us -> 110 us (level)
  the two profiles are of different devices: /device:TPU:6 before, /device:TPU:2 now
where the time goes in v6:
time: 110 us; the launch traced here: 109 us
  waiting for transfers between devices  35.1 us (32%)
  starting transfers between devices  34.3 us (31%)
  blocking collectives  25.8 us (23%)
  Pallas kernels  8.97 us (8%)
  local copies, waits for them, and re-layouts  4.42 us (4%)
    all_to_all x1, waiting for transfers between devices, body(): received = lax.all_to_all(payload, 'psg', 0, 0, tiled=True)  27.3 us
    all_to_all x1, blocking collectives, body(): outputs = lax.all_to_all(finished, 'psg', 0, 0, tiled=True)  25.8 us
    all_to_all x1, starting transfers between devices, body(): received = lax.all_to_all(payload, 'psg', 0, 0, tiled=True)  14.4 us
    ppermute x3, starting transfers between devices, along(): return lax.ppermute(block, ('pb', 'rep'), pairs)  11.8 us
    ppermute x4, starting transfers between devices, swap(): return lax.ppermute(block, 'rep', [(0, 1), (1, 0)])  8.14 us
    ppermute x3, waiting for transfers between devices, along(): return lax.ppermute(block, ('pb', 'rep'), pairs)  7.69 us
    pallas_call x1, Pallas kernels, body(): pl.pallas_call(local_kernel, out_shape=jax.ShapeDtypeStruct((rows, 3 * co...  5.45 us
    unnamed x12, local copies, waits for them, and re-layouts  3.51 us
  transfers between devices with their start and end apart: 8, of which 4 were waited for; matrix products, arithmetic and copies ran while one was open for 0% of the time, Pallas kernels for 3%

profile of v6, /device:TPU:2, one launch (start us, length us, event | category | flops | bytes accessed | tf_op | source)
XLA Modules:
  0.0 109.3 jit_solution(9456671684007215050)
XLA Ops:
  0.6 3.4 %collective-permute-start.1 = (bf16[1024,256]{1,0:T(8,128)(2,1)}, bf16[1024,256]{1,0:T(8,128)(2,1)S(1)}, u32[]{:S(2)}, u32[]{:S(2)}) collective-permute-start(bf16[1024,256]{1,0:T(8,128)(2,1)} %bitcast.15), channel_id=1, source_target_pairs={{0,2},{1,7},{2,4},{3,1},{4,6},{5,3},{6,0},{7,5},{8,10},{9,15},{10,... | collective-permute-start | bytes 1572872 | tf_op jit(solution)/shard_map/ppermute | solution.py:188
  4.1 0.1 stack.35.block_ref
  4.2 1.2 %copy-done = bf16[2048,256]{1,0:T(8,128)(2,1)S(1)} copy-done((bf16[2048,256]{1,0:T(8,128)(2,1)S(1)}, bf16[2048,256]{1,0:T(8,128)(2,1)}, u32[]{:S(2)}) %copy-start) | copy-done | bytes 1048600
  5.4 1.2 %copy-done.1 = bf16[2048,256]{1,0:T(8,128)(2,1)S(1)} copy-done((bf16[2048,256]{1,0:T(8,128)(2,1)S(1)}, bf16[2048,256]{1,0:T(8,128)(2,1)}, u32[]{:S(2)}) %copy-start.1) | copy-done | bytes 1048600
  6.6 1.0 copy-done.2
  7.7 1.0 own_projection.1
  8.7 0.0 copy-start.3
  8.7 0.0 copy-start.4
  8.8 0.0 copy-start.5
  8.8 6.5 %collective-permute-start.3 = (bf16[1024,256]{1,0:T(8,128)(2,1)S(1)}, bf16[1024,256]{1,0:T(8,128)(2,1)S(1)}, u32[]{:S(2)}, u32[]{:S(2)}) collective-permute-start(bf16[1024,256]{1,0:T(8,128)(2,1)S(1)} %bitcast.17), channel_id=1, source_target_pairs={{0,6},{1,3},{2,0},{3,5},{4,2},{5,7},{6,4},{7,1},{8,14},{9,11},{10,... | collective-permute-start | bytes 1572872 | tf_op jit(solution)/shard_map/ppermute | solution.py:188
  15.2 3.3 %collective-permute-done.1.refs_1_ = bf16[1024,256]{1,0:T(8,128)(2,1)S(1)} collective-permute-done((bf16[1024,256]{1,0:T(8,128)(2,1)}, bf16[1024,256]{1,0:T(8,128)(2,1)S(1)}, u32[]{:S(2)}, u32[]{:S(2)}) %collective-permute-start.1) | collective-permute-done | bytes 524320 | tf_op jit(solution)/shard_map/ppermute | solution.py:188
  18.6 1.9 %collective-permute-start.5 = (bf16[1024,256]{1,0:T(8,128)(2,1)S(1)}, bf16[1024,256]{1,0:T(8,128)(2,1)S(1)}, u32[]{:S(2)}, u32[]{:S(2)}) collective-permute-start(bf16[1024,256]{1,0:T(8,128)(2,1)S(1)} %collective-permute-done.1.refs_1_), channel_id=1, source_target_pairs={{0,2},{1,7},{2,4},{3,1},{4,6},{5,3},{6,0},{7,5},{8,10},{9,15},{10,... | collective-permute-start | bytes 1572872 | tf_op jit(solution)/shard_map/ppermute | solution.py:188
  20.5 1.9 %collective-permute-start = (bf16[1024,256]{1,0:T(8,128)(2,1)S(1)}, bf16[1024,256]{1,0:T(8,128)(2,1)S(1)}, u32[]{:S(2)}, u32[]{:S(2)}) collective-permute-start(bf16[1024,256]{1,0:T(8,128)(2,1)S(1)} %bitcast.18), channel_id=1, source_target_pairs={{0,1},{1,0},{2,3},{3,2},{4,5},{5,4},{6,7},{7,6},{8,9},{9,8},{10,11... | collective-permute-start | bytes 1572872 | tf_op jit(solution)/shard_map/ppermute | solution.py:169
  22.4 3.0 %collective-permute-done.3.refs_3_ = bf16[1024,256]{1,0:T(8,128)(2,1)S(1)} collective-permute-done((bf16[1024,256]{1,0:T(8,128)(2,1)S(1)}, bf16[1024,256]{1,0:T(8,128)(2,1)S(1)}, u32[]{:S(2)}, u32[]{:S(2)}) %collective-permute-start.3) | collective-permute-done | bytes 524320 | tf_op jit(solution)/shard_map/ppermute | solution.py:188
  25.4 1.9 %collective-permute-start.4 = (bf16[1024,256]{1,0:T(8,128)(2,1)S(1)}, bf16[1024,256]{1,0:T(8,128)(2,1)S(1)}, u32[]{:S(2)}, u32[]{:S(2)}) collective-permute-start(bf16[1024,256]{1,0:T(8,128)(2,1)S(1)} %collective-permute-done.3.refs_3_), channel_id=1, source_target_pairs={{0,1},{1,0},{2,3},{3,2},{4,5},{5,4},{6,7},{7,6},{8,9},{9,8},{10,11... | collective-permute-start | bytes 1572872 | tf_op jit(solution)/shard_map/ppermute | solution.py:169
  27.3 2.4 %collective-permute-start.2 = (bf16[1024,256]{1,0:T(8,128)(2,1)S(1)}, bf16[1024,256]{1,0:T(8,128)(2,1)S(1)}, u32[]{:S(2)}, u32[]{:S(2)}) collective-permute-start(bf16[1024,256]{1,0:T(8,128)(2,1)S(1)} %collective-permute-done.1.refs_1_), channel_id=1, source_target_pairs={{0,1},{1,0},{2,3},{3,2},{4,5},{5,4},{6,7},{7,6},{8,9},{9,8},{10,11... | collective-permute-start | bytes 1572872 | tf_op jit(solution)/shard_map/ppermute | solution.py:169
  29.8 1.4 %collective-permute-done.5.refs_5_ = bf16[1024,256]{1,0:T(8,128)(2,1)S(1)} collective-permute-done((bf16[1024,256]{1,0:T(8,128)(2,1)S(1)}, bf16[1024,256]{1,0:T(8,128)(2,1)S(1)}, u32[]{:S(2)}, u32[]{:S(2)}) %collective-permute-start.5) | collective-permute-done | bytes 524320 | tf_op jit(solution)/shard_map/ppermute | solution.py:188
  31.1 1.9 %collective-permute-start.6 = (bf16[1024,256]{1,0:T(8,128)(2,1)S(1)}, bf16[1024,256]{1,0:T(8,128)(2,1)S(1)}, u32[]{:S(2)}, u32[]{:S(2)}) collective-permute-start(bf16[1024,256]{1,0:T(8,128)(2,1)S(1)} %collective-permute-done.5.refs_5_), channel_id=1, source_target_pairs={{0,1},{1,0},{2,3},{3,2},{4,5},{5,4},{6,7},{7,6},{8,9},{9,8},{10,11... | collective-permute-start | bytes 1572872 | tf_op jit(solution)/shard_map/ppermute | solution.py:169
  33.0 0.0 collective-permute-done.refs_0_
  33.0 0.0 collective-permute-done.4.refs_4_
  33.0 0.0 collective-permute-done.2.refs_2_
  33.1 1.8 %near_projection.1.acc_ref = f32[1024,512]{1,0:T(8,128)S(1)} custom-call(f32[1024,512]{1,0:T(8,128)S(1)} %get-tuple-element.9.acc_ref, bf16[1792,512]{1,0:T(8,128)(2,1)S(1)} %get-tuple-element.10.rest_ref.refs_1_, bf16[1024,256]{1,0:T(8,128)(2,1)S(1)} %collective-permute-done.refs_0_, bf16[1024,256]{1,0:T(8,128)(2,1)S(1)} %collective-permute-done.1.refs_1_, ...), custom_call_target="tpu_custom_call" | custom-call | tf_op jit(solution)/shard_map/near_projection/pallas_call | solution.py:217
  34.9 0.0 collective-permute-done.6.refs_0_
  34.9 0.0 copy-done.3
  34.9 0.0 copy-done.4
  34.9 0.0 copy-done.5
  34.9 5.5 %local_sums.1 = bf16[512,896]{1,0:T(8,128)(2,1)} custom-call(s32[32]{0:T(128)S(1)} %copy-done.5, f32[1024,512]{1,0:T(8,128)S(1)} %near_projection.1.acc_ref, bf16[1024,256]{1,0:T(8,128)(2,1)S(1)} %collective-permute-done.6.refs_0_, bf16[1792,512]{1,0:T(8,128)(2,1)S(1)} %get-tuple-element.10.rest_ref.refs_1_, bf16[512,256]{1,0:T(8,128)(2,1)S(1)} %copy-done.4, ...), custom_call_target="tpu_custom_call" | custom-call | tf_op jit(solution)/shard_map/local_sums/pallas_call | solution.py:225
  40.4 14.4 %all-to-all-start = ((bf16[64,8,896]{2,1,0:T(8,128)(2,1)}), bf16[64,8,896]{2,1,0:T(8,128)(2,1)S(1)}, u32[]{:S(2)}, u32[]{:S(2)}) async-start(bf16[64,8,896]{2,1,0:T(8,128)(2,1)} %bitcast.9), calls=%async_computation | async-start | bytes 1835008 | tf_op jit(solution)/shard_map/all_to_all | solution.py:246
  54.8 27.3 %all-to-all-done = bf16[64,8,896]{2,1,0:T(8,128)(2,1)S(1)} async-done(((bf16[64,8,896]{2,1,0:T(8,128)(2,1)}), bf16[64,8,896]{2,1,0:T(8,128)(2,1)S(1)}, u32[]{:S(2)}, u32[]{:S(2)}) %all-to-all-start) | async-done | bytes 917536 | tf_op jit(solution)/shard_map/all_to_all | solution.py:246
  82.1 0.7 final_sums.1
  82.8 25.8 %all_to_all.23 = bf16[64,8,512]{2,1,0:T(8,128)(2,1)S(1)} all-to-all(bf16[64,8,512]{2,1,0:T(8,128)(2,1)S(1)} %bitcast.14), channel_id=1, replica_groups=mesh['psg'=64,'pb'=4,'rep'=2] {'psg'}, dimensions={0} | all-to-all | bytes 1048576 | tf_op jit(solution)/shard_map/all_to_all | solution.py:256
  108.5 0.8 fusion
  (4 shorter events, 0.0 us)
Async XLA Ops:
  0.6 17.9 %collective-permute-start.1 = (bf16[1024,256]{1,0:T(8,128)(2,1)}, bf16[1024,256]{1,0:T(8,128)(2,1)S(1)}, u32[]{:S(2)}, u32[]{:S(2)}) collective-permute-start(bf16[1024,256]{1,0:T(8,128)(2,1)} %bitcast.15), channel_id=1, source_target_pairs={{0,2},{1,7},{2,4},{3,1},{4,6},{5,3},{6,0},{7,5},{8,10},{9,15},{10,... | collective-permute-start | bytes 1572872 | tf_op jit(solution)/shard_map/ppermute | solution.py:188
  4.2 1.2 %copy-start = (bf16[2048,256]{1,0:T(8,128)(2,1)S(1)}, bf16[2048,256]{1,0:T(8,128)(2,1)}, u32[]{:S(2)}) copy-start(bf16[2048,256]{1,0:T(8,128)(2,1)} %wk_ref.1) | copy-start | bytes 3145732
  5.4 1.2 %copy-start.1 = (bf16[2048,256]{1,0:T(8,128)(2,1)S(1)}, bf16[2048,256]{1,0:T(8,128)(2,1)}, u32[]{:S(2)}) copy-start(bf16[2048,256]{1,0:T(8,128)(2,1)} %wv_ref.1) | copy-start | bytes 3145732
  6.6 1.0 copy-start.2
  8.7 26.2 %copy-start.3 = (bf16[512,256]{1,0:T(8,128)(2,1)S(1)}, bf16[512,256]{1,0:T(8,128)(2,1)}, u32[]{:S(2)}) copy-start(bf16[512,256]{1,0:T(8,128)(2,1)} %refs_3_.1) | copy-start | bytes 786436
  8.7 26.2 %copy-start.4 = (bf16[512,256]{1,0:T(8,128)(2,1)S(1)}, bf16[512,256]{1,0:T(8,128)(2,1)}, u32[]{:S(2)}) copy-start(bf16[512,256]{1,0:T(8,128)(2,1)} %refs_2_.1) | copy-start | bytes 786436
  8.8 26.2 %copy-start.5 = (s32[32]{0:T(128)S(1)}, s32[32]{0:T(128)}, u32[]{:S(2)}) copy-start(s32[32]{0:T(128)} %owner_ref.1) | copy-start | bytes 388
  8.8 16.7 %collective-permute-start.3 = (bf16[1024,256]{1,0:T(8,128)(2,1)S(1)}, bf16[1024,256]{1,0:T(8,128)(2,1)S(1)}, u32[]{:S(2)}, u32[]{:S(2)}) collective-permute-start(bf16[1024,256]{1,0:T(8,128)(2,1)S(1)} %bitcast.17), channel_id=1, source_target_pairs={{0,6},{1,3},{2,0},{3,5},{4,2},{5,7},{6,4},{7,1},{8,14},{9,11},{10,... | collective-permute-start | bytes 1572872 | tf_op jit(solution)/shard_map/ppermute | solution.py:188
  18.6 12.6 %collective-permute-start.5 = (bf16[1024,256]{1,0:T(8,128)(2,1)S(1)}, bf16[1024,256]{1,0:T(8,128)(2,1)S(1)}, u32[]{:S(2)}, u32[]{:S(2)}) collective-permute-start(bf16[1024,256]{1,0:T(8,128)(2,1)S(1)} %collective-permute-done.1.refs_1_), channel_id=1, source_target_pairs={{0,2},{1,7},{2,4},{3,1},{4,6},{5,3},{6,0},{7,5},{8,10},{9,15},{10,... | collective-permute-start | bytes 1572872 | tf_op jit(solution)/shard_map/ppermute | solution.py:188
  20.5 12.6 %collective-permute-start = (bf16[1024,256]{1,0:T(8,128)(2,1)S(1)}, bf16[1024,256]{1,0:T(8,128)(2,1)S(1)}, u32[]{:S(2)}, u32[]{:S(2)}) collective-permute-start(bf16[1024,256]{1,0:T(8,128)(2,1)S(1)} %bitcast.18), channel_id=1, source_target_pairs={{0,1},{1,0},{2,3},{3,2},{4,5},{5,4},{6,7},{7,6},{8,9},{9,8},{10,11... | collective-permute-start | bytes 1572872 | tf_op jit(solution)/shard_map/ppermute | solution.py:169
  25.4 7.6 %collective-permute-start.4 = (bf16[1024,256]{1,0:T(8,128)(2,1)S(1)}, bf16[1024,256]{1,0:T(8,128)(2,1)S(1)}, u32[]{:S(2)}, u32[]{:S(2)}) collective-permute-start(bf16[1024,256]{1,0:T(8,128)(2,1)S(1)} %collective-permute-done.3.refs_3_), channel_id=1, source_target_pairs={{0,1},{1,0},{2,3},{3,2},{4,5},{5,4},{6,7},{7,6},{8,9},{9,8},{10,11... | collective-permute-start | bytes 1572872 | tf_op jit(solution)/shard_map/ppermute | solution.py:169
  27.3 5.7 %collective-permute-start.2 = (bf16[1024,256]{1,0:T(8,128)(2,1)S(1)}, bf16[1024,256]{1,0:T(8,128)(2,1)S(1)}, u32[]{:S(2)}, u32[]{:S(2)}) collective-permute-start(bf16[1024,256]{1,0:T(8,128)(2,1)S(1)} %collective-permute-done.1.refs_1_), channel_id=1, source_target_pairs={{0,1},{1,0},{2,3},{3,2},{4,5},{5,4},{6,7},{7,6},{8,9},{9,8},{10,11... | collective-permute-start | bytes 1572872 | tf_op jit(solution)/shard_map/ppermute | solution.py:169
  31.1 3.8 %collective-permute-start.6 = (bf16[1024,256]{1,0:T(8,128)(2,1)S(1)}, bf16[1024,256]{1,0:T(8,128)(2,1)S(1)}, u32[]{:S(2)}, u32[]{:S(2)}) collective-permute-start(bf16[1024,256]{1,0:T(8,128)(2,1)S(1)} %collective-permute-done.5.refs_5_), channel_id=1, source_target_pairs={{0,1},{1,0},{2,3},{3,2},{4,5},{5,4},{6,7},{7,6},{8,9},{9,8},{10,11... | collective-permute-start | bytes 1572872 | tf_op jit(solution)/shard_map/ppermute | solution.py:169
  40.4 41.7 %all-to-all-start = ((bf16[64,8,896]{2,1,0:T(8,128)(2,1)}), bf16[64,8,896]{2,1,0:T(8,128)(2,1)S(1)}, u32[]{:S(2)}, u32[]{:S(2)}) async-start(bf16[64,8,896]{2,1,0:T(8,128)(2,1)} %bitcast.9), calls=%async_computation | async-start | bytes 1835008 | tf_op jit(solution)/shard_map/all_to_all | solution.py:246

commit v7 on v6

--- a/solution.py
+++ b/solution.py
@@ -212,7 +212,9 @@
     held, projected, rest = lax.optimization_barrier((passages, projected, rest))
     behind, other = along(held, -1), swap(held)
     far = along(ahead, 1)
-    near = [other, ahead, swap(ahead), behind, swap(behind), far]
+    ahead_other = swap(ahead)
+    far, ahead_other = lax.optimization_barrier((far, ahead_other))
+    near = [other, ahead, ahead_other, behind, swap(behind), far]
     far = swap(far)
     projected = pl.pallas_call(
         near_kernel,

time: 110 us -> 107 us (0.973)
  the two profiles are of different devices: /device:TPU:2 before, /device:TPU:8 now
where the time goes in v7:
time: 107 us
  starting transfers between devices  34.5 us (32%)
  waiting for transfers between devices  32.3 us (30%)
  blocking collectives  25.8 us (24%)
  Pallas kernels  8.96 us (8%)
  local copies, waits for them, and re-layouts  4.42 us (4%)
    all_to_all x1, waiting for transfers between devices, body(): received = lax.all_to_all(payload, 'psg', 0, 0, tiled=True)  27.1 us
    all_to_all x1, blocking collectives, body(): outputs = lax.all_to_all(finished, 'psg', 0, 0, tiled=True)  25.8 us
    all_to_all x1, starting transfers between devices, body(): received = lax.all_to_all(payload, 'psg', 0, 0, tiled=True)  16.6 us
    ppermute x3, starting transfers between devices, along(): return lax.ppermute(block, ('pb', 'rep'), pairs)  9.37 us
    ppermute x4, starting transfers between devices, swap(): return lax.ppermute(block, 'rep', [(0, 1), (1, 0)])  8.57 us
    pallas_call x1, Pallas kernels, body(): pl.pallas_call(local_kernel, out_shape=jax.ShapeDtypeStruct((rows, 3 * co...  5.45 us
    ppermute x3, waiting for transfers between devices, along(): return lax.ppermute(block, ('pb', 'rep'), pairs)  5.22 us
    unnamed x12, local copies, waits for them, and re-layouts  3.51 us
  transfers between devices with their start and end apart: 8, of which 5 were waited for; matrix products, arithmetic and copies ran while one was open for 0% of the time, Pallas kernels for 3%

profile of v7, /device:TPU:8, one launch (start us, length us, event | category | flops | bytes accessed | tf_op | source)
XLA Modules:
  0.0 106.9 jit_solution(1212387185897234466)
XLA Ops:
  0.6 3.4 %collective-permute-start.1 = (bf16[1024,256]{1,0:T(8,128)(2,1)}, bf16[1024,256]{1,0:T(8,128)(2,1)S(1)}, u32[]{:S(2)}, u32[]{:S(2)}) collective-permute-start(bf16[1024,256]{1,0:T(8,128)(2,1)} %bitcast.15), channel_id=1, source_target_pairs={{0,2},{1,7},{2,4},{3,1},{4,6},{5,3},{6,0},{7,5},{8,10},{9,15},{10,... | collective-permute-start | bytes 1572872 | tf_op jit(solution)/shard_map/ppermute | solution.py:188
  4.1 0.1 stack.35.block_ref
  4.2 1.2 %copy-done = bf16[2048,256]{1,0:T(8,128)(2,1)S(1)} copy-done((bf16[2048,256]{1,0:T(8,128)(2,1)S(1)}, bf16[2048,256]{1,0:T(8,128)(2,1)}, u32[]{:S(2)}) %copy-start) | copy-done | bytes 1048600
  5.4 1.2 %copy-done.1 = bf16[2048,256]{1,0:T(8,128)(2,1)S(1)} copy-done((bf16[2048,256]{1,0:T(8,128)(2,1)S(1)}, bf16[2048,256]{1,0:T(8,128)(2,1)}, u32[]{:S(2)}) %copy-start.1) | copy-done | bytes 1048600
  6.6 1.0 copy-done.2
  7.7 1.0 own_projection.1
  8.7 0.0 copy-start.3
  8.7 0.0 copy-start.4
  8.7 0.0 copy-start.5
  8.8 3.8 %collective-permute-start.4 = (bf16[1024,256]{1,0:T(8,128)(2,1)S(1)}, bf16[1024,256]{1,0:T(8,128)(2,1)S(1)}, u32[]{:S(2)}, u32[]{:S(2)}) collective-permute-start(bf16[1024,256]{1,0:T(8,128)(2,1)S(1)} %bitcast.17), channel_id=1, source_target_pairs={{0,6},{1,3},{2,0},{3,5},{4,2},{5,7},{6,4},{7,1},{8,14},{9,11},{10,... | collective-permute-start | bytes 1572872 | tf_op jit(solution)/shard_map/ppermute | solution.py:188
  12.6 0.6 collective-permute-done.1.refs_1_
  13.1 2.2 %collective-permute-start.2 = (bf16[1024,256]{1,0:T(8,128)(2,1)S(1)}, bf16[1024,256]{1,0:T(8,128)(2,1)S(1)}, u32[]{:S(2)}, u32[]{:S(2)}) collective-permute-start(bf16[1024,256]{1,0:T(8,128)(2,1)S(1)} %collective-permute-done.1.refs_1_), channel_id=1, source_target_pairs={{0,2},{1,7},{2,4},{3,1},{4,6},{5,3},{6,0},{7,5},{8,10},{9,15},{10,... | collective-permute-start | bytes 1572872 | tf_op jit(solution)/shard_map/ppermute | solution.py:188
  15.3 2.8 %collective-permute-start.3 = (bf16[1024,256]{1,0:T(8,128)(2,1)S(1)}, bf16[1024,256]{1,0:T(8,128)(2,1)S(1)}, u32[]{:S(2)}, u32[]{:S(2)}) collective-permute-start(bf16[1024,256]{1,0:T(8,128)(2,1)S(1)} %collective-permute-done.1.refs_1_), channel_id=1, source_target_pairs={{0,1},{1,0},{2,3},{3,2},{4,5},{5,4},{6,7},{7,6},{8,9},{9,8},{10,11... | collective-permute-start | bytes 1572872 | tf_op jit(solution)/shard_map/ppermute | solution.py:169
  18.1 1.9 %collective-permute-start = (bf16[1024,256]{1,0:T(8,128)(2,1)S(1)}, bf16[1024,256]{1,0:T(8,128)(2,1)S(1)}, u32[]{:S(2)}, u32[]{:S(2)}) collective-permute-start(bf16[1024,256]{1,0:T(8,128)(2,1)S(1)} %bitcast.18), channel_id=1, source_target_pairs={{0,1},{1,0},{2,3},{3,2},{4,5},{5,4},{6,7},{7,6},{8,9},{9,8},{10,11... | collective-permute-start | bytes 1572872 | tf_op jit(solution)/shard_map/ppermute | solution.py:169
  20.1 3.6 %collective-permute-done.4.refs_3_ = bf16[1024,256]{1,0:T(8,128)(2,1)S(1)} collective-permute-done((bf16[1024,256]{1,0:T(8,128)(2,1)S(1)}, bf16[1024,256]{1,0:T(8,128)(2,1)S(1)}, u32[]{:S(2)}, u32[]{:S(2)}) %collective-permute-start.4) | collective-permute-done | bytes 524320 | tf_op jit(solution)/shard_map/ppermute | solution.py:188
  23.7 1.9 %collective-permute-start.5 = (bf16[1024,256]{1,0:T(8,128)(2,1)S(1)}, bf16[1024,256]{1,0:T(8,128)(2,1)S(1)}, u32[]{:S(2)}, u32[]{:S(2)}) collective-permute-start(bf16[1024,256]{1,0:T(8,128)(2,1)S(1)} %collective-permute-done.4.refs_3_), channel_id=1, source_target_pairs={{0,1},{1,0},{2,3},{3,2},{4,5},{5,4},{6,7},{7,6},{8,9},{9,8},{10,11... | collective-permute-start | bytes 1572872 | tf_op jit(solution)/shard_map/ppermute | solution.py:169
  25.6 1.0 collective-permute-done.2.refs_5_
  26.6 0.0 collective-permute-done.3.refs_2_
  26.6 1.9 %collective-permute-start.6 = (bf16[1024,256]{1,0:T(8,128)(2,1)S(1)}, bf16[1024,256]{1,0:T(8,128)(2,1)S(1)}, u32[]{:S(2)}, u32[]{:S(2)}) collective-permute-start(bf16[1024,256]{1,0:T(8,128)(2,1)S(1)} %collective-permute-done.2.refs_5_), channel_id=1, source_target_pairs={{0,1},{1,0},{2,3},{3,2},{4,5},{5,4},{6,7},{7,6},{8,9},{9,8},{10,11... | collective-permute-start | bytes 1572872 | tf_op jit(solution)/shard_map/ppermute | solution.py:169
  28.6 0.0 collective-permute-done.refs_0_
  28.6 0.0 collective-permute-done.5.refs_4_
  28.6 1.8 %near_projection.1.acc_ref = f32[1024,512]{1,0:T(8,128)S(1)} custom-call(f32[1024,512]{1,0:T(8,128)S(1)} %get-tuple-element.11.acc_ref, bf16[1792,512]{1,0:T(8,128)(2,1)S(1)} %get-tuple-element.12.rest_ref.refs_1_, bf16[1024,256]{1,0:T(8,128)(2,1)S(1)} %collective-permute-done.refs_0_, bf16[1024,256]{1,0:T(8,128)(2,1)S(1)} %collective-permute-done.1.refs_1_, ...), custom_call_target="tpu_custom_call" | custom-call | tf_op jit(solution)/shard_map/near_projection/pallas_call | solution.py:219
  30.4 0.1 collective-permute-done.6.refs_0_
  30.4 0.0 copy-done.3
  30.4 0.0 copy-done.4
  30.4 0.0 copy-done.5
  30.5 5.5 %local_sums.1 = bf16[512,896]{1,0:T(8,128)(2,1)} custom-call(s32[32]{0:T(128)S(1)} %copy-done.5, f32[1024,512]{1,0:T(8,128)S(1)} %near_projection.1.acc_ref, bf16[1024,256]{1,0:T(8,128)(2,1)S(1)} %collective-permute-done.6.refs_0_, bf16[1792,512]{1,0:T(8,128)(2,1)S(1)} %get-tuple-element.12.rest_ref.refs_1_, bf16[512,256]{1,0:T(8,128)(2,1)S(1)} %copy-done.4, ...), custom_call_target="tpu_custom_call" | custom-call | tf_op jit(solution)/shard_map/local_sums/pallas_call | solution.py:227
  35.9 16.6 %all-to-all-start = ((bf16[64,8,896]{2,1,0:T(8,128)(2,1)}), bf16[64,8,896]{2,1,0:T(8,128)(2,1)S(1)}, u32[]{:S(2)}, u32[]{:S(2)}) async-start(bf16[64,8,896]{2,1,0:T(8,128)(2,1)} %bitcast.9), calls=%async_computation | async-start | bytes 1835008 | tf_op jit(solution)/shard_map/all_to_all | solution.py:248
  52.5 27.1 %all-to-all-done = bf16[64,8,896]{2,1,0:T(8,128)(2,1)S(1)} async-done(((bf16[64,8,896]{2,1,0:T(8,128)(2,1)}), bf16[64,8,896]{2,1,0:T(8,128)(2,1)S(1)}, u32[]{:S(2)}, u32[]{:S(2)}) %all-to-all-start) | async-done | bytes 917536 | tf_op jit(solution)/shard_map/all_to_all | solution.py:248
  79.6 0.7 final_sums.1
  80.3 25.8 %all_to_all.23 = bf16[64,8,512]{2,1,0:T(8,128)(2,1)S(1)} all-to-all(bf16[64,8,512]{2,1,0:T(8,128)(2,1)S(1)} %bitcast.14), channel_id=1, replica_groups=mesh['psg'=64,'pb'=4,'rep'=2] {'psg'}, dimensions={0} | all-to-all | bytes 1048576 | tf_op jit(solution)/shard_map/all_to_all | solution.py:258
  106.1 0.8 fusion
  (4 shorter events, 0.0 us)
Async XLA Ops:
  0.6 12.5 %collective-permute-start.1 = (bf16[1024,256]{1,0:T(8,128)(2,1)}, bf16[1024,256]{1,0:T(8,128)(2,1)S(1)}, u32[]{:S(2)}, u32[]{:S(2)}) collective-permute-start(bf16[1024,256]{1,0:T(8,128)(2,1)} %bitcast.15), channel_id=1, source_target_pairs={{0,2},{1,7},{2,4},{3,1},{4,6},{5,3},{6,0},{7,5},{8,10},{9,15},{10,... | collective-permute-start | bytes 1572872 | tf_op jit(solution)/shard_map/ppermute | solution.py:188
  4.2 1.2 %copy-start = (bf16[2048,256]{1,0:T(8,128)(2,1)S(1)}, bf16[2048,256]{1,0:T(8,128)(2,1)}, u32[]{:S(2)}) copy-start(bf16[2048,256]{1,0:T(8,128)(2,1)} %wk_ref.1) | copy-start | bytes 3145732
  5.4 1.2 %copy-start.1 = (bf16[2048,256]{1,0:T(8,128)(2,1)S(1)}, bf16[2048,256]{1,0:T(8,128)(2,1)}, u32[]{:S(2)}) copy-start(bf16[2048,256]{1,0:T(8,128)(2,1)} %wv_ref.1) | copy-start | bytes 3145732
  6.6 1.0 copy-start.2
  8.7 21.7 %copy-start.3 = (bf16[512,256]{1,0:T(8,128)(2,1)S(1)}, bf16[512,256]{1,0:T(8,128)(2,1)}, u32[]{:S(2)}) copy-start(bf16[512,256]{1,0:T(8,128)(2,1)} %refs_3_.1) | copy-start | bytes 786436
  8.7 21.7 %copy-start.4 = (bf16[512,256]{1,0:T(8,128)(2,1)S(1)}, bf16[512,256]{1,0:T(8,128)(2,1)}, u32[]{:S(2)}) copy-start(bf16[512,256]{1,0:T(8,128)(2,1)} %refs_2_.1) | copy-start | bytes 786436
  8.7 21.7 %copy-start.5 = (s32[32]{0:T(128)S(1)}, s32[32]{0:T(128)}, u32[]{:S(2)}) copy-start(s32[32]{0:T(128)} %owner_ref.1) | copy-start | bytes 388
  8.8 15.0 %collective-permute-start.4 = (bf16[1024,256]{1,0:T(8,128)(2,1)S(1)}, bf16[1024,256]{1,0:T(8,128)(2,1)S(1)}, u32[]{:S(2)}, u32[]{:S(2)}) collective-permute-start(bf16[1024,256]{1,0:T(8,128)(2,1)S(1)} %bitcast.17), channel_id=1, source_target_pairs={{0,6},{1,3},{2,0},{3,5},{4,2},{5,7},{6,4},{7,1},{8,14},{9,11},{10,... | collective-permute-start | bytes 1572872 | tf_op jit(solution)/shard_map/ppermute | solution.py:188
  13.1 13.5 %collective-permute-start.2 = (bf16[1024,256]{1,0:T(8,128)(2,1)S(1)}, bf16[1024,256]{1,0:T(8,128)(2,1)S(1)}, u32[]{:S(2)}, u32[]{:S(2)}) collective-permute-start(bf16[1024,256]{1,0:T(8,128)(2,1)S(1)} %collective-permute-done.1.refs_1_), channel_id=1, source_target_pairs={{0,2},{1,7},{2,4},{3,1},{4,6},{5,3},{6,0},{7,5},{8,10},{9,15},{10,... | collective-permute-start | bytes 1572872 | tf_op jit(solution)/shard_map/ppermute | solution.py:188
  15.3 11.3 %collective-permute-start.3 = (bf16[1024,256]{1,0:T(8,128)(2,1)S(1)}, bf16[1024,256]{1,0:T(8,128)(2,1)S(1)}, u32[]{:S(2)}, u32[]{:S(2)}) collective-permute-start(bf16[1024,256]{1,0:T(8,128)(2,1)S(1)} %collective-permute-done.1.refs_1_), channel_id=1, source_target_pairs={{0,1},{1,0},{2,3},{3,2},{4,5},{5,4},{6,7},{7,6},{8,9},{9,8},{10,11... | collective-permute-start | bytes 1572872 | tf_op jit(solution)/shard_map/ppermute | solution.py:169
  18.1 10.4 %collective-permute-start = (bf16[1024,256]{1,0:T(8,128)(2,1)S(1)}, bf16[1024,256]{1,0:T(8,128)(2,1)S(1)}, u32[]{:S(2)}, u32[]{:S(2)}) collective-permute-start(bf16[1024,256]{1,0:T(8,128)(2,1)S(1)} %bitcast.18), channel_id=1, source_target_pairs={{0,1},{1,0},{2,3},{3,2},{4,5},{5,4},{6,7},{7,6},{8,9},{9,8},{10,11... | collective-permute-start | bytes 1572872 | tf_op jit(solution)/shard_map/ppermute | solution.py:169
  23.7 4.9 %collective-permute-start.5 = (bf16[1024,256]{1,0:T(8,128)(2,1)S(1)}, bf16[1024,256]{1,0:T(8,128)(2,1)S(1)}, u32[]{:S(2)}, u32[]{:S(2)}) collective-permute-start(bf16[1024,256]{1,0:T(8,128)(2,1)S(1)} %collective-permute-done.4.refs_3_), channel_id=1, source_target_pairs={{0,1},{1,0},{2,3},{3,2},{4,5},{5,4},{6,7},{7,6},{8,9},{9,8},{10,11... | collective-permute-start | bytes 1572872 | tf_op jit(solution)/shard_map/ppermute | solution.py:169
  26.6 3.8 %collective-permute-start.6 = (bf16[1024,256]{1,0:T(8,128)(2,1)S(1)}, bf16[1024,256]{1,0:T(8,128)(2,1)S(1)}, u32[]{:S(2)}, u32[]{:S(2)}) collective-permute-start(bf16[1024,256]{1,0:T(8,128)(2,1)S(1)} %collective-permute-done.2.refs_5_), channel_id=1, source_target_pairs={{0,1},{1,0},{2,3},{3,2},{4,5},{5,4},{6,7},{7,6},{8,9},{9,8},{10,11... | collective-permute-start | bytes 1572872 | tf_op jit(solution)/shard_map/ppermute | solution.py:169
  35.9 43.7 %all-to-all-start = ((bf16[64,8,896]{2,1,0:T(8,128)(2,1)}), bf16[64,8,896]{2,1,0:T(8,128)(2,1)S(1)}, u32[]{:S(2)}, u32[]{:S(2)}) async-start(bf16[64,8,896]{2,1,0:T(8,128)(2,1)} %bitcast.9), calls=%async_computation | async-start | bytes 1835008 | tf_op jit(solution)/shard_map/all_to_all | solution.py:248

commit v8 on v7

--- a/solution.py
+++ b/solution.py
@@ -33,6 +33,10 @@
         one = reduce(jnp.where(lane_head == head, x, fill), axis=-1, keepdims=True)
         out = jnp.where(lane_head == head, one, out)
     return out
+
+
+def hold_kernel(x_ref, out_ref):
+    out_ref[...] = x_ref[...]
 
 
 def own_kernel(block_ref, x_ref, wk_ref, wv_ref, acc_ref, rest_ref):
@@ -200,20 +204,28 @@
     ahead = along(passages, 1)
     smem = pl.BlockSpec(memory_space=pltpu.SMEM)
     vmem = pl.BlockSpec(memory_space=pltpu.VMEM)
+    small = pltpu.CompilerParams(vmem_limit_bytes=16 * 1024 * 1024)
+    held = pl.pallas_call(
+        hold_kernel,
+        out_shape=jax.ShapeDtypeStruct(passages.shape, bf16),
+        in_specs=[vmem],
+        out_specs=vmem,
+        compiler_params=small,
+        name="hold",
+    )(passages)
+    behind, other = along(held, -1), swap(held)
+    far = along(ahead, 1)
     sums = jax.ShapeDtypeStruct((slots * vectors, 2 * cols), f32)
     projected, rest = pl.pallas_call(
         own_kernel,
         out_shape=(sums, jax.ShapeDtypeStruct((key_weight.shape[0] - features, 2 * cols), bf16)),
         in_specs=[smem] + [vmem] * 3,
         out_specs=(vmem, vmem),
-        compiler_params=pltpu.CompilerParams(vmem_limit_bytes=16 * 1024 * 1024),
+        compiler_params=small,
         name="own_projection",
-    )(block_numbers(), passages, key_weight, value_weight)
-    held, projected, rest = lax.optimization_barrier((passages, projected, rest))
-    behind, other = along(held, -1), swap(held)
-    far = along(ahead, 1)
+    )(block_numbers(), held, key_weight, value_weight)
     ahead_other = swap(ahead)
-    far, ahead_other = lax.optimization_barrier((far, ahead_other))
+    far, ahead_other, projected, rest = lax.optimization_barrier((far, ahead_other, projected, rest))
     near = [other, ahead, ahead_other, behind, swap(behind), far]
     far = swap(far)
     projected = pl.pallas_call(
@@ -221,7 +233,7 @@
         out_shape=sums,
         in_specs=[vmem] * (2 + len(near)),
         out_specs=vmem,
-        compiler_params=pltpu.CompilerParams(vmem_limit_bytes=16 * 1024 * 1024),
+        compiler_params=small,
         name="near_projection",
     )(projected, rest, *near)
     payload = pl.pallas_call(

time: 107 us -> 110 us (1.028)
  the two profiles are of different devices: /device:TPU:8 before, /device:TPU:2 now
where the time goes in v8:
time: 110 us; the launch traced here: 109 us
  waiting for transfers between devices  36.2 us (33%)
  starting transfers between devices  33.5 us (30%)
  blocking collectives  25.1 us (23%)
  Pallas kernels  8.98 us (8%)
  local copies, waits for them, and re-layouts  4.42 us (4%)
    all_to_all x1, waiting for transfers between devices, body(): received = lax.all_to_all(payload, 'psg', 0, 0, tiled=True)  27 us
    all_to_all x1, blocking collectives, body(): outputs = lax.all_to_all(finished, 'psg', 0, 0, tiled=True)  25.1 us
    all_to_all x1, starting transfers between devices, body(): received = lax.all_to_all(payload, 'psg', 0, 0, tiled=True)  13.1 us
    ppermute x3, starting transfers between devices, along(): return lax.ppermute(block, ('pb', 'rep'), pairs)  11.6 us
    ppermute x3, waiting for transfers between devices, along(): return lax.ppermute(block, ('pb', 'rep'), pairs)  9.15 us
    ppermute x4, starting transfers between devices, swap(): return lax.ppermute(block, 'rep', [(0, 1), (1, 0)])  8.68 us
    pallas_call x1, Pallas kernels, body(): pl.pallas_call(local_kernel, out_shape=jax.ShapeDtypeStruct((rows, 3 * co...  5.44 us
    unnamed x12, local copies, waits for them, and re-layouts  3.51 us
  transfers between devices with their start and end apart: 8, of which 3 were waited for; matrix products, arithmetic and copies ran while one was open for 0% of the time, Pallas kernels for 3%

profile of v8, /device:TPU:2, one launch (start us, length us, event | category | flops | bytes accessed | tf_op | source)
XLA Modules:
  0.0 109.0 jit_solution(12017901778098122368)
XLA Ops:
  0.6 3.4 %collective-permute-start = (bf16[1024,256]{1,0:T(8,128)(2,1)}, bf16[1024,256]{1,0:T(8,128)(2,1)S(1)}, u32[]{:S(2)}, u32[]{:S(2)}) collective-permute-start(bf16[1024,256]{1,0:T(8,128)(2,1)} %bitcast.15), channel_id=1, source_target_pairs={{0,2},{1,7},{2,4},{3,1},{4,6},{5,3},{6,0},{7,5},{8,10},{9,15},{10,... | collective-permute-start | bytes 1572872 | tf_op jit(solution)/shard_map/ppermute | solution.py:192
  4.0 0.0 copy-start.2
  4.0 1.0 copy-done.2
  5.1 6.3 %collective-permute-start.4 = (bf16[1024,256]{1,0:T(8,128)(2,1)S(1)}, bf16[1024,256]{1,0:T(8,128)(2,1)S(1)}, u32[]{:S(2)}, u32[]{:S(2)}) collective-permute-start(bf16[1024,256]{1,0:T(8,128)(2,1)S(1)} %hold.1.x_ref), channel_id=1, source_target_pairs={{0,6},{1,3},{2,0},{3,5},{4,2},{5,7},{6,4},{7,1},{8,14},{9,11},{10,... | collective-permute-start | bytes 1572872 | tf_op jit(solution)/shard_map/ppermute | solution.py:192
  11.5 9.0 %collective-permute-done.refs_1_ = bf16[1024,256]{1,0:T(8,128)(2,1)S(1)} collective-permute-done((bf16[1024,256]{1,0:T(8,128)(2,1)}, bf16[1024,256]{1,0:T(8,128)(2,1)S(1)}, u32[]{:S(2)}, u32[]{:S(2)}) %collective-permute-start) | collective-permute-done | bytes 524320 | tf_op jit(solution)/shard_map/ppermute | solution.py:192
  20.5 1.9 %collective-permute-start.1 = (bf16[1024,256]{1,0:T(8,128)(2,1)S(1)}, bf16[1024,256]{1,0:T(8,128)(2,1)S(1)}, u32[]{:S(2)}, u32[]{:S(2)}) collective-permute-start(bf16[1024,256]{1,0:T(8,128)(2,1)S(1)} %collective-permute-done.refs_1_), channel_id=1, source_target_pairs={{0,2},{1,7},{2,4},{3,1},{4,6},{5,3},{6,0},{7,5},{8,10},{9,15},{10,... | collective-permute-start | bytes 1572872 | tf_op jit(solution)/shard_map/ppermute | solution.py:192
  22.4 1.9 %collective-permute-start.2 = (bf16[1024,256]{1,0:T(8,128)(2,1)S(1)}, bf16[1024,256]{1,0:T(8,128)(2,1)S(1)}, u32[]{:S(2)}, u32[]{:S(2)}) collective-permute-start(bf16[1024,256]{1,0:T(8,128)(2,1)S(1)} %collective-permute-done.refs_1_), channel_id=1, source_target_pairs={{0,1},{1,0},{2,3},{3,2},{4,5},{5,4},{6,7},{7,6},{8,9},{9,8},{10,11... | collective-permute-start | bytes 1572872 | tf_op jit(solution)/shard_map/ppermute | solution.py:173
  24.3 2.4 %collective-permute-start.3 = (bf16[1024,256]{1,0:T(8,128)(2,1)S(1)}, bf16[1024,256]{1,0:T(8,128)(2,1)S(1)}, u32[]{:S(2)}, u32[]{:S(2)}) collective-permute-start(bf16[1024,256]{1,0:T(8,128)(2,1)S(1)} %hold.1.x_ref), channel_id=1, source_target_pairs={{0,1},{1,0},{2,3},{3,2},{4,5},{5,4},{6,7},{7,6},{8,9},{9,8},{10,11... | collective-permute-start | bytes 1572872 | tf_op jit(solution)/shard_map/ppermute | solution.py:173
  26.8 0.1 stack.35.block_ref
  26.9 0.0 copy-start
  26.9 1.2 %copy-done = bf16[2048,256]{1,0:T(8,128)(2,1)S(1)} copy-done((bf16[2048,256]{1,0:T(8,128)(2,1)S(1)}, bf16[2048,256]{1,0:T(8,128)(2,1)}, u32[]{:S(2)}) %copy-start) | copy-done | bytes 1048600
  28.1 0.0 copy-start.1
  28.1 1.2 %copy-done.1 = bf16[2048,256]{1,0:T(8,128)(2,1)S(1)} copy-done((bf16[2048,256]{1,0:T(8,128)(2,1)S(1)}, bf16[2048,256]{1,0:T(8,128)(2,1)}, u32[]{:S(2)}) %copy-start.1) | copy-done | bytes 1048600
  29.3 1.0 own_projection.1
  30.4 0.0 collective-permute-done.4.refs_3_
  30.4 1.9 %collective-permute-start.5 = (bf16[1024,256]{1,0:T(8,128)(2,1)S(1)}, bf16[1024,256]{1,0:T(8,128)(2,1)S(1)}, u32[]{:S(2)}, u32[]{:S(2)}) collective-permute-start(bf16[1024,256]{1,0:T(8,128)(2,1)S(1)} %collective-permute-done.4.refs_3_), channel_id=1, source_target_pairs={{0,1},{1,0},{2,3},{3,2},{4,5},{5,4},{6,7},{7,6},{8,9},{9,8},{10,11... | collective-permute-start | bytes 1572872 | tf_op jit(solution)/shard_map/ppermute | solution.py:173
  32.3 0.1 collective-permute-done.1.refs_5_
  32.5 0.0 collective-permute-done.2.refs_2_
  32.5 2.4 %collective-permute-start.6 = (bf16[1024,256]{1,0:T(8,128)(2,1)S(1)}, bf16[1024,256]{1,0:T(8,128)(2,1)S(1)}, u32[]{:S(2)}, u32[]{:S(2)}) collective-permute-start(bf16[1024,256]{1,0:T(8,128)(2,1)S(1)} %collective-permute-done.1.refs_5_), channel_id=1, source_target_pairs={{0,1},{1,0},{2,3},{3,2},{4,5},{5,4},{6,7},{7,6},{8,9},{9,8},{10,11... | collective-permute-start | bytes 1572872 | tf_op jit(solution)/shard_map/ppermute | solution.py:173
  34.9 0.0 collective-permute-done.3.refs_0_
  34.9 0.0 collective-permute-done.5.refs_4_
  34.9 1.8 %near_projection.1.acc_ref = f32[1024,512]{1,0:T(8,128)S(1)} custom-call(f32[1024,512]{1,0:T(8,128)S(1)} %get-tuple-element.10.acc_ref, bf16[1792,512]{1,0:T(8,128)(2,1)S(1)} %get-tuple-element.11.rest_ref.refs_1_, bf16[1024,256]{1,0:T(8,128)(2,1)S(1)} %collective-permute-done.3.refs_0_, bf16[1024,256]{1,0:T(8,128)(2,1)S(1)} %collective-permute-done.refs_1_, ...), custom_call_target="tpu_custom_call" | custom-call | tf_op jit(solution)/shard_map/near_projection/pallas_call | solution.py:231
  36.7 0.0 collective-permute-done.6.refs_0_
  36.8 0.0 copy-done.3
  36.8 0.0 copy-done.4
  36.8 0.0 copy-done.5
  36.8 5.4 %local_sums.1 = bf16[512,896]{1,0:T(8,128)(2,1)} custom-call(s32[32]{0:T(128)S(1)} %copy-done.5, f32[1024,512]{1,0:T(8,128)S(1)} %near_projection.1.acc_ref, bf16[1024,256]{1,0:T(8,128)(2,1)S(1)} %collective-permute-done.6.refs_0_, bf16[1792,512]{1,0:T(8,128)(2,1)S(1)} %get-tuple-element.11.rest_ref.refs_1_, bf16[512,256]{1,0:T(8,128)(2,1)S(1)} %copy-done.4, ...), custom_call_target="tpu_custom_call" | custom-call | tf_op jit(solution)/shard_map/local_sums/pallas_call | solution.py:239
  42.2 13.1 %all-to-all-start = ((bf16[64,8,896]{2,1,0:T(8,128)(2,1)}), bf16[64,8,896]{2,1,0:T(8,128)(2,1)S(1)}, u32[]{:S(2)}, u32[]{:S(2)}) async-start(bf16[64,8,896]{2,1,0:T(8,128)(2,1)} %bitcast.9), calls=%async_computation | async-start | bytes 1835008 | tf_op jit(solution)/shard_map/all_to_all | solution.py:260
  55.4 27.0 %all-to-all-done = bf16[64,8,896]{2,1,0:T(8,128)(2,1)S(1)} async-done(((bf16[64,8,896]{2,1,0:T(8,128)(2,1)}), bf16[64,8,896]{2,1,0:T(8,128)(2,1)S(1)}, u32[]{:S(2)}, u32[]{:S(2)}) %all-to-all-start) | async-done | bytes 917536 | tf_op jit(solution)/shard_map/all_to_all | solution.py:260
  82.4 0.7 final_sums.1
  83.1 25.1 %all_to_all.23 = bf16[64,8,512]{2,1,0:T(8,128)(2,1)S(1)} all-to-all(bf16[64,8,512]{2,1,0:T(8,128)(2,1)S(1)} %bitcast.14), channel_id=1, replica_groups=mesh['psg'=64,'pb'=4,'rep'=2] {'psg'}, dimensions={0} | all-to-all | bytes 1048576 | tf_op jit(solution)/shard_map/all_to_all | solution.py:270
  108.2 0.8 fusion
  (5 shorter events, 0.0 us)
Async XLA Ops:
  0.6 19.8 %collective-permute-start = (bf16[1024,256]{1,0:T(8,128)(2,1)}, bf16[1024,256]{1,0:T(8,128)(2,1)S(1)}, u32[]{:S(2)}, u32[]{:S(2)}) collective-permute-start(bf16[1024,256]{1,0:T(8,128)(2,1)} %bitcast.15), channel_id=1, source_target_pairs={{0,2},{1,7},{2,4},{3,1},{4,6},{5,3},{6,0},{7,5},{8,10},{9,15},{10,... | collective-permute-start | bytes 1572872 | tf_op jit(solution)/shard_map/ppermute | solution.py:192
  4.0 1.1 copy-start.2
  5.1 25.3 %collective-permute-start.4 = (bf16[1024,256]{1,0:T(8,128)(2,1)S(1)}, bf16[1024,256]{1,0:T(8,128)(2,1)S(1)}, u32[]{:S(2)}, u32[]{:S(2)}) collective-permute-start(bf16[1024,256]{1,0:T(8,128)(2,1)S(1)} %hold.1.x_ref), channel_id=1, source_target_pairs={{0,6},{1,3},{2,0},{3,5},{4,2},{5,7},{6,4},{7,1},{8,14},{9,11},{10,... | collective-permute-start | bytes 1572872 | tf_op jit(solution)/shard_map/ppermute | solution.py:192
  20.5 12.0 %collective-permute-start.1 = (bf16[1024,256]{1,0:T(8,128)(2,1)S(1)}, bf16[1024,256]{1,0:T(8,128)(2,1)S(1)}, u32[]{:S(2)}, u32[]{:S(2)}) collective-permute-start(bf16[1024,256]{1,0:T(8,128)(2,1)S(1)} %collective-permute-done.refs_1_), channel_id=1, source_target_pairs={{0,2},{1,7},{2,4},{3,1},{4,6},{5,3},{6,0},{7,5},{8,10},{9,15},{10,... | collective-permute-start | bytes 1572872 | tf_op jit(solution)/shard_map/ppermute | solution.py:192
  22.4 10.1 %collective-permute-start.2 = (bf16[1024,256]{1,0:T(8,128)(2,1)S(1)}, bf16[1024,256]{1,0:T(8,128)(2,1)S(1)}, u32[]{:S(2)}, u32[]{:S(2)}) collective-permute-start(bf16[1024,256]{1,0:T(8,128)(2,1)S(1)} %collective-permute-done.refs_1_), channel_id=1, source_target_pairs={{0,1},{1,0},{2,3},{3,2},{4,5},{5,4},{6,7},{7,6},{8,9},{9,8},{10,11... | collective-permute-start | bytes 1572872 | tf_op jit(solution)/shard_map/ppermute | solution.py:173
  24.3 10.6 %collective-permute-start.3 = (bf16[1024,256]{1,0:T(8,128)(2,1)S(1)}, bf16[1024,256]{1,0:T(8,128)(2,1)S(1)}, u32[]{:S(2)}, u32[]{:S(2)}) collective-permute-start(bf16[1024,256]{1,0:T(8,128)(2,1)S(1)} %hold.1.x_ref), channel_id=1, source_target_pairs={{0,1},{1,0},{2,3},{3,2},{4,5},{5,4},{6,7},{7,6},{8,9},{9,8},{10,11... | collective-permute-start | bytes 1572872 | tf_op jit(solution)/shard_map/ppermute | solution.py:173
  26.9 1.2 %copy-start = (bf16[2048,256]{1,0:T(8,128)(2,1)S(1)}, bf16[2048,256]{1,0:T(8,128)(2,1)}, u32[]{:S(2)}) copy-start(bf16[2048,256]{1,0:T(8,128)(2,1)} %wk_ref.1) | copy-start | bytes 3145732
  28.1 1.2 %copy-start.1 = (bf16[2048,256]{1,0:T(8,128)(2,1)S(1)}, bf16[2048,256]{1,0:T(8,128)(2,1)}, u32[]{:S(2)}) copy-start(bf16[2048,256]{1,0:T(8,128)(2,1)} %wv_ref.1) | copy-start | bytes 3145732
  30.4 4.5 %collective-permute-start.5 = (bf16[1024,256]{1,0:T(8,128)(2,1)S(1)}, bf16[1024,256]{1,0:T(8,128)(2,1)S(1)}, u32[]{:S(2)}, u32[]{:S(2)}) collective-permute-start(bf16[1024,256]{1,0:T(8,128)(2,1)S(1)} %collective-permute-done.4.refs_3_), channel_id=1, source_target_pairs={{0,1},{1,0},{2,3},{3,2},{4,5},{5,4},{6,7},{7,6},{8,9},{9,8},{10,11... | collective-permute-start | bytes 1572872 | tf_op jit(solution)/shard_map/ppermute | solution.py:173
  32.5 4.3 %copy-start.3 = (bf16[512,256]{1,0:T(8,128)(2,1)S(1)}, bf16[512,256]{1,0:T(8,128)(2,1)}, u32[]{:S(2)}) copy-start(bf16[512,256]{1,0:T(8,128)(2,1)} %refs_3_.1) | copy-start | bytes 786436
  32.5 4.3 %copy-start.4 = (bf16[512,256]{1,0:T(8,128)(2,1)S(1)}, bf16[512,256]{1,0:T(8,128)(2,1)}, u32[]{:S(2)}) copy-start(bf16[512,256]{1,0:T(8,128)(2,1)} %refs_2_.1) | copy-start | bytes 786436
  32.5 4.3 %copy-start.5 = (s32[32]{0:T(128)S(1)}, s32[32]{0:T(128)}, u32[]{:S(2)}) copy-start(s32[32]{0:T(128)} %owner_ref.1) | copy-start | bytes 388
  32.5 4.3 %collective-permute-start.6 = (bf16[1024,256]{1,0:T(8,128)(2,1)S(1)}, bf16[1024,256]{1,0:T(8,128)(2,1)S(1)}, u32[]{:S(2)}, u32[]{:S(2)}) collective-permute-start(bf16[1024,256]{1,0:T(8,128)(2,1)S(1)} %collective-permute-done.1.refs_5_), channel_id=1, source_target_pairs={{0,1},{1,0},{2,3},{3,2},{4,5},{5,4},{6,7},{7,6},{8,9},{9,8},{10,11... | collective-permute-start | bytes 1572872 | tf_op jit(solution)/shard_map/ppermute | solution.py:173
  42.2 40.2 %all-to-all-start = ((bf16[64,8,896]{2,1,0:T(8,128)(2,1)}), bf16[64,8,896]{2,1,0:T(8,128)(2,1)S(1)}, u32[]{:S(2)}, u32[]{:S(2)}) async-start(bf16[64,8,896]{2,1,0:T(8,128)(2,1)} %bitcast.9), calls=%async_computation | async-start | bytes 1835008 | tf_op jit(solution)/shard_map/all_to_all | solution.py:260

commit v9 on v7

--- a/solution.py
+++ b/solution.py
@@ -35,22 +35,42 @@
     return out
 
 
-def own_kernel(block_ref, x_ref, wk_ref, wv_ref, acc_ref, rest_ref):
+def block_rows(block_ref, n, wide):
+    return pl.ds(pl.multiple_of(block_ref[n] * wide, wide), wide)
+
+
+def reorder(block_ref, w_ref, rest_ref, wide):
+    for n in range(1, w_ref.shape[0] // wide):
+        rest_ref[(n - 1) * wide : n * wide, :] = w_ref[block_rows(block_ref, n, wide), :]
+
+
+def own_kernel(block_ref, x_ref, wk_ref, keys_ref, rest_ref):
     wide = x_ref.shape[1]
-    cols = wk_ref.shape[1]
-    for n in range(wk_ref.shape[0] // wide):
-        at = pl.ds(pl.multiple_of(block_ref[n] * wide, wide), wide)
-        for side, ref in enumerate((wk_ref, wv_ref)):
-            columns = slice(side * cols, (side + 1) * cols)
-            if n == 0:
-                acc_ref[:, columns] = jnp.dot(x_ref[...], ref[at, :], preferred_element_type=f32)
-            else:
-                rest_ref[(n - 1) * wide : n * wide, columns] = ref[at, :]
-
-
-def near_kernel(acc_ref, rest_ref, *refs):
+    weight = wk_ref[block_rows(block_ref, 0, wide), :]
+    keys_ref[...] = jnp.dot(x_ref[...], weight, preferred_element_type=f32)
+    reorder(block_ref, wk_ref, rest_ref, wide)
+
+
+def early_kernel(block_ref, keys_ref, rest_key_ref, x_ref, wv_ref, *refs):
+    x_refs, out_ref, rest_ref = refs[:-2], refs[-2], refs[-1]
+    wide = x_ref.shape[1]
+    cols = wv_ref.shape[1]
+    depth = len(x_refs) * wide
+    reorder(block_ref, wv_ref, rest_ref, wide)
+    chunk = 512
+    for low in range(0, x_ref.shape[0], chunk):
+        at = slice(low, low + chunk)
+        rows = jnp.concatenate([x[at, :] for x in x_refs], axis=1)
+        out_ref[at, :cols] = keys_ref[at, :] + jnp.dot(rows, rest_key_ref[:depth, :], preferred_element_type=f32)
+        rows = jnp.concatenate([rows, x_ref[at, :]], axis=1)
+        weight = jnp.concatenate([rest_ref[:depth, :], wv_ref[block_rows(block_ref, 0, wide), :]], axis=0)
+        out_ref[at, cols:] = jnp.dot(rows, weight, preferred_element_type=f32)
+
+
+def late_kernel(first, acc_ref, rest_key_ref, rest_value_ref, *refs):
     x_refs, out_ref = refs[:-1], refs[-1]
-    weight = rest_ref[0 : len(x_refs) * x_refs[0].shape[1], :]
+    at = slice(first, first + len(x_refs) * x_refs[0].shape[1])
+    weight = jnp.concatenate([rest_key_ref[at, :], rest_value_ref[at, :]], axis=1)
     chunk = 512
     for low in range(0, acc_ref.shape[0], chunk):
         rows = jnp.concatenate([x[low : low + chunk, :] for x in x_refs], axis=1)
@@ -60,7 +80,7 @@
 
 
 def local_kernel(owner_ref, acc_ref, *refs):
-    (far_ref, rest_ref, q_ref, c_ref, out_ref, kblk, vblk, score, product, top, total, dots, corr, acc_v, acc_k) = refs
+    (far_ref, rest_key_ref, rest_value_ref, q_ref, c_ref, out_ref, kblk, vblk, score, product, top, total, dots, corr, acc_v, acc_k) = refs
     slots = owner_ref.shape[0]
     half = slots // 2
     cols = q_ref.shape[1]
@@ -78,12 +98,11 @@
         == lax.broadcasted_iota(jnp.int32, (keys, cols), 1) // HDIM
     ).astype(f32).astype(bf16)
 
+    weight = jnp.concatenate([ref[-far_ref.shape[1] :, :] for ref in (rest_key_ref, rest_value_ref)], axis=1)
     for side in range(2):
         low = side * half * PL
         rows = far_ref[low : low + half * PL, :]
-        projected = acc_ref[low : low + half * PL, :] + jnp.dot(
-            rows, rest_ref[-rows.shape[1] :, :], preferred_element_type=f32
-        )
+        projected = acc_ref[low : low + half * PL, :] + jnp.dot(rows, weight, preferred_element_type=f32)
         projected = projected.astype(bf16)
         for i in range(half):
             slot = side * half + i
@@ -197,37 +216,51 @@
     own = rows // devices
 
     passages = prefixes.reshape(slots * vectors, features)
-    ahead = along(passages, 1)
     smem = pl.BlockSpec(memory_space=pltpu.SMEM)
     vmem = pl.BlockSpec(memory_space=pltpu.VMEM)
-    sums = jax.ShapeDtypeStruct((slots * vectors, 2 * cols), f32)
-    projected, rest = pl.pallas_call(
+    small = pltpu.CompilerParams(vmem_limit_bytes=16 * 1024 * 1024)
+    count = slots * vectors
+    sums = jax.ShapeDtypeStruct((count, 2 * cols), f32)
+    rest_rows = jax.ShapeDtypeStruct((key_weight.shape[0] - features, cols), bf16)
+    block = block_numbers()
+
+    ahead = along(passages, 1)
+    keys_sum, rest_key = pl.pallas_call(
         own_kernel,
-        out_shape=(sums, jax.ShapeDtypeStruct((key_weight.shape[0] - features, 2 * cols), bf16)),
-        in_specs=[smem] + [vmem] * 3,
+        out_shape=(jax.ShapeDtypeStruct((count, cols), f32), rest_rows),
+        in_specs=[smem] + [vmem] * 2,
         out_specs=(vmem, vmem),
-        compiler_params=pltpu.CompilerParams(vmem_limit_bytes=16 * 1024 * 1024),
-        name="own_projection",
-    )(block_numbers(), passages, key_weight, value_weight)
-    held, projected, rest = lax.optimization_barrier((passages, projected, rest))
+        compiler_params=small,
+        name="own_keys",
+    )(block, passages, key_weight)
+    held, keys_sum, rest_key = lax.optimization_barrier((passages, keys_sum, rest_key))
     behind, other = along(held, -1), swap(held)
     far = along(ahead, 1)
     ahead_other = swap(ahead)
-    far, ahead_other = lax.optimization_barrier((far, ahead_other))
-    near = [other, ahead, ahead_other, behind, swap(behind), far]
+    early = [other, ahead]
+    projected, rest_value = pl.pallas_call(
+        early_kernel,
+        out_shape=(sums, rest_rows),
+        in_specs=[smem] + [vmem] * (4 + len(early)),
+        out_specs=(vmem, vmem),
+        compiler_params=small,
+        name="early_blocks",
+    )(block, keys_sum, rest_key, held, value_weight, *early)
+    far, ahead_other, projected, rest_value = lax.optimization_barrier((far, ahead_other, projected, rest_value))
+    late = [ahead_other, behind, swap(behind), far]
     far = swap(far)
     projected = pl.pallas_call(
-        near_kernel,
+        lambda *refs: late_kernel(len(early) * features, *refs),
         out_shape=sums,
-        in_specs=[vmem] * (2 + len(near)),
+        in_specs=[vmem] * (3 + len(late)),
         out_specs=vmem,
-        compiler_params=pltpu.CompilerParams(vmem_limit_bytes=16 * 1024 * 1024),
-        name="near_projection",
-    )(projected, rest, *near)
+        compiler_params=small,
+        name="late_blocks",
+    )(projected, rest_key, rest_value, *late)
     payload = pl.pallas_call(
         local_kernel,
         out_shape=jax.ShapeDtypeStruct((rows, 3 * cols + keys), bf16),
-        in_specs=[smem] + [vmem] * 5,
+        in_specs=[smem] + [vmem] * 6,
         out_specs=vmem,
         scratch_shapes=[
             pltpu.VMEM((slots, keys, cols), bf16),
@@ -243,7 +276,7 @@
         ],
         compiler_params=pltpu.CompilerParams(vmem_limit_bytes=24 * 1024 * 1024),
         name="local_sums",
-    )(owner, projected, far, rest, queries, cotangent)
+    )(owner, projected, far, rest_key, rest_value, queries, cotangent)
 
     received = lax.all_to_all(payload, "psg", 0, 0, tiled=True)
     own_cotangent = lax.dynamic_slice_in_dim(cotangent, lax.axis_index("psg") * own, own, 0).astype(f32)

time: 107 us -> 105 us (0.981)
  the two profiles are of different devices: /device:TPU:8 before, /device:TPU:6 now
where the time goes in v9:
time: 105 us; the launch traced here: 104 us
  waiting for transfers between devices  33.1 us (32%)
  starting transfers between devices  31.9 us (30%)
  blocking collectives  25.2 us (24%)
  Pallas kernels  9.66 us (9%)
  local copies, waits for them, and re-layouts  3.19 us (3%)
    all_to_all x1, waiting for transfers between devices, body(): received = lax.all_to_all(payload, 'psg', 0, 0, tiled=True)  27.1 us
    all_to_all x1, blocking collectives, body(): outputs = lax.all_to_all(finished, 'psg', 0, 0, tiled=True)  25.2 us
    ppermute x3, starting transfers between devices, along(): return lax.ppermute(block, ('pb', 'rep'), pairs)  15.2 us
    all_to_all x1, starting transfers between devices, body(): received = lax.all_to_all(payload, 'psg', 0, 0, tiled=True)  8.48 us
    ppermute x4, starting transfers between devices, swap(): return lax.ppermute(block, 'rep', [(0, 1), (1, 0)])  8.3 us
    pallas_call x1, Pallas kernels, body(): pl.pallas_call(local_kernel, out_shape=jax.ShapeDtypeStruct((rows, 3 * co...  5.45 us
    ppermute x3, waiting for transfers between devices, along(): return lax.ppermute(block, ('pb', 'rep'), pairs)  5.43 us
    unnamed x12, local copies, waits for them, and re-layouts  2.28 us
  transfers between devices with their start and end apart: 8, of which 4 were waited for; matrix products, arithmetic and copies ran while one was open for 0% of the time, Pallas kernels for 3%

profile of v9, /device:TPU:6, one launch (start us, length us, event | category | flops | bytes accessed | tf_op | source)
XLA Modules:
  0.0 103.9 jit_solution(4737424313617520959)
XLA Ops:
  0.6 7.8 %collective-permute-start = (bf16[1024,256]{1,0:T(8,128)(2,1)}, bf16[1024,256]{1,0:T(8,128)(2,1)S(1)}, u32[]{:S(2)}, u32[]{:S(2)}) collective-permute-start(bf16[1024,256]{1,0:T(8,128)(2,1)} %bitcast.14), channel_id=1, source_target_pairs={{0,2},{1,7},{2,4},{3,1},{4,6},{5,3},{6,0},{7,5},{8,10},{9,15},{10,... | collective-permute-start | bytes 1572872 | tf_op jit(solution)/shard_map/ppermute | solution.py:207
  8.4 0.1 stack.35.block_ref
  8.5 0.0 copy-start
  8.5 1.0 %copy-done = bf16[32,32,256]{2,1,0:T(8,128)(2,1)S(1)} copy-done((bf16[32,32,256]{2,1,0:T(8,128)(2,1)S(1)}, bf16[32,32,256]{2,1,0:T(8,128)(2,1)}, u32[]{:S(2)}) %copy-start) | copy-done | bytes 524312
  9.6 0.0 copy-start.2
  9.6 1.2 %copy-done.2 = bf16[2048,256]{1,0:T(8,128)(2,1)S(1)} copy-done((bf16[2048,256]{1,0:T(8,128)(2,1)S(1)}, bf16[2048,256]{1,0:T(8,128)(2,1)}, u32[]{:S(2)}) %copy-start.2) | copy-done | bytes 1048600
  10.8 0.8 own_keys.1
  11.7 1.9 %collective-permute-start.4 = (bf16[1024,256]{1,0:T(8,128)(2,1)S(1)}, bf16[1024,256]{1,0:T(8,128)(2,1)S(1)}, u32[]{:S(2)}, u32[]{:S(2)}) collective-permute-start(bf16[1024,256]{1,0:T(8,128)(2,1)S(1)} %bitcast.16), channel_id=1, source_target_pairs={{0,6},{1,3},{2,0},{3,5},{4,2},{5,7},{6,4},{7,1},{8,14},{9,11},{10,... | collective-permute-start | bytes 1572872 | tf_op jit(solution)/shard_map/ppermute | solution.py:207
  13.6 1.9 %collective-permute-start.3 = (bf16[1024,256]{1,0:T(8,128)(2,1)S(1)}, bf16[1024,256]{1,0:T(8,128)(2,1)S(1)}, u32[]{:S(2)}, u32[]{:S(2)}) collective-permute-start(bf16[1024,256]{1,0:T(8,128)(2,1)S(1)} %bitcast.17), channel_id=1, source_target_pairs={{0,1},{1,0},{2,3},{3,2},{4,5},{5,4},{6,7},{7,6},{8,9},{9,8},{10,11... | collective-permute-start | bytes 1572872 | tf_op jit(solution)/shard_map/ppermute | solution.py:188
  15.5 4.6 %collective-permute-done.refs_1_ = bf16[1024,256]{1,0:T(8,128)(2,1)S(1)} collective-permute-done((bf16[1024,256]{1,0:T(8,128)(2,1)}, bf16[1024,256]{1,0:T(8,128)(2,1)S(1)}, u32[]{:S(2)}, u32[]{:S(2)}) %collective-permute-start) | collective-permute-done | bytes 524320 | tf_op jit(solution)/shard_map/ppermute | solution.py:207
  20.1 5.5 %collective-permute-start.1 = (bf16[1024,256]{1,0:T(8,128)(2,1)S(1)}, bf16[1024,256]{1,0:T(8,128)(2,1)S(1)}, u32[]{:S(2)}, u32[]{:S(2)}) collective-permute-start(bf16[1024,256]{1,0:T(8,128)(2,1)S(1)} %collective-permute-done.refs_1_), channel_id=1, source_target_pairs={{0,2},{1,7},{2,4},{3,1},{4,6},{5,3},{6,0},{7,5},{8,10},{9,15},{10,... | collective-permute-start | bytes 1572872 | tf_op jit(solution)/shard_map/ppermute | solution.py:207
  25.6 1.9 %collective-permute-start.2 = (bf16[1024,256]{1,0:T(8,128)(2,1)S(1)}, bf16[1024,256]{1,0:T(8,128)(2,1)S(1)}, u32[]{:S(2)}, u32[]{:S(2)}) collective-permute-start(bf16[1024,256]{1,0:T(8,128)(2,1)S(1)} %collective-permute-done.refs_1_), channel_id=1, source_target_pairs={{0,1},{1,0},{2,3},{3,2},{4,5},{5,4},{6,7},{7,6},{8,9},{9,8},{10,11... | collective-permute-start | bytes 1572872 | tf_op jit(solution)/shard_map/ppermute | solution.py:188
  27.5 0.0 collective-permute-done.4.refs_4_
  27.5 2.4 %collective-permute-start.5 = (bf16[1024,256]{1,0:T(8,128)(2,1)S(1)}, bf16[1024,256]{1,0:T(8,128)(2,1)S(1)}, u32[]{:S(2)}, u32[]{:S(2)}) collective-permute-start(bf16[1024,256]{1,0:T(8,128)(2,1)S(1)} %collective-permute-done.4.refs_4_), channel_id=1, source_target_pairs={{0,1},{1,0},{2,3},{3,2},{4,5},{5,4},{6,7},{7,6},{8,9},{9,8},{10,11... | collective-permute-start | bytes 1572872 | tf_op jit(solution)/shard_map/ppermute | solution.py:188
  29.9 0.0 collective-permute-done.3.refs_0_
  29.9 0.0 copy-done.1
  29.9 1.4 %early_blocks.1 = (f32[1024,512]{1,0:T(8,128)S(1)}, bf16[1792,256]{1,0:T(8,128)(2,1)S(1)}) custom-call(s32[8]{0:T(128)S(1)} %stack.35.block_ref, f32[1024,256]{1,0:T(8,128)S(1)} %get-tuple-element.15.keys_ref, bf16[1792,256]{1,0:T(8,128)(2,1)S(1)} %get-tuple-element.16.rest_key_ref.refs_1_, bf16[1024,256]{1,0:T(8,128)(2,1)S(1)} %bitcast.18, ...), custom_call_target="tpu_custom_call" | custom-call | tf_op jit(solution)/shard_map/early_blocks/pallas_call | solution.py:241
  31.4 0.9 collective-permute-done.1.refs_6_
  32.2 0.0 collective-permute-done.2.refs_3_
  32.3 2.1 %collective-permute-start.6 = (bf16[1024,256]{1,0:T(8,128)(2,1)S(1)}, bf16[1024,256]{1,0:T(8,128)(2,1)S(1)}, u32[]{:S(2)}, u32[]{:S(2)}) collective-permute-start(bf16[1024,256]{1,0:T(8,128)(2,1)S(1)} %collective-permute-done.1.refs_6_), channel_id=1, source_target_pairs={{0,1},{1,0},{2,3},{3,2},{4,5},{5,4},{6,7},{7,6},{8,9},{9,8},{10,11... | collective-permute-start | bytes 1572872 | tf_op jit(solution)/shard_map/ppermute | solution.py:188
  34.3 0.0 collective-permute-done.5.refs_5_
  34.3 1.3 %late_blocks.1.acc_ref = f32[1024,512]{1,0:T(8,128)S(1)} custom-call(f32[1024,512]{1,0:T(8,128)S(1)} %get-tuple-element.20.refs_0_, bf16[1792,256]{1,0:T(8,128)(2,1)S(1)} %get-tuple-element.16.rest_key_ref.refs_1_, bf16[1792,256]{1,0:T(8,128)(2,1)S(1)} %get-tuple-element.21.refs_2_, bf16[1024,256]{1,0:T(8,128)(2,1)S(1)} %collective-permute-done.2.refs_3_, ...), custom_call_target="tpu_custom_call" | custom-call | tf_op jit(solution)/shard_map/late_blocks/pallas_call | solution.py:252
  35.6 0.6 collective-permute-done.6.refs_0_
  36.2 0.0 copy-done.3
  36.2 0.0 copy-done.4
  36.2 0.0 copy-done.5
  36.2 5.5 %local_sums.1 = bf16[512,896]{1,0:T(8,128)(2,1)} custom-call(s32[32]{0:T(128)S(1)} %copy-done.5, f32[1024,512]{1,0:T(8,128)S(1)} %late_blocks.1.acc_ref, bf16[1024,256]{1,0:T(8,128)(2,1)S(1)} %collective-permute-done.6.refs_0_, bf16[1792,256]{1,0:T(8,128)(2,1)S(1)} %get-tuple-element.16.rest_key_ref.refs_1_, ...), custom_call_target="tpu_custom_call" | custom-call | tf_op jit(solution)/shard_map/local_sums/pallas_call | solution.py:260
  41.7 8.5 %all-to-all-start = ((bf16[64,8,896]{2,1,0:T(8,128)(2,1)}), bf16[64,8,896]{2,1,0:T(8,128)(2,1)S(1)}, u32[]{:S(2)}, u32[]{:S(2)}) async-start(bf16[64,8,896]{2,1,0:T(8,128)(2,1)} %bitcast.9), calls=%async_computation | async-start | bytes 1835008 | tf_op jit(solution)/shard_map/all_to_all | solution.py:281
  50.2 27.1 %all-to-all-done = bf16[64,8,896]{2,1,0:T(8,128)(2,1)S(1)} async-done(((bf16[64,8,896]{2,1,0:T(8,128)(2,1)}), bf16[64,8,896]{2,1,0:T(8,128)(2,1)S(1)}, u32[]{:S(2)}, u32[]{:S(2)}) %all-to-all-start) | async-done | bytes 917536 | tf_op jit(solution)/shard_map/all_to_all | solution.py:281
  77.2 0.7 final_sums.1
  77.9 25.2 %all_to_all.23 = bf16[64,8,512]{2,1,0:T(8,128)(2,1)S(1)} all-to-all(bf16[64,8,512]{2,1,0:T(8,128)(2,1)S(1)} %bitcast.19), channel_id=1, replica_groups=mesh['psg'=64,'pb'=4,'rep'=2] {'psg'}, dimensions={0} | all-to-all | bytes 1048576 | tf_op jit(solution)/shard_map/all_to_all | solution.py:291
  103.1 0.8 fusion
  (5 shorter events, 0.0 us)
Async XLA Ops:
  0.6 19.4 %collective-permute-start = (bf16[1024,256]{1,0:T(8,128)(2,1)}, bf16[1024,256]{1,0:T(8,128)(2,1)S(1)}, u32[]{:S(2)}, u32[]{:S(2)}) collective-permute-start(bf16[1024,256]{1,0:T(8,128)(2,1)} %bitcast.14), channel_id=1, source_target_pairs={{0,2},{1,7},{2,4},{3,1},{4,6},{5,3},{6,0},{7,5},{8,10},{9,15},{10,... | collective-permute-start | bytes 1572872 | tf_op jit(solution)/shard_map/ppermute | solution.py:207
  8.5 1.0 %copy-start = (bf16[32,32,256]{2,1,0:T(8,128)(2,1)S(1)}, bf16[32,32,256]{2,1,0:T(8,128)(2,1)}, u32[]{:S(2)}) copy-start(bf16[32,32,256]{2,1,0:T(8,128)(2,1)} %param.7) | copy-start | bytes 1572868
  9.6 1.2 %copy-start.2 = (bf16[2048,256]{1,0:T(8,128)(2,1)S(1)}, bf16[2048,256]{1,0:T(8,128)(2,1)}, u32[]{:S(2)}) copy-start(bf16[2048,256]{1,0:T(8,128)(2,1)} %wk_ref.1) | copy-start | bytes 3145732
  10.8 19.1 %copy-start.1 = (bf16[2048,256]{1,0:T(8,128)(2,1)S(1)}, bf16[2048,256]{1,0:T(8,128)(2,1)}, u32[]{:S(2)}) copy-start(bf16[2048,256]{1,0:T(8,128)(2,1)} %wv_ref.1) | copy-start | bytes 3145732
  11.7 15.8 %collective-permute-start.4 = (bf16[1024,256]{1,0:T(8,128)(2,1)S(1)}, bf16[1024,256]{1,0:T(8,128)(2,1)S(1)}, u32[]{:S(2)}, u32[]{:S(2)}) collective-permute-start(bf16[1024,256]{1,0:T(8,128)(2,1)S(1)} %bitcast.16), channel_id=1, source_target_pairs={{0,6},{1,3},{2,0},{3,5},{4,2},{5,7},{6,4},{7,1},{8,14},{9,11},{10,... | collective-permute-start | bytes 1572872 | tf_op jit(solution)/shard_map/ppermute | solution.py:207
  13.6 16.3 %collective-permute-start.3 = (bf16[1024,256]{1,0:T(8,128)(2,1)S(1)}, bf16[1024,256]{1,0:T(8,128)(2,1)S(1)}, u32[]{:S(2)}, u32[]{:S(2)}) collective-permute-start(bf16[1024,256]{1,0:T(8,128)(2,1)S(1)} %bitcast.17), channel_id=1, source_target_pairs={{0,1},{1,0},{2,3},{3,2},{4,5},{5,4},{6,7},{7,6},{8,9},{9,8},{10,11... | collective-permute-start | bytes 1572872 | tf_op jit(solution)/shard_map/ppermute | solution.py:188
  20.1 12.2 %collective-permute-start.1 = (bf16[1024,256]{1,0:T(8,128)(2,1)S(1)}, bf16[1024,256]{1,0:T(8,128)(2,1)S(1)}, u32[]{:S(2)}, u32[]{:S(2)}) collective-permute-start(bf16[1024,256]{1,0:T(8,128)(2,1)S(1)} %collective-permute-done.refs_1_), channel_id=1, source_target_pairs={{0,2},{1,7},{2,4},{3,1},{4,6},{5,3},{6,0},{7,5},{8,10},{9,15},{10,... | collective-permute-start | bytes 1572872 | tf_op jit(solution)/shard_map/ppermute | solution.py:207
  25.6 6.7 %collective-permute-start.2 = (bf16[1024,256]{1,0:T(8,128)(2,1)S(1)}, bf16[1024,256]{1,0:T(8,128)(2,1)S(1)}, u32[]{:S(2)}, u32[]{:S(2)}) collective-permute-start(bf16[1024,256]{1,0:T(8,128)(2,1)S(1)} %collective-permute-done.refs_1_), channel_id=1, source_target_pairs={{0,1},{1,0},{2,3},{3,2},{4,5},{5,4},{6,7},{7,6},{8,9},{9,8},{10,11... | collective-permute-start | bytes 1572872 | tf_op jit(solution)/shard_map/ppermute | solution.py:188
  27.5 6.8 %collective-permute-start.5 = (bf16[1024,256]{1,0:T(8,128)(2,1)S(1)}, bf16[1024,256]{1,0:T(8,128)(2,1)S(1)}, u32[]{:S(2)}, u32[]{:S(2)}) collective-permute-start(bf16[1024,256]{1,0:T(8,128)(2,1)S(1)} %collective-permute-done.4.refs_4_), channel_id=1, source_target_pairs={{0,1},{1,0},{2,3},{3,2},{4,5},{5,4},{6,7},{7,6},{8,9},{9,8},{10,11... | collective-permute-start | bytes 1572872 | tf_op jit(solution)/shard_map/ppermute | solution.py:188
  32.2 3.9 %copy-start.3 = (bf16[512,256]{1,0:T(8,128)(2,1)S(1)}, bf16[512,256]{1,0:T(8,128)(2,1)}, u32[]{:S(2)}) copy-start(bf16[512,256]{1,0:T(8,128)(2,1)} %refs_4_.1) | copy-start | bytes 786436
  32.3 3.9 %copy-start.4 = (bf16[512,256]{1,0:T(8,128)(2,1)S(1)}, bf16[512,256]{1,0:T(8,128)(2,1)}, u32[]{:S(2)}) copy-start(bf16[512,256]{1,0:T(8,128)(2,1)} %refs_3_.1) | copy-start | bytes 786436
  32.3 3.9 %copy-start.5 = (s32[32]{0:T(128)S(1)}, s32[32]{0:T(128)}, u32[]{:S(2)}) copy-start(s32[32]{0:T(128)} %owner_ref.1) | copy-start | bytes 388
  32.3 3.9 %collective-permute-start.6 = (bf16[1024,256]{1,0:T(8,128)(2,1)S(1)}, bf16[1024,256]{1,0:T(8,128)(2,1)S(1)}, u32[]{:S(2)}, u32[]{:S(2)}) collective-permute-start(bf16[1024,256]{1,0:T(8,128)(2,1)S(1)} %collective-permute-done.1.refs_6_), channel_id=1, source_target_pairs={{0,1},{1,0},{2,3},{3,2},{4,5},{5,4},{6,7},{7,6},{8,9},{9,8},{10,11... | collective-permute-start | bytes 1572872 | tf_op jit(solution)/shard_map/ppermute | solution.py:188
  41.7 35.6 %all-to-all-start = ((bf16[64,8,896]{2,1,0:T(8,128)(2,1)}), bf16[64,8,896]{2,1,0:T(8,128)(2,1)S(1)}, u32[]{:S(2)}, u32[]{:S(2)}) async-start(bf16[64,8,896]{2,1,0:T(8,128)(2,1)} %bitcast.9), calls=%async_computation | async-start | bytes 1835008 | tf_op jit(solution)/shard_map/all_to_all | solution.py:281

commit v10 on v9

--- a/solution.py
+++ b/solution.py
@@ -10,6 +10,7 @@
 PL = 32
 QUESTIONS = 16
 PARTS = 3
+ROWS_EACH = 8
 
 masked_value = -1e30
 
@@ -156,11 +157,15 @@
         out_ref[at, 3 * cols :] = extra.astype(bf16)
 
 
-def final_kernel(r_ref, c_ref, out_ref):
-    rows, cols = c_ref.shape
+def final_kernel(block_ref, r_ref, c_ref, out_ref):
+    cols = c_ref.shape[1]
     heads = cols // HDIM
     keys = heads * PL
+    rows = ROWS_EACH
     devices = r_ref.shape[0] // rows
+    place = block_ref[block_ref.shape[0] - 1]
+    pair = c_ref[pl.ds(pl.multiple_of((place >> 1) * 2 * rows, 2 * rows), 2 * rows), :].astype(f32)
+    cotangent = jnp.where((place & 1) == 1, pair[rows:], pair[:rows])
     lane = lax.broadcasted_iota(jnp.int32, (keys, 3 * cols), 0)
     spot = lax.broadcasted_iota(jnp.int32, (keys, 3 * cols), 1)
     pick = (lane // PL == (spot % cols) // HDIM) & ((lane % PL) // PARTS == spot // cols)
@@ -175,7 +180,7 @@
 
     summed = jnp.sum(weight * read(0), axis=0)
     attended = (summed / total).astype(bf16).astype(f32)
-    corr = per_head(c_ref[...] * attended, HDIM, jnp.sum, 0.0)
+    corr = per_head(cotangent * attended, HDIM, jnp.sum, 0.0)
     shift = wide[:, :, 2 * cols :] - corr[None]
     grad = jnp.sum(weight * (read(1) + shift * read(2)), axis=0) / total
     both = jnp.concatenate([attended, grad], axis=1)
@@ -195,7 +200,7 @@
     own = [(pb + shift) % n for shift in (0, n - step, n + step, 2)]
     other = [(pb + shift) % n for shift in (0, n + step, n - step, 2)]
     numbers = [number for pair in zip(own, other) for number in (pair[0] * 2 + rep, pair[1] * 2 + 1 - rep)]
-    return jnp.stack(numbers).astype(jnp.int32)
+    return jnp.stack(numbers + [lax.axis_index("psg")]).astype(jnp.int32)
 
 
 def along(block, way):
@@ -213,7 +218,7 @@
     heads = cols // HDIM
     keys = heads * PL
     devices = lax.axis_size("psg")
-    own = rows // devices
+    assert rows == ROWS_EACH * devices
 
     passages = prefixes.reshape(slots * vectors, features)
     smem = pl.BlockSpec(memory_space=pltpu.SMEM)
@@ -279,15 +284,14 @@
     )(owner, projected, far, rest_key, rest_value, queries, cotangent)
 
     received = lax.all_to_all(payload, "psg", 0, 0, tiled=True)
-    own_cotangent = lax.dynamic_slice_in_dim(cotangent, lax.axis_index("psg") * own, own, 0).astype(f32)
     finished = pl.pallas_call(
         final_kernel,
         out_shape=jax.ShapeDtypeStruct((rows, 2 * cols), bf16),
-        in_specs=[vmem, vmem],
+        in_specs=[smem, vmem, vmem],
         out_specs=vmem,
         compiler_params=pltpu.CompilerParams(vmem_limit_bytes=24 * 1024 * 1024),
         name="final_sums",
-    )(received, own_cotangent)
+    )(block, received, cotangent)
     outputs = lax.all_to_all(finished, "psg", 0, 0, tiled=True)
     return outputs[:, :cols], outputs[:, cols:]
 

time: 105 us -> 105 us (level)
  blocking collectives: 25.2 us -> 60.6 us
  waiting for transfers between devices: 33.1 us -> 6.03 us
  starting transfers between devices: 31.9 us -> 23.5 us
    all_to_all x0 -> x1, blocking collectives: none -> 35.4 us  [body(): received = lax.all_to_all(payload, 'psg', 0, 0, tiled=True)]
    all_to_all x1 -> x0, waiting for transfers between devices: 27.1 us -> none  [body(): received = lax.all_to_all(payload, 'psg', 0, 0, tiled=True)]
    all_to_all x1 -> x0, starting transfers between devices: 8.48 us -> none  [body(): received = lax.all_to_all(payload, 'psg', 0, 0, tiled=True)]
  transfers between devices with their start and end apart: 8 -> 7, of which waited for: 4 -> 3; matrix products, arithmetic and copies ran while one was open for 0% -> 0% of each run, Pallas kernels for 3% -> 3%
where the time goes in v10:
time: 105 us; the launch traced here: 103 us
  blocking collectives  60.6 us (58%)
  starting transfers between devices  23.5 us (22%)
  Pallas kernels  9.25 us (9%)
  waiting for transfers between devices  6.03 us (6%)
  local copies, waits for them, and re-layouts  3.19 us (3%)
    all_to_all x1, blocking collectives, body(): received = lax.all_to_all(payload, 'psg', 0, 0, tiled=True)  35.4 us
    all_to_all x1, blocking collectives, body(): outputs = lax.all_to_all(finished, 'psg', 0, 0, tiled=True)  25.2 us
    ppermute x3, starting transfers between devices, along(): return lax.ppermute(block, ('pb', 'rep'), pairs)  15.2 us
    ppermute x4, starting transfers between devices, swap(): return lax.ppermute(block, 'rep', [(0, 1), (1, 0)])  8.3 us
    ppermute x3, waiting for transfers between devices, along(): return lax.ppermute(block, ('pb', 'rep'), pairs)  5.42 us
    pallas_call x1, Pallas kernels, body(): pl.pallas_call(local_kernel, out_shape=jax.ShapeDtypeStruct((rows, 3 * co...  4.53 us
    unnamed x12, local copies, waits for them, and re-layouts  2.28 us
  transfers between devices with their start and end apart: 7, of which 3 were waited for; matrix products, arithmetic and copies ran while one was open for 0% of the time, Pallas kernels for 3%

profile of v10, /device:TPU:6, one launch (start us, length us, event | category | flops | bytes accessed | tf_op | source)
XLA Modules:
  0.0 103.4 jit_solution(10243630369276706872)
XLA Ops:
  0.6 7.8 %collective-permute-start = (bf16[1024,256]{1,0:T(8,128)(2,1)}, bf16[1024,256]{1,0:T(8,128)(2,1)S(1)}, u32[]{:S(2)}, u32[]{:S(2)}) collective-permute-start(bf16[1024,256]{1,0:T(8,128)(2,1)} %bitcast.16), channel_id=1, source_target_pairs={{0,2},{1,7},{2,4},{3,1},{4,6},{5,3},{6,0},{7,5},{8,10},{9,15},{10,... | collective-permute-start | bytes 1572872 | tf_op jit(solution)/shard_map/ppermute | solution.py:212
  8.4 0.1 stack.39.block_ref
  8.5 0.0 copy-start
  8.5 1.0 %copy-done = bf16[32,32,256]{2,1,0:T(8,128)(2,1)S(1)} copy-done((bf16[32,32,256]{2,1,0:T(8,128)(2,1)S(1)}, bf16[32,32,256]{2,1,0:T(8,128)(2,1)}, u32[]{:S(2)}) %copy-start) | copy-done | bytes 524312
  9.6 0.0 copy-start.3
  9.6 1.2 %copy-done.3 = bf16[2048,256]{1,0:T(8,128)(2,1)S(1)} copy-done((bf16[2048,256]{1,0:T(8,128)(2,1)S(1)}, bf16[2048,256]{1,0:T(8,128)(2,1)}, u32[]{:S(2)}) %copy-start.3) | copy-done | bytes 1048600
  10.8 0.0 copy-start.1
  10.8 0.8 own_keys.1
  11.7 1.9 %collective-permute-start.4 = (bf16[1024,256]{1,0:T(8,128)(2,1)S(1)}, bf16[1024,256]{1,0:T(8,128)(2,1)S(1)}, u32[]{:S(2)}, u32[]{:S(2)}) collective-permute-start(bf16[1024,256]{1,0:T(8,128)(2,1)S(1)} %bitcast.18), channel_id=1, source_target_pairs={{0,6},{1,3},{2,0},{3,5},{4,2},{5,7},{6,4},{7,1},{8,14},{9,11},{10,... | collective-permute-start | bytes 1572872 | tf_op jit(solution)/shard_map/ppermute | solution.py:212
  13.6 1.9 %collective-permute-start.3 = (bf16[1024,256]{1,0:T(8,128)(2,1)S(1)}, bf16[1024,256]{1,0:T(8,128)(2,1)S(1)}, u32[]{:S(2)}, u32[]{:S(2)}) collective-permute-start(bf16[1024,256]{1,0:T(8,128)(2,1)S(1)} %bitcast.19), channel_id=1, source_target_pairs={{0,1},{1,0},{2,3},{3,2},{4,5},{5,4},{6,7},{7,6},{8,9},{9,8},{10,11... | collective-permute-start | bytes 1572872 | tf_op jit(solution)/shard_map/ppermute | solution.py:193
  15.5 4.6 %collective-permute-done.refs_1_ = bf16[1024,256]{1,0:T(8,128)(2,1)S(1)} collective-permute-done((bf16[1024,256]{1,0:T(8,128)(2,1)}, bf16[1024,256]{1,0:T(8,128)(2,1)S(1)}, u32[]{:S(2)}, u32[]{:S(2)}) %collective-permute-start) | collective-permute-done | bytes 524320 | tf_op jit(solution)/shard_map/ppermute | solution.py:212
  20.1 5.5 %collective-permute-start.1 = (bf16[1024,256]{1,0:T(8,128)(2,1)S(1)}, bf16[1024,256]{1,0:T(8,128)(2,1)S(1)}, u32[]{:S(2)}, u32[]{:S(2)}) collective-permute-start(bf16[1024,256]{1,0:T(8,128)(2,1)S(1)} %collective-permute-done.refs_1_), channel_id=1, source_target_pairs={{0,2},{1,7},{2,4},{3,1},{4,6},{5,3},{6,0},{7,5},{8,10},{9,15},{10,... | collective-permute-start | bytes 1572872 | tf_op jit(solution)/shard_map/ppermute | solution.py:212
  25.6 1.9 %collective-permute-start.2 = (bf16[1024,256]{1,0:T(8,128)(2,1)S(1)}, bf16[1024,256]{1,0:T(8,128)(2,1)S(1)}, u32[]{:S(2)}, u32[]{:S(2)}) collective-permute-start(bf16[1024,256]{1,0:T(8,128)(2,1)S(1)} %collective-permute-done.refs_1_), channel_id=1, source_target_pairs={{0,1},{1,0},{2,3},{3,2},{4,5},{5,4},{6,7},{7,6},{8,9},{9,8},{10,11... | collective-permute-start | bytes 1572872 | tf_op jit(solution)/shard_map/ppermute | solution.py:193
  27.5 0.0 collective-permute-done.4.refs_4_
  27.5 2.4 %collective-permute-start.5 = (bf16[1024,256]{1,0:T(8,128)(2,1)S(1)}, bf16[1024,256]{1,0:T(8,128)(2,1)S(1)}, u32[]{:S(2)}, u32[]{:S(2)}) collective-permute-start(bf16[1024,256]{1,0:T(8,128)(2,1)S(1)} %collective-permute-done.4.refs_4_), channel_id=1, source_target_pairs={{0,1},{1,0},{2,3},{3,2},{4,5},{5,4},{6,7},{7,6},{8,9},{9,8},{10,11... | collective-permute-start | bytes 1572872 | tf_op jit(solution)/shard_map/ppermute | solution.py:193
  29.9 0.0 collective-permute-done.3.refs_0_
  29.9 0.0 copy-done.1
  29.9 1.4 %early_blocks.1 = (f32[1024,512]{1,0:T(8,128)S(1)}, bf16[1792,256]{1,0:T(8,128)(2,1)S(1)}) custom-call(s32[9]{0:T(128)S(1)} %stack.39.block_ref, f32[1024,256]{1,0:T(8,128)S(1)} %get-tuple-element.15.keys_ref, bf16[1792,256]{1,0:T(8,128)(2,1)S(1)} %get-tuple-element.16.rest_key_ref.refs_1_, bf16[1024,256]{1,0:T(8,128)(2,1)S(1)} %bitcast.20, ...), custom_call_target="tpu_custom_call" | custom-call | tf_op jit(solution)/shard_map/early_blocks/pallas_call | solution.py:246
  31.4 0.9 collective-permute-done.1.refs_6_
  32.2 0.0 collective-permute-done.2.refs_3_
  32.3 2.1 %collective-permute-start.6 = (bf16[1024,256]{1,0:T(8,128)(2,1)S(1)}, bf16[1024,256]{1,0:T(8,128)(2,1)S(1)}, u32[]{:S(2)}, u32[]{:S(2)}) collective-permute-start(bf16[1024,256]{1,0:T(8,128)(2,1)S(1)} %collective-permute-done.1.refs_6_), channel_id=1, source_target_pairs={{0,1},{1,0},{2,3},{3,2},{4,5},{5,4},{6,7},{7,6},{8,9},{9,8},{10,11... | collective-permute-start | bytes 1572872 | tf_op jit(solution)/shard_map/ppermute | solution.py:193
  34.3 0.0 collective-permute-done.5.refs_5_
  34.3 1.3 %late_blocks.1.acc_ref = f32[1024,512]{1,0:T(8,128)S(1)} custom-call(f32[1024,512]{1,0:T(8,128)S(1)} %get-tuple-element.20.refs_0_, bf16[1792,256]{1,0:T(8,128)(2,1)S(1)} %get-tuple-element.16.rest_key_ref.refs_1_, bf16[1792,256]{1,0:T(8,128)(2,1)S(1)} %get-tuple-element.21.refs_2_, bf16[1024,256]{1,0:T(8,128)(2,1)S(1)} %collective-permute-done.2.refs_3_, ...), custom_call_target="tpu_custom_call" | custom-call | tf_op jit(solution)/shard_map/late_blocks/pallas_call | solution.py:257
  35.6 0.6 collective-permute-done.6.refs_0_
  36.2 0.0 copy-done.2
  36.2 0.0 copy-done.4
  36.2 0.0 copy-done.5
  36.2 4.5 %local_sums.1 = bf16[512,896]{1,0:T(8,128)(2,1)S(1)} custom-call(s32[32]{0:T(128)S(1)} %copy-done.5, f32[1024,512]{1,0:T(8,128)S(1)} %late_blocks.1.acc_ref, bf16[1024,256]{1,0:T(8,128)(2,1)S(1)} %collective-permute-done.6.refs_0_, bf16[1792,256]{1,0:T(8,128)(2,1)S(1)} %get-tuple-element.16.rest_key_ref.refs_1_, ...), custom_call_target="tpu_custom_call" | custom-call | tf_op jit(solution)/shard_map/local_sums/pallas_call | solution.py:265
  40.7 35.4 %all_to_all.23 = bf16[64,8,896]{2,1,0:T(8,128)(2,1)S(1)} all-to-all(bf16[64,8,896]{2,1,0:T(8,128)(2,1)S(1)} %bitcast.15), channel_id=1, replica_groups=mesh['psg'=64,'pb'=4,'rep'=2] {'psg'}, dimensions={0} | all-to-all | bytes 1835008 | tf_op jit(solution)/shard_map/all_to_all | solution.py:286
  76.1 1.2 %final_sums.1 = bf16[512,512]{1,0:T(8,128)(2,1)S(1)} custom-call(s32[9]{0:T(128)S(1)} %stack.39.block_ref, bf16[512,896]{1,0:T(8,128)(2,1)S(1)} %bitcast.14, bf16[512,256]{1,0:T(8,128)(2,1)S(1)} %copy-done.2), custom_call_target="tpu_custom_call" | custom-call | tf_op jit(solution)/shard_map/final_sums/pallas_call | solution.py:287
  77.3 25.2 %all_to_all.24 = bf16[64,8,512]{2,1,0:T(8,128)(2,1)S(1)} all-to-all(bf16[64,8,512]{2,1,0:T(8,128)(2,1)S(1)} %bitcast.21), channel_id=1, replica_groups=mesh['psg'=64,'pb'=4,'rep'=2] {'psg'}, dimensions={0} | all-to-all | bytes 1048576 | tf_op jit(solution)/shard_map/all_to_all | solution.py:295
  102.5 0.8 fusion
  (3 shorter events, 0.0 us)
Async XLA Ops:
  0.6 19.4 %collective-permute-start = (bf16[1024,256]{1,0:T(8,128)(2,1)}, bf16[1024,256]{1,0:T(8,128)(2,1)S(1)}, u32[]{:S(2)}, u32[]{:S(2)}) collective-permute-start(bf16[1024,256]{1,0:T(8,128)(2,1)} %bitcast.16), channel_id=1, source_target_pairs={{0,2},{1,7},{2,4},{3,1},{4,6},{5,3},{6,0},{7,5},{8,10},{9,15},{10,... | collective-permute-start | bytes 1572872 | tf_op jit(solution)/shard_map/ppermute | solution.py:212
  8.5 1.0 %copy-start = (bf16[32,32,256]{2,1,0:T(8,128)(2,1)S(1)}, bf16[32,32,256]{2,1,0:T(8,128)(2,1)}, u32[]{:S(2)}) copy-start(bf16[32,32,256]{2,1,0:T(8,128)(2,1)} %param.7) | copy-start | bytes 1572868
  9.6 1.2 %copy-start.3 = (bf16[2048,256]{1,0:T(8,128)(2,1)S(1)}, bf16[2048,256]{1,0:T(8,128)(2,1)}, u32[]{:S(2)}) copy-start(bf16[2048,256]{1,0:T(8,128)(2,1)} %wk_ref.1) | copy-start | bytes 3145732
  10.8 19.1 %copy-start.1 = (bf16[2048,256]{1,0:T(8,128)(2,1)S(1)}, bf16[2048,256]{1,0:T(8,128)(2,1)}, u32[]{:S(2)}) copy-start(bf16[2048,256]{1,0:T(8,128)(2,1)} %wv_ref.1) | copy-start | bytes 3145732
  11.7 15.8 %collective-permute-start.4 = (bf16[1024,256]{1,0:T(8,128)(2,1)S(1)}, bf16[1024,256]{1,0:T(8,128)(2,1)S(1)}, u32[]{:S(2)}, u32[]{:S(2)}) collective-permute-start(bf16[1024,256]{1,0:T(8,128)(2,1)S(1)} %bitcast.18), channel_id=1, source_target_pairs={{0,6},{1,3},{2,0},{3,5},{4,2},{5,7},{6,4},{7,1},{8,14},{9,11},{10,... | collective-permute-start | bytes 1572872 | tf_op jit(solution)/shard_map/ppermute | solution.py:212
  13.6 16.3 %collective-permute-start.3 = (bf16[1024,256]{1,0:T(8,128)(2,1)S(1)}, bf16[1024,256]{1,0:T(8,128)(2,1)S(1)}, u32[]{:S(2)}, u32[]{:S(2)}) collective-permute-start(bf16[1024,256]{1,0:T(8,128)(2,1)S(1)} %bitcast.19), channel_id=1, source_target_pairs={{0,1},{1,0},{2,3},{3,2},{4,5},{5,4},{6,7},{7,6},{8,9},{9,8},{10,11... | collective-permute-start | bytes 1572872 | tf_op jit(solution)/shard_map/ppermute | solution.py:193
  20.1 12.2 %collective-permute-start.1 = (bf16[1024,256]{1,0:T(8,128)(2,1)S(1)}, bf16[1024,256]{1,0:T(8,128)(2,1)S(1)}, u32[]{:S(2)}, u32[]{:S(2)}) collective-permute-start(bf16[1024,256]{1,0:T(8,128)(2,1)S(1)} %collective-permute-done.refs_1_), channel_id=1, source_target_pairs={{0,2},{1,7},{2,4},{3,1},{4,6},{5,3},{6,0},{7,5},{8,10},{9,15},{10,... | collective-permute-start | bytes 1572872 | tf_op jit(solution)/shard_map/ppermute | solution.py:212
  25.6 6.7 %collective-permute-start.2 = (bf16[1024,256]{1,0:T(8,128)(2,1)S(1)}, bf16[1024,256]{1,0:T(8,128)(2,1)S(1)}, u32[]{:S(2)}, u32[]{:S(2)}) collective-permute-start(bf16[1024,256]{1,0:T(8,128)(2,1)S(1)} %collective-permute-done.refs_1_), channel_id=1, source_target_pairs={{0,1},{1,0},{2,3},{3,2},{4,5},{5,4},{6,7},{7,6},{8,9},{9,8},{10,11... | collective-permute-start | bytes 1572872 | tf_op jit(solution)/shard_map/ppermute | solution.py:193
  27.5 6.8 %collective-permute-start.5 = (bf16[1024,256]{1,0:T(8,128)(2,1)S(1)}, bf16[1024,256]{1,0:T(8,128)(2,1)S(1)}, u32[]{:S(2)}, u32[]{:S(2)}) collective-permute-start(bf16[1024,256]{1,0:T(8,128)(2,1)S(1)} %collective-permute-done.4.refs_4_), channel_id=1, source_target_pairs={{0,1},{1,0},{2,3},{3,2},{4,5},{5,4},{6,7},{7,6},{8,9},{9,8},{10,11... | collective-permute-start | bytes 1572872 | tf_op jit(solution)/shard_map/ppermute | solution.py:193
  32.2 3.9 %copy-start.2 = (bf16[512,256]{1,0:T(8,128)(2,1)S(1)}, bf16[512,256]{1,0:T(8,128)(2,1)}, u32[]{:S(2)}) copy-start(bf16[512,256]{1,0:T(8,128)(2,1)} %c_ref.1) | copy-start | bytes 786436
  32.2 3.9 %copy-start.4 = (bf16[512,256]{1,0:T(8,128)(2,1)S(1)}, bf16[512,256]{1,0:T(8,128)(2,1)}, u32[]{:S(2)}) copy-start(bf16[512,256]{1,0:T(8,128)(2,1)} %refs_3_.1) | copy-start | bytes 786436
  32.2 3.9 %copy-start.5 = (s32[32]{0:T(128)S(1)}, s32[32]{0:T(128)}, u32[]{:S(2)}) copy-start(s32[32]{0:T(128)} %owner_ref.1) | copy-start | bytes 388
  32.3 3.9 %collective-permute-start.6 = (bf16[1024,256]{1,0:T(8,128)(2,1)S(1)}, bf16[1024,256]{1,0:T(8,128)(2,1)S(1)}, u32[]{:S(2)}, u32[]{:S(2)}) collective-permute-start(bf16[1024,256]{1,0:T(8,128)(2,1)S(1)} %collective-permute-done.1.refs_6_), channel_id=1, source_target_pairs={{0,1},{1,0},{2,3},{3,2},{4,5},{5,4},{6,7},{7,6},{8,9},{9,8},{10,11... | collective-permute-start | bytes 1572872 | tf_op jit(solution)/shard_map/ppermute | solution.py:193

commit v11 on v9

--- a/solution.py
+++ b/solution.py
@@ -1,5 +1,6 @@
 import jax
 import jax.numpy as jnp
+import numpy as np
 from jax import lax
 from jax.experimental import pallas as pl
 from jax.experimental.pallas import tpu as pltpu
@@ -10,6 +11,8 @@
 PL = 32
 QUESTIONS = 16
 PARTS = 3
+SIDE = 8
+ROWS_EACH = 8
 
 masked_value = -1e30
 
@@ -51,8 +54,12 @@
     reorder(block_ref, wk_ref, rest_ref, wide)
 
 
-def early_kernel(block_ref, keys_ref, rest_key_ref, x_ref, wv_ref, *refs):
-    x_refs, out_ref, rest_ref = refs[:-2], refs[-2], refs[-1]
+def early_kernel(block_ref, keys_ref, rest_key_ref, x_ref, wv_ref, c_ref, *refs):
+    x_refs, out_ref, rest_ref, own_ref = refs[:-3], refs[-3], refs[-2], refs[-1]
+    place = block_ref[block_ref.shape[0] - 1]
+    count = own_ref.shape[0]
+    pair = c_ref[pl.ds(pl.multiple_of((place >> 1) * 2 * count, 2 * count), 2 * count), :].astype(f32)
+    own_ref[...] = jnp.where((place & 1) == 1, pair[count:], pair[:count])
     wide = x_ref.shape[1]
     cols = wv_ref.shape[1]
     depth = len(x_refs) * wide
@@ -143,44 +150,74 @@
         acc_v[o] = acc_v[o] + jnp.dot(both[:TGT], vblk[slot], preferred_element_type=f32)
         acc_k[o] = acc_k[o] + jnp.dot(both, kblk[slot], preferred_element_type=f32)
 
-    part = lax.broadcasted_iota(jnp.int32, (TGT, keys), 1) % PL
     for q in range(QUESTIONS):
         at = slice(q * TGT, (q + 1) * TGT)
         out_ref[at, 0:cols] = acc_v[q].astype(bf16)
         out_ref[at, cols : 2 * cols] = acc_k[q, TGT:, :].astype(bf16)
         out_ref[at, 2 * cols : 3 * cols] = acc_k[q, :TGT, :].astype(bf16)
-        extra = jnp.zeros((TGT, keys), f32)
-        pieces_of = split_parts(top[q]) + split_parts(total[q]) + split_parts(corr[q])
-        for n, piece in enumerate(pieces_of):
-            extra = jnp.where(part == n, piece, extra)
-        out_ref[at, 3 * cols :] = extra.astype(bf16)
+        out_ref[at, 3 * cols :] = pack((top[q], total[q], corr[q]))
+
+
+def spread(extra, cols):
+    keys = extra.shape[1]
+    heads = keys // PL
+    lane = lax.broadcasted_iota(jnp.int32, (keys, 3 * cols), 0)
+    spot = lax.broadcasted_iota(jnp.int32, (keys, 3 * cols), 1)
+    pick = (lane // PL == (spot % cols) // (cols // heads)) & ((lane % PL) // PARTS == spot // cols)
+    wide = jnp.dot(extra, pick.astype(f32).astype(bf16), preferred_element_type=f32)
+    return [wide[:, n * cols : (n + 1) * cols] for n in range(3)]
+
+
+def pack(values):
+    part = lax.broadcasted_iota(jnp.int32, values[0].shape, 1) % PL
+    out = jnp.zeros_like(values[0])
+    for n, piece in enumerate([piece for value in values for piece in split_parts(value)]):
+        out = jnp.where(part == n, piece, out)
+    return out.astype(bf16)
+
+
+def merge(extra, cols, rows):
+    top, total, corr = [x.reshape(-1, rows, cols) for x in spread(extra, cols)]
+    high = jnp.max(top, axis=0)
+    scale = jnp.exp(top - high[None])
+    sums = jnp.sum(scale * total, axis=0)
+    dots = jnp.sum(scale * total * corr, axis=0)
+    mean = jnp.where(sums > 0.0, dots / jnp.where(sums > 0.0, sums, 1.0), 0.0)
+    return scale, corr, high, sums, mean
+
+
+def merge_kernel(r_ref, out_ref):
+    rows = out_ref.shape[0]
+    keys = r_ref.shape[1] % 256
+    cols = (r_ref.shape[1] - keys) // 3
+    extra = r_ref[:, 3 * cols :]
+
+    def read(n):
+        return r_ref[:, n * cols : (n + 1) * cols].astype(f32).reshape(-1, rows, cols)
+
+    scale, corr, _, _, mean = merge(extra, cols, rows)
+    out_ref[:, 0:cols] = jnp.sum(scale * read(0), axis=0).astype(bf16)
+    low = scale * read(2)
+    grad = jnp.sum(scale * read(1) + (corr - mean[None]) * low, axis=0)
+    out_ref[:, cols : 2 * cols] = grad.astype(bf16)
+    out_ref[:, 2 * cols : 3 * cols] = jnp.sum(low, axis=0).astype(bf16)
+    out_ref[:, 3 * cols :] = pack(merge(extra, keys, rows)[2:])
 
 
 def final_kernel(r_ref, c_ref, out_ref):
     rows, cols = c_ref.shape
-    heads = cols // HDIM
-    keys = heads * PL
-    devices = r_ref.shape[0] // rows
-    lane = lax.broadcasted_iota(jnp.int32, (keys, 3 * cols), 0)
-    spot = lax.broadcasted_iota(jnp.int32, (keys, 3 * cols), 1)
-    pick = (lane // PL == (spot % cols) // HDIM) & ((lane % PL) // PARTS == spot // cols)
-    pick = pick.astype(f32).astype(bf16)
-    wide = jnp.dot(r_ref[:, 3 * cols :], pick, preferred_element_type=f32).reshape(devices, rows, 3 * cols)
-    top = wide[:, :, 0:cols]
-    weight = jnp.exp(top - jnp.max(top, axis=0, keepdims=True))
-    total = jnp.sum(weight * wide[:, :, cols : 2 * cols], axis=0)
+    scale, own, _, total, _ = merge(r_ref[:, 3 * cols :], cols, rows)
 
     def read(n):
-        return r_ref[:, n * cols : (n + 1) * cols].astype(f32).reshape(devices, rows, cols)
-
-    summed = jnp.sum(weight * read(0), axis=0)
+        return r_ref[:, n * cols : (n + 1) * cols].astype(f32).reshape(-1, rows, cols)
+
+    summed = jnp.sum(scale * read(0), axis=0)
     attended = (summed / total).astype(bf16).astype(f32)
     corr = per_head(c_ref[...] * attended, HDIM, jnp.sum, 0.0)
-    shift = wide[:, :, 2 * cols :] - corr[None]
-    grad = jnp.sum(weight * (read(1) + shift * read(2)), axis=0) / total
+    grad = jnp.sum(scale * (read(1) + (own - corr[None]) * read(2)), axis=0) / total
     both = jnp.concatenate([attended, grad], axis=1)
     two = jnp.concatenate([both, both], axis=0).astype(bf16)
-    for n in range(devices // 2):
+    for n in range(out_ref.shape[0] // (2 * rows)):
         out_ref[2 * rows * n : 2 * rows * (n + 1), :] = two
 
 
@@ -195,7 +232,10 @@
     own = [(pb + shift) % n for shift in (0, n - step, n + step, 2)]
     other = [(pb + shift) % n for shift in (0, n + step, n - step, 2)]
     numbers = [number for pair in zip(own, other) for number in (pair[0] * 2 + rep, pair[1] * 2 + 1 - rep)]
-    return jnp.stack(numbers).astype(jnp.int32)
+    place = lax.axis_index("psg")
+    first, second = place // SIDE, place % SIDE
+    row_block = jnp.where(rep == 0, second, first) * SIDE + jnp.where(rep == 0, first, second)
+    return jnp.stack(numbers + [row_block]).astype(jnp.int32)
 
 
 def along(block, way):
@@ -207,13 +247,42 @@
     return lax.ppermute(block, ("pb", "rep"), pairs)
 
 
+AXES = ("psg", "pb", "rep")
+
+
+def line_groups(mesh_shape, turn):
+    side = SIDE
+    assert side * side == mesh_shape[0]
+    ids = np.arange(np.prod(mesh_shape)).reshape((side, side) + tuple(mesh_shape[1:]))
+    groups = []
+    for core in range(mesh_shape[2]):
+        along = (core + turn + 1) % 2
+        lines = np.moveaxis(ids[:, :, :, core], along, -1)
+        groups += lines.reshape(-1, side).tolist()
+    return groups
+
+
+def plane_groups(mesh_shape):
+    ids = np.arange(np.prod(mesh_shape)).reshape((SIDE, SIDE) + tuple(mesh_shape[1:]))
+    groups = []
+    for core in range(mesh_shape[2]):
+        plane = ids[:, :, :, core]
+        plane = np.moveaxis(plane, 2, 0) if core else np.transpose(plane, (2, 1, 0))
+        groups += plane.reshape(mesh_shape[1], -1).tolist()
+    return groups
+
+
+def exchange(x, groups):
+    return lax.all_to_all(x, AXES, 0, 0, axis_index_groups=groups, tiled=True)
+
+
 def body(queries, prefixes, owner, key_weight, value_weight, cotangent):
     slots, vectors, features = prefixes.shape
     rows, cols = queries.shape
     heads = cols // HDIM
     keys = heads * PL
     devices = lax.axis_size("psg")
-    own = rows // devices
+    assert rows == ROWS_EACH * devices
 
     passages = prefixes.reshape(slots * vectors, features)
     smem = pl.BlockSpec(memory_space=pltpu.SMEM)
@@ -238,14 +307,14 @@
     far = along(ahead, 1)
     ahead_other = swap(ahead)
     early = [other, ahead]
-    projected, rest_value = pl.pallas_call(
+    projected, rest_value, own_cotangent = pl.pallas_call(
         early_kernel,
-        out_shape=(sums, rest_rows),
-        in_specs=[smem] + [vmem] * (4 + len(early)),
-        out_specs=(vmem, vmem),
+        out_shape=(sums, rest_rows, jax.ShapeDtypeStruct((ROWS_EACH, cols), f32)),
+        in_specs=[smem] + [vmem] * (5 + len(early)),
+        out_specs=(vmem, vmem, vmem),
         compiler_params=small,
         name="early_blocks",
-    )(block, keys_sum, rest_key, held, value_weight, *early)
+    )(block, keys_sum, rest_key, held, value_weight, cotangent, *early)
     far, ahead_other, projected, rest_value = lax.optimization_barrier((far, ahead_other, projected, rest_value))
     late = [ahead_other, behind, swap(behind), far]
     far = swap(far)
@@ -278,8 +347,17 @@
         name="local_sums",
     )(owner, projected, far, rest_key, rest_value, queries, cotangent)
 
-    received = lax.all_to_all(payload, "psg", 0, 0, tiled=True)
-    own_cotangent = lax.dynamic_slice_in_dim(cotangent, lax.axis_index("psg") * own, own, 0).astype(f32)
+    shape = tuple(lax.axis_size(name) for name in AXES)
+    first_lines, second_lines = line_groups(shape, 0), line_groups(shape, 1)
+    merged = pl.pallas_call(
+        merge_kernel,
+        out_shape=jax.ShapeDtypeStruct((rows // SIDE, payload.shape[1]), bf16),
+        in_specs=[vmem],
+        out_specs=vmem,
+        compiler_params=pltpu.CompilerParams(vmem_limit_bytes=24 * 1024 * 1024),
+        name="line_sums",
+    )(exchange(payload, first_lines))
+    received = exchange(merged, second_lines)
     finished = pl.pallas_call(
         final_kernel,
         out_shape=jax.ShapeDtypeStruct((rows, 2 * cols), bf16),
@@ -288,7 +366,7 @@
         compiler_params=pltpu.CompilerParams(vmem_limit_bytes=24 * 1024 * 1024),
         name="final_sums",
     )(received, own_cotangent)
-    outputs = lax.all_to_all(finished, "psg", 0, 0, tiled=True)
+    outputs = exchange(finished, plane_groups(shape))
     return outputs[:, :cols], outputs[:, cols:]
 
 

time: 105 us -> 101 us (0.962)
  blocking collectives: 25.2 us -> 56.3 us
  waiting for transfers between devices: 33.1 us -> 5.13 us
  starting transfers between devices: 31.9 us -> 23.5 us
    all_to_all x1 -> x3, blocking collectives: 25.2 us -> 56.3 us  [exchange(): return lax.all_to_all(x, AXES, 0, 0, axis_index_groups=groups, tiled=True)]
    all_to_all x1 -> x0, waiting for transfers between devices: 27.1 us -> none  [body(): received = lax.all_to_all(payload, 'psg', 0, 0, tiled=True)]
    all_to_all x1 -> x0, starting transfers between devices: 8.48 us -> none  [body(): received = lax.all_to_all(payload, 'psg', 0, 0, tiled=True)]
    unnamed x12 -> x14, local copies, waits for them, and re-layouts: 2.28 us -> 3.24 us
    pallas_call x1 -> x2, Pallas kernels: 1.43 us -> 2.17 us  [the longest x1 1.43 us: body(): pl.pallas_call(early_kernel, out_shape=(sums, rest_rows, jax.ShapeDtypeSt...]
  transfers between devices with their start and end apart: 8 -> 7, of which waited for: 4 -> 2; matrix products, arithmetic and copies ran while one was open for 0% -> 0% of each run, Pallas kernels for 3% -> 4%
where the time goes in v11:
time: 101 us; the launch traced here: 99.1 us
  blocking collectives  56.3 us (56%)
  starting transfers between devices  23.5 us (23%)
  Pallas kernels  9.12 us (9%)
  waiting for transfers between devices  5.13 us (5%)
  local copies, waits for them, and re-layouts  4.15 us (4%)
    all_to_all x3, blocking collectives, exchange(): return lax.all_to_all(x, AXES, 0, 0, axis_index_groups=groups, tiled=True)  56.3 us
    ppermute x3, starting transfers between devices, along(): return lax.ppermute(block, ('pb', 'rep'), pairs)  15.2 us
    ppermute x4, starting transfers between devices, swap(): return lax.ppermute(block, 'rep', [(0, 1), (1, 0)])  8.3 us
    ppermute x3, waiting for transfers between devices, along(): return lax.ppermute(block, ('pb', 'rep'), pairs)  4.52 us
    pallas_call x1, Pallas kernels, body(): pl.pallas_call(local_kernel, out_shape=jax.ShapeDtypeStruct((rows, 3 * co...  4.52 us
    unnamed x14, local copies, waits for them, and re-layouts  3.24 us
  transfers between devices with their start and end apart: 7, of which 2 were waited for; matrix products, arithmetic and copies ran while one was open for 0% of the time, Pallas kernels for 4%

profile of v11, /device:TPU:6, one launch (start us, length us, event | category | flops | bytes accessed | tf_op | source)
XLA Modules:
  0.0 99.1 jit_solution(11249306672863880804)
XLA Ops:
  0.6 7.8 %collective-permute-start = (bf16[1024,256]{1,0:T(8,128)(2,1)}, bf16[1024,256]{1,0:T(8,128)(2,1)S(1)}, u32[]{:S(2)}, u32[]{:S(2)}) collective-permute-start(bf16[1024,256]{1,0:T(8,128)(2,1)} %bitcast.18), channel_id=1, source_target_pairs={{0,2},{1,7},{2,4},{3,1},{4,6},{5,3},{6,0},{7,5},{8,10},{9,15},{10,... | collective-permute-start | bytes 1572872 | tf_op jit(solution)/shard_map/ppermute | solution.py:247
  8.5 0.1 stack.39.block_ref
  8.6 1.0 %copy-done = bf16[32,32,256]{2,1,0:T(8,128)(2,1)S(1)} copy-done((bf16[32,32,256]{2,1,0:T(8,128)(2,1)S(1)}, bf16[32,32,256]{2,1,0:T(8,128)(2,1)}, u32[]{:S(2)}) %copy-start) | copy-done | bytes 524312
  9.6 1.2 %copy-done.4 = bf16[2048,256]{1,0:T(8,128)(2,1)S(1)} copy-done((bf16[2048,256]{1,0:T(8,128)(2,1)S(1)}, bf16[2048,256]{1,0:T(8,128)(2,1)}, u32[]{:S(2)}) %copy-start.4) | copy-done | bytes 1048600
  10.8 0.8 own_keys.1
  11.7 1.9 %collective-permute-start.4 = (bf16[1024,256]{1,0:T(8,128)(2,1)S(1)}, bf16[1024,256]{1,0:T(8,128)(2,1)S(1)}, u32[]{:S(2)}, u32[]{:S(2)}) collective-permute-start(bf16[1024,256]{1,0:T(8,128)(2,1)S(1)} %bitcast.20), channel_id=1, source_target_pairs={{0,6},{1,3},{2,0},{3,5},{4,2},{5,7},{6,4},{7,1},{8,14},{9,11},{10,... | collective-permute-start | bytes 1572872 | tf_op jit(solution)/shard_map/ppermute | solution.py:247
  13.6 1.9 %collective-permute-start.3 = (bf16[1024,256]{1,0:T(8,128)(2,1)S(1)}, bf16[1024,256]{1,0:T(8,128)(2,1)S(1)}, u32[]{:S(2)}, u32[]{:S(2)}) collective-permute-start(bf16[1024,256]{1,0:T(8,128)(2,1)S(1)} %bitcast.21), channel_id=1, source_target_pairs={{0,1},{1,0},{2,3},{3,2},{4,5},{5,4},{6,7},{7,6},{8,9},{9,8},{10,11... | collective-permute-start | bytes 1572872 | tf_op jit(solution)/shard_map/ppermute | solution.py:225
  15.5 4.5 %collective-permute-done.refs_1_ = bf16[1024,256]{1,0:T(8,128)(2,1)S(1)} collective-permute-done((bf16[1024,256]{1,0:T(8,128)(2,1)}, bf16[1024,256]{1,0:T(8,128)(2,1)S(1)}, u32[]{:S(2)}, u32[]{:S(2)}) %collective-permute-start) | collective-permute-done | bytes 524320 | tf_op jit(solution)/shard_map/ppermute | solution.py:247
  20.1 5.5 %collective-permute-start.1 = (bf16[1024,256]{1,0:T(8,128)(2,1)S(1)}, bf16[1024,256]{1,0:T(8,128)(2,1)S(1)}, u32[]{:S(2)}, u32[]{:S(2)}) collective-permute-start(bf16[1024,256]{1,0:T(8,128)(2,1)S(1)} %collective-permute-done.refs_1_), channel_id=1, source_target_pairs={{0,2},{1,7},{2,4},{3,1},{4,6},{5,3},{6,0},{7,5},{8,10},{9,15},{10,... | collective-permute-start | bytes 1572872 | tf_op jit(solution)/shard_map/ppermute | solution.py:247
  25.5 1.9 %collective-permute-start.2 = (bf16[1024,256]{1,0:T(8,128)(2,1)S(1)}, bf16[1024,256]{1,0:T(8,128)(2,1)S(1)}, u32[]{:S(2)}, u32[]{:S(2)}) collective-permute-start(bf16[1024,256]{1,0:T(8,128)(2,1)S(1)} %collective-permute-done.refs_1_), channel_id=1, source_target_pairs={{0,1},{1,0},{2,3},{3,2},{4,5},{5,4},{6,7},{7,6},{8,9},{9,8},{10,11... | collective-permute-start | bytes 1572872 | tf_op jit(solution)/shard_map/ppermute | solution.py:225
  27.5 0.0 collective-permute-done.4.refs_4_
  27.5 2.4 %collective-permute-start.5 = (bf16[1024,256]{1,0:T(8,128)(2,1)S(1)}, bf16[1024,256]{1,0:T(8,128)(2,1)S(1)}, u32[]{:S(2)}, u32[]{:S(2)}) collective-permute-start(bf16[1024,256]{1,0:T(8,128)(2,1)S(1)} %collective-permute-done.4.refs_4_), channel_id=1, source_target_pairs={{0,1},{1,0},{2,3},{3,2},{4,5},{5,4},{6,7},{7,6},{8,9},{9,8},{10,11... | collective-permute-start | bytes 1572872 | tf_op jit(solution)/shard_map/ppermute | solution.py:225
  29.9 0.0 collective-permute-done.3.refs_0_
  29.9 0.0 copy-start.2
  29.9 0.9 copy-done.2
  30.9 1.4 %early_blocks.1 = (f32[1024,512]{1,0:T(8,128)S(1)}, bf16[1792,256]{1,0:T(8,128)(2,1)S(1)}, f32[8,256]{1,0:T(8,128)S(1)}) custom-call(s32[9]{0:T(128)S(1)} %stack.39.block_ref, f32[1024,256]{1,0:T(8,128)S(1)} %get-tuple-element.16.keys_ref, bf16[1792,256]{1,0:T(8,128)(2,1)S(1)} %get-tuple-element.17.rest_key_ref.refs_1_, bf16[1024,256]{1,0:T(8,128)(2,1)S(1)} %bitcast.22, ...), custom_call_target="tpu_custom_call" | custom-call | tf_op jit(solution)/shard_map/early_blocks/pallas_call | solution.py:310
  32.3 0.0 collective-permute-done.1.refs_6_
  32.3 0.0 collective-permute-done.2.refs_3_
  32.3 0.0 copy-start.3
  32.3 0.0 copy-start.5
  32.4 0.0 copy-start.6
  32.4 2.1 %collective-permute-start.6 = (bf16[1024,256]{1,0:T(8,128)(2,1)S(1)}, bf16[1024,256]{1,0:T(8,128)(2,1)S(1)}, u32[]{:S(2)}, u32[]{:S(2)}) collective-permute-start(bf16[1024,256]{1,0:T(8,128)(2,1)S(1)} %collective-permute-done.1.refs_6_), channel_id=1, source_target_pairs={{0,1},{1,0},{2,3},{3,2},{4,5},{5,4},{6,7},{7,6},{8,9},{9,8},{10,11... | collective-permute-start | bytes 1572872 | tf_op jit(solution)/shard_map/ppermute | solution.py:225
  34.4 0.0 collective-permute-done.5.refs_5_
  34.4 1.3 %late_blocks.1.acc_ref = f32[1024,512]{1,0:T(8,128)S(1)} custom-call(f32[1024,512]{1,0:T(8,128)S(1)} %get-tuple-element.21.refs_0_, bf16[1792,256]{1,0:T(8,128)(2,1)S(1)} %get-tuple-element.17.rest_key_ref.refs_1_, bf16[1792,256]{1,0:T(8,128)(2,1)S(1)} %get-tuple-element.22.refs_2_, bf16[1024,256]{1,0:T(8,128)(2,1)S(1)} %collective-permute-done.2.refs_3_, ...), custom_call_target="tpu_custom_call" | custom-call | tf_op jit(solution)/shard_map/late_blocks/pallas_call | solution.py:321
  35.7 0.6 collective-permute-done.6.refs_0_
  36.3 4.5 %local_sums.1 = bf16[512,896]{1,0:T(8,128)(2,1)S(1)} custom-call(s32[32]{0:T(128)S(1)} %copy-done.6, f32[1024,512]{1,0:T(8,128)S(1)} %late_blocks.1.acc_ref, bf16[1024,256]{1,0:T(8,128)(2,1)S(1)} %collective-permute-done.6.refs_0_, bf16[1792,256]{1,0:T(8,128)(2,1)S(1)} %get-tuple-element.17.rest_key_ref.refs_1_, ...), custom_call_target="tpu_custom_call" | custom-call | tf_op jit(solution)/shard_map/local_sums/pallas_call | solution.py:329
  40.8 19.9 %all_to_all.34 = bf16[8,64,896]{2,1,0:T(8,128)(2,1)S(1)} all-to-all(bf16[8,64,896]{2,1,0:T(8,128)(2,1)S(1)} %bitcast.17), channel_id=1, replica_groups={{0,8,16,24,32,40,48,56},{2,10,18,26,34,42,50,58},{4,12,20,28,36,44,52,6..., dimensions={0} | all-to-all | bytes 1835008 | tf_op jit(solution)/shard_map/all_to_all | solution.py:276
  60.7 0.7 line_sums.1
  61.5 15.3 %all_to_all.35 = bf16[8,8,896]{2,1,0:T(8,128)(2,1)S(1)} all-to-all(bf16[8,8,896]{2,1,0:T(8,128)(2,1)S(1)} %bitcast.25), channel_id=1, replica_groups={{0,64,128,192,256,320,384,448},{2,66,130,194,258,322,386,450},{4,68,132..., dimensions={0} | all-to-all | bytes 229376 | tf_op jit(solution)/shard_map/all_to_all | solution.py:276
  76.8 0.3 final_sums.1
  77.1 21.1 %all_to_all.36 = bf16[64,8,512]{2,1,0:T(8,128)(2,1)S(1)} all-to-all(bf16[64,8,512]{2,1,0:T(8,128)(2,1)S(1)} %bitcast.23), channel_id=1, replica_groups={{0,64,128,192,256,320,384,448,8,72,136,200,264,328,392,456,16,80,144,20..., dimensions={0} | all-to-all | bytes 1048576 | tf_op jit(solution)/shard_map/all_to_all | solution.py:276
  98.3 0.8 fusion
  (7 shorter events, 0.0 us)
Async XLA Ops:
  0.6 19.4 %collective-permute-start = (bf16[1024,256]{1,0:T(8,128)(2,1)}, bf16[1024,256]{1,0:T(8,128)(2,1)S(1)}, u32[]{:S(2)}, u32[]{:S(2)}) collective-permute-start(bf16[1024,256]{1,0:T(8,128)(2,1)} %bitcast.18), channel_id=1, source_target_pairs={{0,2},{1,7},{2,4},{3,1},{4,6},{5,3},{6,0},{7,5},{8,10},{9,15},{10,... | collective-permute-start | bytes 1572872 | tf_op jit(solution)/shard_map/ppermute | solution.py:247
  8.6 1.0 %copy-start = (bf16[32,32,256]{2,1,0:T(8,128)(2,1)S(1)}, bf16[32,32,256]{2,1,0:T(8,128)(2,1)}, u32[]{:S(2)}) copy-start(bf16[32,32,256]{2,1,0:T(8,128)(2,1)} %param.7) | copy-start | bytes 1572868
  9.6 1.2 %copy-start.4 = (bf16[2048,256]{1,0:T(8,128)(2,1)S(1)}, bf16[2048,256]{1,0:T(8,128)(2,1)}, u32[]{:S(2)}) copy-start(bf16[2048,256]{1,0:T(8,128)(2,1)} %wk_ref.1) | copy-start | bytes 3145732
  10.8 19.1 %copy-start.1 = (bf16[2048,256]{1,0:T(8,128)(2,1)S(1)}, bf16[2048,256]{1,0:T(8,128)(2,1)}, u32[]{:S(2)}) copy-start(bf16[2048,256]{1,0:T(8,128)(2,1)} %wv_ref.1) | copy-start | bytes 3145732
  11.7 15.8 %collective-permute-start.4 = (bf16[1024,256]{1,0:T(8,128)(2,1)S(1)}, bf16[1024,256]{1,0:T(8,128)(2,1)S(1)}, u32[]{:S(2)}, u32[]{:S(2)}) collective-permute-start(bf16[1024,256]{1,0:T(8,128)(2,1)S(1)} %bitcast.20), channel_id=1, source_target_pairs={{0,6},{1,3},{2,0},{3,5},{4,2},{5,7},{6,4},{7,1},{8,14},{9,11},{10,... | collective-permute-start | bytes 1572872 | tf_op jit(solution)/shard_map/ppermute | solution.py:247
  13.6 16.3 %collective-permute-start.3 = (bf16[1024,256]{1,0:T(8,128)(2,1)S(1)}, bf16[1024,256]{1,0:T(8,128)(2,1)S(1)}, u32[]{:S(2)}, u32[]{:S(2)}) collective-permute-start(bf16[1024,256]{1,0:T(8,128)(2,1)S(1)} %bitcast.21), channel_id=1, source_target_pairs={{0,1},{1,0},{2,3},{3,2},{4,5},{5,4},{6,7},{7,6},{8,9},{9,8},{10,11... | collective-permute-start | bytes 1572872 | tf_op jit(solution)/shard_map/ppermute | solution.py:225
  20.1 12.3 %collective-permute-start.1 = (bf16[1024,256]{1,0:T(8,128)(2,1)S(1)}, bf16[1024,256]{1,0:T(8,128)(2,1)S(1)}, u32[]{:S(2)}, u32[]{:S(2)}) collective-permute-start(bf16[1024,256]{1,0:T(8,128)(2,1)S(1)} %collective-permute-done.refs_1_), channel_id=1, source_target_pairs={{0,2},{1,7},{2,4},{3,1},{4,6},{5,3},{6,0},{7,5},{8,10},{9,15},{10,... | collective-permute-start | bytes 1572872 | tf_op jit(solution)/shard_map/ppermute | solution.py:247
  25.5 6.8 %collective-permute-start.2 = (bf16[1024,256]{1,0:T(8,128)(2,1)S(1)}, bf16[1024,256]{1,0:T(8,128)(2,1)S(1)}, u32[]{:S(2)}, u32[]{:S(2)}) collective-permute-start(bf16[1024,256]{1,0:T(8,128)(2,1)S(1)} %collective-permute-done.refs_1_), channel_id=1, source_target_pairs={{0,1},{1,0},{2,3},{3,2},{4,5},{5,4},{6,7},{7,6},{8,9},{9,8},{10,11... | collective-permute-start | bytes 1572872 | tf_op jit(solution)/shard_map/ppermute | solution.py:225
  27.5 6.9 %collective-permute-start.5 = (bf16[1024,256]{1,0:T(8,128)(2,1)S(1)}, bf16[1024,256]{1,0:T(8,128)(2,1)S(1)}, u32[]{:S(2)}, u32[]{:S(2)}) collective-permute-start(bf16[1024,256]{1,0:T(8,128)(2,1)S(1)} %collective-permute-done.4.refs_4_), channel_id=1, source_target_pairs={{0,1},{1,0},{2,3},{3,2},{4,5},{5,4},{6,7},{7,6},{8,9},{9,8},{10,11... | collective-permute-start | bytes 1572872 | tf_op jit(solution)/shard_map/ppermute | solution.py:225
  29.9 1.0 copy-start.2
  32.3 4.0 %copy-start.3 = (bf16[512,256]{1,0:T(8,128)(2,1)S(1)}, bf16[512,256]{1,0:T(8,128)(2,1)}, u32[]{:S(2)}) copy-start(bf16[512,256]{1,0:T(8,128)(2,1)} %refs_4_.1) | copy-start | bytes 786436
  32.3 4.0 %copy-start.5 = (bf16[512,256]{1,0:T(8,128)(2,1)S(1)}, bf16[512,256]{1,0:T(8,128)(2,1)}, u32[]{:S(2)}) copy-start(bf16[512,256]{1,0:T(8,128)(2,1)} %refs_3_.1) | copy-start | bytes 786436
  32.4 4.0 %copy-start.6 = (s32[32]{0:T(128)S(1)}, s32[32]{0:T(128)}, u32[]{:S(2)}) copy-start(s32[32]{0:T(128)} %owner_ref.1) | copy-start | bytes 388
  32.4 3.9 %collective-permute-start.6 = (bf16[1024,256]{1,0:T(8,128)(2,1)S(1)}, bf16[1024,256]{1,0:T(8,128)(2,1)S(1)}, u32[]{:S(2)}, u32[]{:S(2)}) collective-permute-start(bf16[1024,256]{1,0:T(8,128)(2,1)S(1)} %collective-permute-done.1.refs_6_), channel_id=1, source_target_pairs={{0,1},{1,0},{2,3},{3,2},{4,5},{5,4},{6,7},{7,6},{8,9},{9,8},{10,11... | collective-permute-start | bytes 1572872 | tf_op jit(solution)/shard_map/ppermute | solution.py:225

commit v12 on v11

--- a/solution.py
+++ b/solution.py
@@ -12,6 +12,9 @@
 QUESTIONS = 16
 PARTS = 3
 SIDE = 8
+LANES = 8
+PACKED = 16
+CHUNK = 400
 ROWS_EACH = 8
 
 masked_value = -1e30
@@ -21,12 +24,17 @@
 NT = (((1,), (1,)), ((), ()))
 
 
-def split_parts(x):
-    first = x.astype(bf16)
-    rest = x - first.astype(f32)
-    second = rest.astype(bf16)
-    third = (rest - second.astype(f32)).astype(bf16)
-    return first.astype(f32), second.astype(f32), third.astype(f32)
+def split_parts(x, count=PARTS):
+    parts = []
+    for _ in range(count):
+        parts.append(x.astype(bf16).astype(f32))
+        x = x - parts[-1]
+    return parts
+
+
+def two_parts(x):
+    first, second = split_parts(x, 2)
+    return first + second
 
 
 def per_head(x, width, reduce, fill):
@@ -139,7 +147,7 @@
         t = per_head(total[q], PL, jnp.sum, 0.0)
         d = per_head(dots[q], PL, jnp.sum, 0.0)
         total[q] = t
-        corr[q] = jnp.where(t > 0.0, d / jnp.where(t > 0.0, t, 1.0), 0.0)
+        corr[q] = two_parts(jnp.where(t > 0.0, d / jnp.where(t > 0.0, t, 1.0), 0.0))
     corr[QUESTIONS] = jnp.zeros_like(corr[QUESTIONS])
 
     for slot in range(slots):
@@ -150,12 +158,21 @@
         acc_v[o] = acc_v[o] + jnp.dot(both[:TGT], vblk[slot], preferred_element_type=f32)
         acc_k[o] = acc_k[o] + jnp.dot(both, kblk[slot], preferred_element_type=f32)
 
-    for q in range(QUESTIONS):
-        at = slice(q * TGT, (q + 1) * TGT)
-        out_ref[at, 0:cols] = acc_v[q].astype(bf16)
-        out_ref[at, cols : 2 * cols] = acc_k[q, TGT:, :].astype(bf16)
-        out_ref[at, 2 * cols : 3 * cols] = acc_k[q, :TGT, :].astype(bf16)
-        out_ref[at, 3 * cols :] = pack((top[q], total[q], corr[q]))
+    segment = lax.broadcasted_iota(jnp.int32, (PACKED, keys), 1) % PL
+    for block in range(QUESTIONS // 2):
+        extras = []
+        for side in range(2):
+            q = 2 * block + side
+            sums = jnp.concatenate([acc_v[q], acc_k[q, TGT:, :], acc_k[q, :TGT, :]], axis=1).astype(bf16)
+            for n in range(sums.shape[1] // keys):
+                low = block * CHUNK + (2 * n + side) * TGT
+                out_ref[low : low + TGT, :] = sums[:, n * keys : (n + 1) * keys]
+            extras.append(pack(top[q], total[q], corr[q]))
+        quarters = [extra[low : low + PACKED] for extra in extras for low in range(0, TGT, PACKED)]
+        packed = quarters[0]
+        for n in range(1, len(quarters)):
+            packed = jnp.where(segment // LANES == n, pltpu.roll(quarters[n], n * LANES, 1), packed)
+        out_ref[(block + 1) * CHUNK - PACKED : (block + 1) * CHUNK, :] = packed.astype(bf16)
 
 
 def spread(extra, cols):
@@ -164,16 +181,17 @@
     lane = lax.broadcasted_iota(jnp.int32, (keys, 3 * cols), 0)
     spot = lax.broadcasted_iota(jnp.int32, (keys, 3 * cols), 1)
     pick = (lane // PL == (spot % cols) // (cols // heads)) & ((lane % PL) // PARTS == spot // cols)
+    pick = pick & (lane % PL < LANES)
     wide = jnp.dot(extra, pick.astype(f32).astype(bf16), preferred_element_type=f32)
     return [wide[:, n * cols : (n + 1) * cols] for n in range(3)]
 
 
-def pack(values):
-    part = lax.broadcasted_iota(jnp.int32, values[0].shape, 1) % PL
-    out = jnp.zeros_like(values[0])
-    for n, piece in enumerate([piece for value in values for piece in split_parts(value)]):
+def pack(top, total, corr):
+    part = lax.broadcasted_iota(jnp.int32, top.shape, 1) % PL
+    out = jnp.zeros_like(top)
+    for n, piece in enumerate(split_parts(top) + split_parts(total) + split_parts(corr, 2)):
         out = jnp.where(part == n, piece, out)
-    return out.astype(bf16)
+    return out
 
 
 def merge(extra, cols, rows):
@@ -182,18 +200,29 @@
     scale = jnp.exp(top - high[None])
     sums = jnp.sum(scale * total, axis=0)
     dots = jnp.sum(scale * total * corr, axis=0)
-    mean = jnp.where(sums > 0.0, dots / jnp.where(sums > 0.0, sums, 1.0), 0.0)
+    mean = two_parts(jnp.where(sums > 0.0, dots / jnp.where(sums > 0.0, sums, 1.0), 0.0))
     return scale, corr, high, sums, mean
 
 
 def merge_kernel(r_ref, out_ref):
     rows = out_ref.shape[0]
-    keys = r_ref.shape[1] % 256
-    cols = (r_ref.shape[1] - keys) // 3
-    extra = r_ref[:, 3 * cols :]
+    keys = r_ref.shape[1]
+    cols = (out_ref.shape[1] - keys) // 3
+    starts = range(0, r_ref.shape[0], CHUNK)
+    extras = []
+    for start in starts:
+        packed = r_ref[start + CHUNK - PACKED : start + CHUNK, :]
+        extras.append(packed)
+        for n in range(1, rows // PACKED):
+            extras.append(pltpu.roll(packed.astype(f32), keys - n * LANES, 1).astype(bf16))
+    extra = jnp.concatenate(extras, axis=0)
 
     def read(n):
-        return r_ref[:, n * cols : (n + 1) * cols].astype(f32).reshape(-1, rows, cols)
+        each = []
+        for start in starts:
+            lows = [start + (n * cols // keys + part) * rows for part in range(cols // keys)]
+            each.append(jnp.concatenate([r_ref[low : low + rows, :].astype(f32) for low in lows], axis=1))
+        return jnp.stack(each)
 
     scale, corr, _, _, mean = merge(extra, cols, rows)
     out_ref[:, 0:cols] = jnp.sum(scale * read(0), axis=0).astype(bf16)
@@ -201,7 +230,7 @@
     grad = jnp.sum(scale * read(1) + (corr - mean[None]) * low, axis=0)
     out_ref[:, cols : 2 * cols] = grad.astype(bf16)
     out_ref[:, 2 * cols : 3 * cols] = jnp.sum(low, axis=0).astype(bf16)
-    out_ref[:, 3 * cols :] = pack(merge(extra, keys, rows)[2:])
+    out_ref[:, 3 * cols :] = pack(*merge(extra, keys, rows)[2:]).astype(bf16)
 
 
 def final_kernel(r_ref, c_ref, out_ref):
@@ -328,7 +357,7 @@
     )(projected, rest_key, rest_value, *late)
     payload = pl.pallas_call(
         local_kernel,
-        out_shape=jax.ShapeDtypeStruct((rows, 3 * cols + keys), bf16),
+        out_shape=jax.ShapeDtypeStruct((SIDE * CHUNK, keys), bf16),
         in_specs=[smem] + [vmem] * 6,
         out_specs=vmem,
         scratch_shapes=[
@@ -351,7 +380,7 @@
     first_lines, second_lines = line_groups(shape, 0), line_groups(shape, 1)
     merged = pl.pallas_call(
         merge_kernel,
-        out_shape=jax.ShapeDtypeStruct((rows // SIDE, payload.shape[1]), bf16),
+        out_shape=jax.ShapeDtypeStruct((rows // SIDE, 3 * cols + keys), bf16),
         in_specs=[vmem],
         out_specs=vmem,
         compiler_params=pltpu.CompilerParams(vmem_limit_bytes=24 * 1024 * 1024),

time: 101 us -> 99.6 us (0.986)
    all_to_all x3, blocking collectives: 56.3 us -> 55.3 us  [exchange(): return lax.all_to_all(x, AXES, 0, 0, axis_index_groups=groups, tiled=True)]
where the time goes in v12:
time: 99.6 us; the launch traced here: 98.1 us
  blocking collectives  55.3 us (56%)
  starting transfers between devices  23.5 us (24%)
  Pallas kernels  9.19 us (9%)
  waiting for transfers between devices  5.13 us (5%)
  local copies, waits for them, and re-layouts  4.15 us (4%)
    all_to_all x3, blocking collectives, exchange(): return lax.all_to_all(x, AXES, 0, 0, axis_index_groups=groups, tiled=True)  55.3 us
    ppermute x3, starting transfers between devices, along(): return lax.ppermute(block, ('pb', 'rep'), pairs)  15.2 us
    ppermute x4, starting transfers between devices, swap(): return lax.ppermute(block, 'rep', [(0, 1), (1, 0)])  8.3 us
    pallas_call x1, Pallas kernels, body(): pl.pallas_call(local_kernel, out_shape=jax.ShapeDtypeStruct((SIDE * CHUNK...  4.57 us
    ppermute x3, waiting for transfers between devices, along(): return lax.ppermute(block, ('pb', 'rep'), pairs)  4.52 us
    unnamed x14, local copies, waits for them, and re-layouts  3.24 us
  transfers between devices with their start and end apart: 7, of which 2 were waited for; matrix products, arithmetic and copies ran while one was open for 0% of the time, Pallas kernels for 4%

profile of v12, /device:TPU:6, one launch (start us, length us, event | category | flops | bytes accessed | tf_op | source)
XLA Modules:
  0.0 98.1 jit_solution(14692738875116932005)
XLA Ops:
  0.6 7.8 %collective-permute-start = (bf16[1024,256]{1,0:T(8,128)(2,1)}, bf16[1024,256]{1,0:T(8,128)(2,1)S(1)}, u32[]{:S(2)}, u32[]{:S(2)}) collective-permute-start(bf16[1024,256]{1,0:T(8,128)(2,1)} %bitcast.18), channel_id=1, source_target_pairs={{0,2},{1,7},{2,4},{3,1},{4,6},{5,3},{6,0},{7,5},{8,10},{9,15},{10,... | collective-permute-start | bytes 1572872 | tf_op jit(solution)/shard_map/ppermute | solution.py:276
  8.5 0.1 stack.39.block_ref
  8.6 1.0 %copy-done = bf16[32,32,256]{2,1,0:T(8,128)(2,1)S(1)} copy-done((bf16[32,32,256]{2,1,0:T(8,128)(2,1)S(1)}, bf16[32,32,256]{2,1,0:T(8,128)(2,1)}, u32[]{:S(2)}) %copy-start) | copy-done | bytes 524312
  9.6 1.2 %copy-done.4 = bf16[2048,256]{1,0:T(8,128)(2,1)S(1)} copy-done((bf16[2048,256]{1,0:T(8,128)(2,1)S(1)}, bf16[2048,256]{1,0:T(8,128)(2,1)}, u32[]{:S(2)}) %copy-start.4) | copy-done | bytes 1048600
  10.8 0.8 own_keys.1
  11.7 1.9 %collective-permute-start.4 = (bf16[1024,256]{1,0:T(8,128)(2,1)S(1)}, bf16[1024,256]{1,0:T(8,128)(2,1)S(1)}, u32[]{:S(2)}, u32[]{:S(2)}) collective-permute-start(bf16[1024,256]{1,0:T(8,128)(2,1)S(1)} %bitcast.20), channel_id=1, source_target_pairs={{0,6},{1,3},{2,0},{3,5},{4,2},{5,7},{6,4},{7,1},{8,14},{9,11},{10,... | collective-permute-start | bytes 1572872 | tf_op jit(solution)/shard_map/ppermute | solution.py:276
  13.6 1.9 %collective-permute-start.3 = (bf16[1024,256]{1,0:T(8,128)(2,1)S(1)}, bf16[1024,256]{1,0:T(8,128)(2,1)S(1)}, u32[]{:S(2)}, u32[]{:S(2)}) collective-permute-start(bf16[1024,256]{1,0:T(8,128)(2,1)S(1)} %bitcast.21), channel_id=1, source_target_pairs={{0,1},{1,0},{2,3},{3,2},{4,5},{5,4},{6,7},{7,6},{8,9},{9,8},{10,11... | collective-permute-start | bytes 1572872 | tf_op jit(solution)/shard_map/ppermute | solution.py:254
  15.5 4.5 %collective-permute-done.refs_1_ = bf16[1024,256]{1,0:T(8,128)(2,1)S(1)} collective-permute-done((bf16[1024,256]{1,0:T(8,128)(2,1)}, bf16[1024,256]{1,0:T(8,128)(2,1)S(1)}, u32[]{:S(2)}, u32[]{:S(2)}) %collective-permute-start) | collective-permute-done | bytes 524320 | tf_op jit(solution)/shard_map/ppermute | solution.py:276
  20.1 5.5 %collective-permute-start.1 = (bf16[1024,256]{1,0:T(8,128)(2,1)S(1)}, bf16[1024,256]{1,0:T(8,128)(2,1)S(1)}, u32[]{:S(2)}, u32[]{:S(2)}) collective-permute-start(bf16[1024,256]{1,0:T(8,128)(2,1)S(1)} %collective-permute-done.refs_1_), channel_id=1, source_target_pairs={{0,2},{1,7},{2,4},{3,1},{4,6},{5,3},{6,0},{7,5},{8,10},{9,15},{10,... | collective-permute-start | bytes 1572872 | tf_op jit(solution)/shard_map/ppermute | solution.py:276
  25.5 1.9 %collective-permute-start.2 = (bf16[1024,256]{1,0:T(8,128)(2,1)S(1)}, bf16[1024,256]{1,0:T(8,128)(2,1)S(1)}, u32[]{:S(2)}, u32[]{:S(2)}) collective-permute-start(bf16[1024,256]{1,0:T(8,128)(2,1)S(1)} %collective-permute-done.refs_1_), channel_id=1, source_target_pairs={{0,1},{1,0},{2,3},{3,2},{4,5},{5,4},{6,7},{7,6},{8,9},{9,8},{10,11... | collective-permute-start | bytes 1572872 | tf_op jit(solution)/shard_map/ppermute | solution.py:254
  27.5 0.0 collective-permute-done.4.refs_4_
  27.5 2.4 %collective-permute-start.5 = (bf16[1024,256]{1,0:T(8,128)(2,1)S(1)}, bf16[1024,256]{1,0:T(8,128)(2,1)S(1)}, u32[]{:S(2)}, u32[]{:S(2)}) collective-permute-start(bf16[1024,256]{1,0:T(8,128)(2,1)S(1)} %collective-permute-done.4.refs_4_), channel_id=1, source_target_pairs={{0,1},{1,0},{2,3},{3,2},{4,5},{5,4},{6,7},{7,6},{8,9},{9,8},{10,11... | collective-permute-start | bytes 1572872 | tf_op jit(solution)/shard_map/ppermute | solution.py:254
  29.9 0.0 collective-permute-done.3.refs_0_
  29.9 0.0 copy-start.2
  29.9 0.9 copy-done.2
  30.9 1.4 %early_blocks.1 = (f32[1024,512]{1,0:T(8,128)S(1)}, bf16[1792,256]{1,0:T(8,128)(2,1)S(1)}, f32[8,256]{1,0:T(8,128)S(1)}) custom-call(s32[9]{0:T(128)S(1)} %stack.39.block_ref, f32[1024,256]{1,0:T(8,128)S(1)} %get-tuple-element.16.keys_ref, bf16[1792,256]{1,0:T(8,128)(2,1)S(1)} %get-tuple-element.17.rest_key_ref.refs_1_, bf16[1024,256]{1,0:T(8,128)(2,1)S(1)} %bitcast.22, ...), custom_call_target="tpu_custom_call" | custom-call | tf_op jit(solution)/shard_map/early_blocks/pallas_call | solution.py:339
  32.3 0.0 collective-permute-done.1.refs_6_
  32.3 0.0 collective-permute-done.2.refs_3_
  32.3 0.0 copy-start.3
  32.3 0.0 copy-start.5
  32.4 0.0 copy-start.6
  32.4 2.1 %collective-permute-start.6 = (bf16[1024,256]{1,0:T(8,128)(2,1)S(1)}, bf16[1024,256]{1,0:T(8,128)(2,1)S(1)}, u32[]{:S(2)}, u32[]{:S(2)}) collective-permute-start(bf16[1024,256]{1,0:T(8,128)(2,1)S(1)} %collective-permute-done.1.refs_6_), channel_id=1, source_target_pairs={{0,1},{1,0},{2,3},{3,2},{4,5},{5,4},{6,7},{7,6},{8,9},{9,8},{10,11... | collective-permute-start | bytes 1572872 | tf_op jit(solution)/shard_map/ppermute | solution.py:254
  34.4 0.0 collective-permute-done.5.refs_5_
  34.4 1.3 %late_blocks.1.acc_ref = f32[1024,512]{1,0:T(8,128)S(1)} custom-call(f32[1024,512]{1,0:T(8,128)S(1)} %get-tuple-element.21.refs_0_, bf16[1792,256]{1,0:T(8,128)(2,1)S(1)} %get-tuple-element.17.rest_key_ref.refs_1_, bf16[1792,256]{1,0:T(8,128)(2,1)S(1)} %get-tuple-element.22.refs_2_, bf16[1024,256]{1,0:T(8,128)(2,1)S(1)} %collective-permute-done.2.refs_3_, ...), custom_call_target="tpu_custom_call" | custom-call | tf_op jit(solution)/shard_map/late_blocks/pallas_call | solution.py:350
  35.7 0.6 collective-permute-done.6.refs_0_
  36.3 4.6 %local_sums.1 = bf16[3200,128]{1,0:T(8,128)(2,1)S(1)} custom-call(s32[32]{0:T(128)S(1)} %copy-done.6, f32[1024,512]{1,0:T(8,128)S(1)} %late_blocks.1.acc_ref, bf16[1024,256]{1,0:T(8,128)(2,1)S(1)} %collective-permute-done.6.refs_0_, bf16[1792,256]{1,0:T(8,128)(2,1)S(1)} %get-tuple-element.17.rest_key_ref.refs_1_, ...), custom_call_target="tpu_custom_call" | custom-call | tf_op jit(solution)/shard_map/local_sums/pallas_call | solution.py:358
  40.9 18.8 %all_to_all.34 = bf16[8,400,128]{2,1,0:T(8,128)(2,1)S(1)} all-to-all(bf16[8,400,128]{2,1,0:T(8,128)(2,1)S(1)} %bitcast.17), channel_id=1, replica_groups={{0,8,16,24,32,40,48,56},{2,10,18,26,34,42,50,58},{4,12,20,28,36,44,52,6..., dimensions={0} | all-to-all | bytes 1638400 | tf_op jit(solution)/shard_map/all_to_all | solution.py:305
  59.7 0.8 line_sums.1
  60.5 15.3 %all_to_all.35 = bf16[8,8,896]{2,1,0:T(8,128)(2,1)S(1)} all-to-all(bf16[8,8,896]{2,1,0:T(8,128)(2,1)S(1)} %bitcast.25), channel_id=1, replica_groups={{0,64,128,192,256,320,384,448},{2,66,130,194,258,322,386,450},{4,68,132..., dimensions={0} | all-to-all | bytes 229376 | tf_op jit(solution)/shard_map/all_to_all | solution.py:305
  75.8 0.3 final_sums.1
  76.1 21.2 %all_to_all.36 = bf16[64,8,512]{2,1,0:T(8,128)(2,1)S(1)} all-to-all(bf16[64,8,512]{2,1,0:T(8,128)(2,1)S(1)} %bitcast.23), channel_id=1, replica_groups={{0,64,128,192,256,320,384,448,8,72,136,200,264,328,392,456,16,80,144,20..., dimensions={0} | all-to-all | bytes 1048576 | tf_op jit(solution)/shard_map/all_to_all | solution.py:305
  97.3 0.8 fusion
  (7 shorter events, 0.0 us)
Async XLA Ops:
  0.6 19.4 %collective-permute-start = (bf16[1024,256]{1,0:T(8,128)(2,1)}, bf16[1024,256]{1,0:T(8,128)(2,1)S(1)}, u32[]{:S(2)}, u32[]{:S(2)}) collective-permute-start(bf16[1024,256]{1,0:T(8,128)(2,1)} %bitcast.18), channel_id=1, source_target_pairs={{0,2},{1,7},{2,4},{3,1},{4,6},{5,3},{6,0},{7,5},{8,10},{9,15},{10,... | collective-permute-start | bytes 1572872 | tf_op jit(solution)/shard_map/ppermute | solution.py:276
  8.6 1.0 %copy-start = (bf16[32,32,256]{2,1,0:T(8,128)(2,1)S(1)}, bf16[32,32,256]{2,1,0:T(8,128)(2,1)}, u32[]{:S(2)}) copy-start(bf16[32,32,256]{2,1,0:T(8,128)(2,1)} %param.7) | copy-start | bytes 1572868
  9.6 1.2 %copy-start.4 = (bf16[2048,256]{1,0:T(8,128)(2,1)S(1)}, bf16[2048,256]{1,0:T(8,128)(2,1)}, u32[]{:S(2)}) copy-start(bf16[2048,256]{1,0:T(8,128)(2,1)} %wk_ref.1) | copy-start | bytes 3145732
  10.8 19.1 %copy-start.1 = (bf16[2048,256]{1,0:T(8,128)(2,1)S(1)}, bf16[2048,256]{1,0:T(8,128)(2,1)}, u32[]{:S(2)}) copy-start(bf16[2048,256]{1,0:T(8,128)(2,1)} %wv_ref.1) | copy-start | bytes 3145732
  11.7 15.8 %collective-permute-start.4 = (bf16[1024,256]{1,0:T(8,128)(2,1)S(1)}, bf16[1024,256]{1,0:T(8,128)(2,1)S(1)}, u32[]{:S(2)}, u32[]{:S(2)}) collective-permute-start(bf16[1024,256]{1,0:T(8,128)(2,1)S(1)} %bitcast.20), channel_id=1, source_target_pairs={{0,6},{1,3},{2,0},{3,5},{4,2},{5,7},{6,4},{7,1},{8,14},{9,11},{10,... | collective-permute-start | bytes 1572872 | tf_op jit(solution)/shard_map/ppermute | solution.py:276
  13.6 16.3 %collective-permute-start.3 = (bf16[1024,256]{1,0:T(8,128)(2,1)S(1)}, bf16[1024,256]{1,0:T(8,128)(2,1)S(1)}, u32[]{:S(2)}, u32[]{:S(2)}) collective-permute-start(bf16[1024,256]{1,0:T(8,128)(2,1)S(1)} %bitcast.21), channel_id=1, source_target_pairs={{0,1},{1,0},{2,3},{3,2},{4,5},{5,4},{6,7},{7,6},{8,9},{9,8},{10,11... | collective-permute-start | bytes 1572872 | tf_op jit(solution)/shard_map/ppermute | solution.py:254
  20.1 12.3 %collective-permute-start.1 = (bf16[1024,256]{1,0:T(8,128)(2,1)S(1)}, bf16[1024,256]{1,0:T(8,128)(2,1)S(1)}, u32[]{:S(2)}, u32[]{:S(2)}) collective-permute-start(bf16[1024,256]{1,0:T(8,128)(2,1)S(1)} %collective-permute-done.refs_1_), channel_id=1, source_target_pairs={{0,2},{1,7},{2,4},{3,1},{4,6},{5,3},{6,0},{7,5},{8,10},{9,15},{10,... | collective-permute-start | bytes 1572872 | tf_op jit(solution)/shard_map/ppermute | solution.py:276
  25.5 6.8 %collective-permute-start.2 = (bf16[1024,256]{1,0:T(8,128)(2,1)S(1)}, bf16[1024,256]{1,0:T(8,128)(2,1)S(1)}, u32[]{:S(2)}, u32[]{:S(2)}) collective-permute-start(bf16[1024,256]{1,0:T(8,128)(2,1)S(1)} %collective-permute-done.refs_1_), channel_id=1, source_target_pairs={{0,1},{1,0},{2,3},{3,2},{4,5},{5,4},{6,7},{7,6},{8,9},{9,8},{10,11... | collective-permute-start | bytes 1572872 | tf_op jit(solution)/shard_map/ppermute | solution.py:254
  27.5 6.9 %collective-permute-start.5 = (bf16[1024,256]{1,0:T(8,128)(2,1)S(1)}, bf16[1024,256]{1,0:T(8,128)(2,1)S(1)}, u32[]{:S(2)}, u32[]{:S(2)}) collective-permute-start(bf16[1024,256]{1,0:T(8,128)(2,1)S(1)} %collective-permute-done.4.refs_4_), channel_id=1, source_target_pairs={{0,1},{1,0},{2,3},{3,2},{4,5},{5,4},{6,7},{7,6},{8,9},{9,8},{10,11... | collective-permute-start | bytes 1572872 | tf_op jit(solution)/shard_map/ppermute | solution.py:254
  29.9 1.0 copy-start.2
  32.3 4.0 %copy-start.3 = (bf16[512,256]{1,0:T(8,128)(2,1)S(1)}, bf16[512,256]{1,0:T(8,128)(2,1)}, u32[]{:S(2)}) copy-start(bf16[512,256]{1,0:T(8,128)(2,1)} %refs_4_.1) | copy-start | bytes 786436
  32.3 4.0 %copy-start.5 = (bf16[512,256]{1,0:T(8,128)(2,1)S(1)}, bf16[512,256]{1,0:T(8,128)(2,1)}, u32[]{:S(2)}) copy-start(bf16[512,256]{1,0:T(8,128)(2,1)} %refs_3_.1) | copy-start | bytes 786436
  32.4 4.0 %copy-start.6 = (s32[32]{0:T(128)S(1)}, s32[32]{0:T(128)}, u32[]{:S(2)}) copy-start(s32[32]{0:T(128)} %owner_ref.1) | copy-start | bytes 388
  32.4 3.9 %collective-permute-start.6 = (bf16[1024,256]{1,0:T(8,128)(2,1)S(1)}, bf16[1024,256]{1,0:T(8,128)(2,1)S(1)}, u32[]{:S(2)}, u32[]{:S(2)}) collective-permute-start(bf16[1024,256]{1,0:T(8,128)(2,1)S(1)} %collective-permute-done.1.refs_6_), channel_id=1, source_target_pairs={{0,1},{1,0},{2,3},{3,2},{4,5},{5,4},{6,7},{7,6},{8,9},{9,8},{10,11... | collective-permute-start | bytes 1572872 | tf_op jit(solution)/shard_map/ppermute | solution.py:254

commit v13 on v12

--- a/solution.py
+++ b/solution.py
@@ -97,7 +97,6 @@
 def local_kernel(owner_ref, acc_ref, *refs):
     (far_ref, rest_key_ref, rest_value_ref, q_ref, c_ref, out_ref, kblk, vblk, score, product, top, total, dots, corr, acc_v, acc_k) = refs
     slots = owner_ref.shape[0]
-    half = slots // 2
     cols = q_ref.shape[1]
     heads = cols // HDIM
     keys = heads * PL
@@ -114,24 +113,31 @@
     ).astype(f32).astype(bf16)
 
     weight = jnp.concatenate([ref[-far_ref.shape[1] :, :] for ref in (rest_key_ref, rest_value_ref)], axis=1)
-    for side in range(2):
-        low = side * half * PL
-        rows = far_ref[low : low + half * PL, :]
-        projected = acc_ref[low : low + half * PL, :] + jnp.dot(rows, weight, preferred_element_type=f32)
-        projected = projected.astype(bf16)
-        for i in range(half):
-            slot = side * half + i
-            own = projected[i * PL : (i + 1) * PL]
-            kb = jnp.concatenate([own[:, :cols]] * heads, axis=0) * on_diagonal
-            vb = jnp.concatenate([own[:, cols:]] * heads, axis=0) * on_diagonal
-            kblk[slot] = kb
-            vblk[slot] = vb
-            o = owner_ref[slot]
-            at = pl.ds(pl.multiple_of(jnp.minimum(o, QUESTIONS - 1) * TGT, TGT), TGT)
-            s = lax.dot_general(q_ref[at, :], kb, NT, preferred_element_type=f32)
-            score[slot] = s
-            product[slot] = lax.dot_general(c_ref[at, :], vb, NT, preferred_element_type=f32)
-            top[o] = jnp.maximum(top[o], s)
+    rows = far_ref[...]
+    projected = acc_ref[...] + jnp.dot(rows, weight, preferred_element_type=f32)
+    projected = projected.astype(bf16)
+    for slot in range(slots):
+        own = projected[slot * PL : (slot + 1) * PL]
+        kb = jnp.concatenate([own[:, :cols]] * heads, axis=0) * on_diagonal
+        vb = jnp.concatenate([own[:, cols:]] * heads, axis=0) * on_diagonal
+        kblk[slot] = kb
+        vblk[slot] = vb
+    for slot in range(0, slots, 2):
+        owners = [owner_ref[slot + n] for n in range(2)]
+        ats = [pl.ds(pl.multiple_of(jnp.minimum(o, QUESTIONS - 1) * TGT, TGT), TGT) for o in owners]
+
+        def both_ways(rows_ref, block_ref):
+            rows = jnp.concatenate([rows_ref[at, :] for at in ats], axis=0)
+            blocks = jnp.concatenate([block_ref[slot], block_ref[slot + 1]], axis=0)
+            return lax.dot_general(rows, blocks, NT, preferred_element_type=f32)
+
+        s = both_ways(q_ref, kblk)
+        p = both_ways(c_ref, vblk)
+        for n, o in enumerate(owners):
+            part = s[n * TGT : (n + 1) * TGT, n * keys : (n + 1) * keys]
+            score[slot + n] = part
+            product[slot + n] = p[n * TGT : (n + 1) * TGT, n * keys : (n + 1) * keys]
+            top[o] = jnp.maximum(top[o], part)
 
     for q in range(QUESTIONS):
         top[q] = per_head(top[q], PL, jnp.max, masked_value)

time: 99.6 us -> 99.3 us (level)
  no operation moved by 1% of the time
where the time goes in v13:
time: 99.3 us; the launch traced here: 97.9 us
  blocking collectives  55.3 us (56%)
  starting transfers between devices  23.5 us (24%)
  Pallas kernels  8.95 us (9%)
  waiting for transfers between devices  5.13 us (5%)
  local copies, waits for them, and re-layouts  4.15 us (4%)
    all_to_all x3, blocking collectives, exchange(): return lax.all_to_all(x, AXES, 0, 0, axis_index_groups=groups, tiled=True)  55.3 us
    ppermute x3, starting transfers between devices, along(): return lax.ppermute(block, ('pb', 'rep'), pairs)  15.2 us
    ppermute x4, starting transfers between devices, swap(): return lax.ppermute(block, 'rep', [(0, 1), (1, 0)])  8.3 us
    ppermute x3, waiting for transfers between devices, along(): return lax.ppermute(block, ('pb', 'rep'), pairs)  4.52 us
    pallas_call x1, Pallas kernels, body(): pl.pallas_call(local_kernel, out_shape=jax.ShapeDtypeStruct((SIDE * CHUNK...  4.33 us
    unnamed x14, local copies, waits for them, and re-layouts  3.24 us
  transfers between devices with their start and end apart: 7, of which 2 were waited for; matrix products, arithmetic and copies ran while one was open for 0% of the time, Pallas kernels for 4%

profile of v13, /device:TPU:6, one launch (start us, length us, event | category | flops | bytes accessed | tf_op | source)
XLA Modules:
  0.0 97.9 jit_solution(8327525642006632280)
XLA Ops:
  0.6 7.8 %collective-permute-start = (bf16[1024,256]{1,0:T(8,128)(2,1)}, bf16[1024,256]{1,0:T(8,128)(2,1)S(1)}, u32[]{:S(2)}, u32[]{:S(2)}) collective-permute-start(bf16[1024,256]{1,0:T(8,128)(2,1)} %bitcast.18), channel_id=1, source_target_pairs={{0,2},{1,7},{2,4},{3,1},{4,6},{5,3},{6,0},{7,5},{8,10},{9,15},{10,... | collective-permute-start | bytes 1572872 | tf_op jit(solution)/shard_map/ppermute | solution.py:282
  8.5 0.1 stack.39.block_ref
  8.6 1.0 %copy-done = bf16[32,32,256]{2,1,0:T(8,128)(2,1)S(1)} copy-done((bf16[32,32,256]{2,1,0:T(8,128)(2,1)S(1)}, bf16[32,32,256]{2,1,0:T(8,128)(2,1)}, u32[]{:S(2)}) %copy-start) | copy-done | bytes 524312
  9.6 1.2 %copy-done.4 = bf16[2048,256]{1,0:T(8,128)(2,1)S(1)} copy-done((bf16[2048,256]{1,0:T(8,128)(2,1)S(1)}, bf16[2048,256]{1,0:T(8,128)(2,1)}, u32[]{:S(2)}) %copy-start.4) | copy-done | bytes 1048600
  10.8 0.8 own_keys.1
  11.7 1.9 %collective-permute-start.4 = (bf16[1024,256]{1,0:T(8,128)(2,1)S(1)}, bf16[1024,256]{1,0:T(8,128)(2,1)S(1)}, u32[]{:S(2)}, u32[]{:S(2)}) collective-permute-start(bf16[1024,256]{1,0:T(8,128)(2,1)S(1)} %bitcast.20), channel_id=1, source_target_pairs={{0,6},{1,3},{2,0},{3,5},{4,2},{5,7},{6,4},{7,1},{8,14},{9,11},{10,... | collective-permute-start | bytes 1572872 | tf_op jit(solution)/shard_map/ppermute | solution.py:282
  13.6 1.9 %collective-permute-start.3 = (bf16[1024,256]{1,0:T(8,128)(2,1)S(1)}, bf16[1024,256]{1,0:T(8,128)(2,1)S(1)}, u32[]{:S(2)}, u32[]{:S(2)}) collective-permute-start(bf16[1024,256]{1,0:T(8,128)(2,1)S(1)} %bitcast.21), channel_id=1, source_target_pairs={{0,1},{1,0},{2,3},{3,2},{4,5},{5,4},{6,7},{7,6},{8,9},{9,8},{10,11... | collective-permute-start | bytes 1572872 | tf_op jit(solution)/shard_map/ppermute | solution.py:260
  15.5 4.5 %collective-permute-done.refs_1_ = bf16[1024,256]{1,0:T(8,128)(2,1)S(1)} collective-permute-done((bf16[1024,256]{1,0:T(8,128)(2,1)}, bf16[1024,256]{1,0:T(8,128)(2,1)S(1)}, u32[]{:S(2)}, u32[]{:S(2)}) %collective-permute-start) | collective-permute-done | bytes 524320 | tf_op jit(solution)/shard_map/ppermute | solution.py:282
  20.1 5.5 %collective-permute-start.1 = (bf16[1024,256]{1,0:T(8,128)(2,1)S(1)}, bf16[1024,256]{1,0:T(8,128)(2,1)S(1)}, u32[]{:S(2)}, u32[]{:S(2)}) collective-permute-start(bf16[1024,256]{1,0:T(8,128)(2,1)S(1)} %collective-permute-done.refs_1_), channel_id=1, source_target_pairs={{0,2},{1,7},{2,4},{3,1},{4,6},{5,3},{6,0},{7,5},{8,10},{9,15},{10,... | collective-permute-start | bytes 1572872 | tf_op jit(solution)/shard_map/ppermute | solution.py:282
  25.5 1.9 %collective-permute-start.2 = (bf16[1024,256]{1,0:T(8,128)(2,1)S(1)}, bf16[1024,256]{1,0:T(8,128)(2,1)S(1)}, u32[]{:S(2)}, u32[]{:S(2)}) collective-permute-start(bf16[1024,256]{1,0:T(8,128)(2,1)S(1)} %collective-permute-done.refs_1_), channel_id=1, source_target_pairs={{0,1},{1,0},{2,3},{3,2},{4,5},{5,4},{6,7},{7,6},{8,9},{9,8},{10,11... | collective-permute-start | bytes 1572872 | tf_op jit(solution)/shard_map/ppermute | solution.py:260
  27.5 0.0 collective-permute-done.4.refs_4_
  27.5 2.4 %collective-permute-start.5 = (bf16[1024,256]{1,0:T(8,128)(2,1)S(1)}, bf16[1024,256]{1,0:T(8,128)(2,1)S(1)}, u32[]{:S(2)}, u32[]{:S(2)}) collective-permute-start(bf16[1024,256]{1,0:T(8,128)(2,1)S(1)} %collective-permute-done.4.refs_4_), channel_id=1, source_target_pairs={{0,1},{1,0},{2,3},{3,2},{4,5},{5,4},{6,7},{7,6},{8,9},{9,8},{10,11... | collective-permute-start | bytes 1572872 | tf_op jit(solution)/shard_map/ppermute | solution.py:260
  29.9 0.0 collective-permute-done.3.refs_0_
  29.9 0.0 copy-start.2
  29.9 0.9 copy-done.2
  30.9 1.4 %early_blocks.1 = (f32[1024,512]{1,0:T(8,128)S(1)}, bf16[1792,256]{1,0:T(8,128)(2,1)S(1)}, f32[8,256]{1,0:T(8,128)S(1)}) custom-call(s32[9]{0:T(128)S(1)} %stack.39.block_ref, f32[1024,256]{1,0:T(8,128)S(1)} %get-tuple-element.16.keys_ref, bf16[1792,256]{1,0:T(8,128)(2,1)S(1)} %get-tuple-element.17.rest_key_ref.refs_1_, bf16[1024,256]{1,0:T(8,128)(2,1)S(1)} %bitcast.22, ...), custom_call_target="tpu_custom_call" | custom-call | tf_op jit(solution)/shard_map/early_blocks/pallas_call | solution.py:345
  32.3 0.0 collective-permute-done.1.refs_6_
  32.3 0.0 collective-permute-done.2.refs_3_
  32.3 0.0 copy-start.3
  32.3 0.0 copy-start.5
  32.4 0.0 copy-start.6
  32.4 2.1 %collective-permute-start.6 = (bf16[1024,256]{1,0:T(8,128)(2,1)S(1)}, bf16[1024,256]{1,0:T(8,128)(2,1)S(1)}, u32[]{:S(2)}, u32[]{:S(2)}) collective-permute-start(bf16[1024,256]{1,0:T(8,128)(2,1)S(1)} %collective-permute-done.1.refs_6_), channel_id=1, source_target_pairs={{0,1},{1,0},{2,3},{3,2},{4,5},{5,4},{6,7},{7,6},{8,9},{9,8},{10,11... | collective-permute-start | bytes 1572872 | tf_op jit(solution)/shard_map/ppermute | solution.py:260
  34.4 0.0 collective-permute-done.5.refs_5_
  34.4 1.3 %late_blocks.1.acc_ref = f32[1024,512]{1,0:T(8,128)S(1)} custom-call(f32[1024,512]{1,0:T(8,128)S(1)} %get-tuple-element.21.refs_0_, bf16[1792,256]{1,0:T(8,128)(2,1)S(1)} %get-tuple-element.17.rest_key_ref.refs_1_, bf16[1792,256]{1,0:T(8,128)(2,1)S(1)} %get-tuple-element.22.refs_2_, bf16[1024,256]{1,0:T(8,128)(2,1)S(1)} %collective-permute-done.2.refs_3_, ...), custom_call_target="tpu_custom_call" | custom-call | tf_op jit(solution)/shard_map/late_blocks/pallas_call | solution.py:356
  35.7 0.6 collective-permute-done.6.refs_0_
  36.3 4.3 %local_sums.1 = bf16[3200,128]{1,0:T(8,128)(2,1)S(1)} custom-call(s32[32]{0:T(128)S(1)} %copy-done.6, f32[1024,512]{1,0:T(8,128)S(1)} %late_blocks.1.acc_ref, bf16[1024,256]{1,0:T(8,128)(2,1)S(1)} %collective-permute-done.6.refs_0_, bf16[1792,256]{1,0:T(8,128)(2,1)S(1)} %get-tuple-element.17.rest_key_ref.refs_1_, ...), custom_call_target="tpu_custom_call" | custom-call | tf_op jit(solution)/shard_map/local_sums/pallas_call | solution.py:364
  40.7 18.8 %all_to_all.34 = bf16[8,400,128]{2,1,0:T(8,128)(2,1)S(1)} all-to-all(bf16[8,400,128]{2,1,0:T(8,128)(2,1)S(1)} %bitcast.17), channel_id=1, replica_groups={{0,8,16,24,32,40,48,56},{2,10,18,26,34,42,50,58},{4,12,20,28,36,44,52,6..., dimensions={0} | all-to-all | bytes 1638400 | tf_op jit(solution)/shard_map/all_to_all | solution.py:311
  59.5 0.8 line_sums.1
  60.3 15.3 %all_to_all.35 = bf16[8,8,896]{2,1,0:T(8,128)(2,1)S(1)} all-to-all(bf16[8,8,896]{2,1,0:T(8,128)(2,1)S(1)} %bitcast.25), channel_id=1, replica_groups={{0,64,128,192,256,320,384,448},{2,66,130,194,258,322,386,450},{4,68,132..., dimensions={0} | all-to-all | bytes 229376 | tf_op jit(solution)/shard_map/all_to_all | solution.py:311
  75.6 0.3 final_sums.1
  75.9 21.2 %all_to_all.36 = bf16[64,8,512]{2,1,0:T(8,128)(2,1)S(1)} all-to-all(bf16[64,8,512]{2,1,0:T(8,128)(2,1)S(1)} %bitcast.23), channel_id=1, replica_groups={{0,64,128,192,256,320,384,448,8,72,136,200,264,328,392,456,16,80,144,20..., dimensions={0} | all-to-all | bytes 1048576 | tf_op jit(solution)/shard_map/all_to_all | solution.py:311
  97.0 0.8 fusion
  (7 shorter events, 0.0 us)
Async XLA Ops:
  0.6 19.4 %collective-permute-start = (bf16[1024,256]{1,0:T(8,128)(2,1)}, bf16[1024,256]{1,0:T(8,128)(2,1)S(1)}, u32[]{:S(2)}, u32[]{:S(2)}) collective-permute-start(bf16[1024,256]{1,0:T(8,128)(2,1)} %bitcast.18), channel_id=1, source_target_pairs={{0,2},{1,7},{2,4},{3,1},{4,6},{5,3},{6,0},{7,5},{8,10},{9,15},{10,... | collective-permute-start | bytes 1572872 | tf_op jit(solution)/shard_map/ppermute | solution.py:282
  8.6 1.0 %copy-start = (bf16[32,32,256]{2,1,0:T(8,128)(2,1)S(1)}, bf16[32,32,256]{2,1,0:T(8,128)(2,1)}, u32[]{:S(2)}) copy-start(bf16[32,32,256]{2,1,0:T(8,128)(2,1)} %param.7) | copy-start | bytes 1572868
  9.6 1.2 %copy-start.4 = (bf16[2048,256]{1,0:T(8,128)(2,1)S(1)}, bf16[2048,256]{1,0:T(8,128)(2,1)}, u32[]{:S(2)}) copy-start(bf16[2048,256]{1,0:T(8,128)(2,1)} %wk_ref.1) | copy-start | bytes 3145732
  10.8 19.1 %copy-start.1 = (bf16[2048,256]{1,0:T(8,128)(2,1)S(1)}, bf16[2048,256]{1,0:T(8,128)(2,1)}, u32[]{:S(2)}) copy-start(bf16[2048,256]{1,0:T(8,128)(2,1)} %wv_ref.1) | copy-start | bytes 3145732
  11.7 15.8 %collective-permute-start.4 = (bf16[1024,256]{1,0:T(8,128)(2,1)S(1)}, bf16[1024,256]{1,0:T(8,128)(2,1)S(1)}, u32[]{:S(2)}, u32[]{:S(2)}) collective-permute-start(bf16[1024,256]{1,0:T(8,128)(2,1)S(1)} %bitcast.20), channel_id=1, source_target_pairs={{0,6},{1,3},{2,0},{3,5},{4,2},{5,7},{6,4},{7,1},{8,14},{9,11},{10,... | collective-permute-start | bytes 1572872 | tf_op jit(solution)/shard_map/ppermute | solution.py:282
  13.6 16.3 %collective-permute-start.3 = (bf16[1024,256]{1,0:T(8,128)(2,1)S(1)}, bf16[1024,256]{1,0:T(8,128)(2,1)S(1)}, u32[]{:S(2)}, u32[]{:S(2)}) collective-permute-start(bf16[1024,256]{1,0:T(8,128)(2,1)S(1)} %bitcast.21), channel_id=1, source_target_pairs={{0,1},{1,0},{2,3},{3,2},{4,5},{5,4},{6,7},{7,6},{8,9},{9,8},{10,11... | collective-permute-start | bytes 1572872 | tf_op jit(solution)/shard_map/ppermute | solution.py:260
  20.1 12.3 %collective-permute-start.1 = (bf16[1024,256]{1,0:T(8,128)(2,1)S(1)}, bf16[1024,256]{1,0:T(8,128)(2,1)S(1)}, u32[]{:S(2)}, u32[]{:S(2)}) collective-permute-start(bf16[1024,256]{1,0:T(8,128)(2,1)S(1)} %collective-permute-done.refs_1_), channel_id=1, source_target_pairs={{0,2},{1,7},{2,4},{3,1},{4,6},{5,3},{6,0},{7,5},{8,10},{9,15},{10,... | collective-permute-start | bytes 1572872 | tf_op jit(solution)/shard_map/ppermute | solution.py:282
  25.5 6.8 %collective-permute-start.2 = (bf16[1024,256]{1,0:T(8,128)(2,1)S(1)}, bf16[1024,256]{1,0:T(8,128)(2,1)S(1)}, u32[]{:S(2)}, u32[]{:S(2)}) collective-permute-start(bf16[1024,256]{1,0:T(8,128)(2,1)S(1)} %collective-permute-done.refs_1_), channel_id=1, source_target_pairs={{0,1},{1,0},{2,3},{3,2},{4,5},{5,4},{6,7},{7,6},{8,9},{9,8},{10,11... | collective-permute-start | bytes 1572872 | tf_op jit(solution)/shard_map/ppermute | solution.py:260
  27.5 6.9 %collective-permute-start.5 = (bf16[1024,256]{1,0:T(8,128)(2,1)S(1)}, bf16[1024,256]{1,0:T(8,128)(2,1)S(1)}, u32[]{:S(2)}, u32[]{:S(2)}) collective-permute-start(bf16[1024,256]{1,0:T(8,128)(2,1)S(1)} %collective-permute-done.4.refs_4_), channel_id=1, source_target_pairs={{0,1},{1,0},{2,3},{3,2},{4,5},{5,4},{6,7},{7,6},{8,9},{9,8},{10,11... | collective-permute-start | bytes 1572872 | tf_op jit(solution)/shard_map/ppermute | solution.py:260
  29.9 1.0 copy-start.2
  32.3 4.0 %copy-start.3 = (bf16[512,256]{1,0:T(8,128)(2,1)S(1)}, bf16[512,256]{1,0:T(8,128)(2,1)}, u32[]{:S(2)}) copy-start(bf16[512,256]{1,0:T(8,128)(2,1)} %refs_4_.1) | copy-start | bytes 786436
  32.3 4.0 %copy-start.5 = (bf16[512,256]{1,0:T(8,128)(2,1)S(1)}, bf16[512,256]{1,0:T(8,128)(2,1)}, u32[]{:S(2)}) copy-start(bf16[512,256]{1,0:T(8,128)(2,1)} %refs_3_.1) | copy-start | bytes 786436
  32.4 4.0 %copy-start.6 = (s32[32]{0:T(128)S(1)}, s32[32]{0:T(128)}, u32[]{:S(2)}) copy-start(s32[32]{0:T(128)} %owner_ref.1) | copy-start | bytes 388
  32.4 3.9 %collective-permute-start.6 = (bf16[1024,256]{1,0:T(8,128)(2,1)S(1)}, bf16[1024,256]{1,0:T(8,128)(2,1)S(1)}, u32[]{:S(2)}, u32[]{:S(2)}) collective-permute-start(bf16[1024,256]{1,0:T(8,128)(2,1)S(1)} %collective-permute-done.1.refs_6_), channel_id=1, source_target_pairs={{0,1},{1,0},{2,3},{3,2},{4,5},{5,4},{6,7},{7,6},{8,9},{9,8},{10,11... | collective-permute-start | bytes 1572872 | tf_op jit(solution)/shard_map/ppermute | solution.py:260

commit v14 on v13

--- a/solution.py
+++ b/solution.py
@@ -149,11 +149,19 @@
         total[o] = total[o] + e
         dots[o] = dots[o] + e * product[slot]
 
-    for q in range(QUESTIONS):
-        t = per_head(total[q], PL, jnp.sum, 0.0)
-        d = per_head(dots[q], PL, jnp.sum, 0.0)
-        total[q] = t
-        corr[q] = two_parts(jnp.where(t > 0.0, d / jnp.where(t > 0.0, t, 1.0), 0.0))
+    same_head = (
+        lax.broadcasted_iota(jnp.int32, (PARTS * keys, keys), 0) % keys // PL
+        == lax.broadcasted_iota(jnp.int32, (PARTS * keys, keys), 1) // PL
+    ).astype(f32).astype(bf16)
+
+    def head_sums(ref):
+        parts = jnp.concatenate(split_parts(ref[:QUESTIONS].reshape(QUESTIONS * TGT, keys)), axis=1)
+        return jnp.dot(parts.astype(bf16), same_head, preferred_element_type=f32).reshape(QUESTIONS, TGT, keys)
+
+    t = head_sums(total)
+    d = head_sums(dots)
+    total[:QUESTIONS] = t
+    corr[:QUESTIONS] = two_parts(jnp.where(t > 0.0, d / jnp.where(t > 0.0, t, 1.0), 0.0))
     corr[QUESTIONS] = jnp.zeros_like(corr[QUESTIONS])
 
     for slot in range(slots):

time: 99.3 us -> 99 us (level)
  no operation moved by 1% of the time
where the time goes in v14:
time: 99 us; the launch traced here: 97.6 us
  blocking collectives  55.3 us (56%)
  starting transfers between devices  23.5 us (24%)
  Pallas kernels  8.62 us (9%)
  waiting for transfers between devices  5.13 us (5%)
  local copies, waits for them, and re-layouts  4.15 us (4%)
    all_to_all x3, blocking collectives, exchange(): return lax.all_to_all(x, AXES, 0, 0, axis_index_groups=groups, tiled=True)  55.3 us
    ppermute x3, starting transfers between devices, along(): return lax.ppermute(block, ('pb', 'rep'), pairs)  15.2 us
    ppermute x4, starting transfers between devices, swap(): return lax.ppermute(block, 'rep', [(0, 1), (1, 0)])  8.3 us
    ppermute x3, waiting for transfers between devices, along(): return lax.ppermute(block, ('pb', 'rep'), pairs)  4.52 us
    pallas_call x1, Pallas kernels, body(): pl.pallas_call(local_kernel, out_shape=jax.ShapeDtypeStruct((SIDE * CHUNK...  4 us
    unnamed x14, local copies, waits for them, and re-layouts  3.24 us
  transfers between devices with their start and end apart: 7, of which 2 were waited for; matrix products, arithmetic and copies ran while one was open for 0% of the time, Pallas kernels for 4%

profile of v14, /device:TPU:6, one launch (start us, length us, event | category | flops | bytes accessed | tf_op | source)
XLA Modules:
  0.0 97.6 jit_solution(18261684820732570787)
XLA Ops:
  0.6 7.8 %collective-permute-start = (bf16[1024,256]{1,0:T(8,128)(2,1)}, bf16[1024,256]{1,0:T(8,128)(2,1)S(1)}, u32[]{:S(2)}, u32[]{:S(2)}) collective-permute-start(bf16[1024,256]{1,0:T(8,128)(2,1)} %bitcast.18), channel_id=1, source_target_pairs={{0,2},{1,7},{2,4},{3,1},{4,6},{5,3},{6,0},{7,5},{8,10},{9,15},{10,... | collective-permute-start | bytes 1572872 | tf_op jit(solution)/shard_map/ppermute | solution.py:290
  8.5 0.1 stack.39.block_ref
  8.6 1.0 %copy-done = bf16[32,32,256]{2,1,0:T(8,128)(2,1)S(1)} copy-done((bf16[32,32,256]{2,1,0:T(8,128)(2,1)S(1)}, bf16[32,32,256]{2,1,0:T(8,128)(2,1)}, u32[]{:S(2)}) %copy-start) | copy-done | bytes 524312
  9.6 1.2 %copy-done.4 = bf16[2048,256]{1,0:T(8,128)(2,1)S(1)} copy-done((bf16[2048,256]{1,0:T(8,128)(2,1)S(1)}, bf16[2048,256]{1,0:T(8,128)(2,1)}, u32[]{:S(2)}) %copy-start.4) | copy-done | bytes 1048600
  10.8 0.8 own_keys.1
  11.7 1.9 %collective-permute-start.4 = (bf16[1024,256]{1,0:T(8,128)(2,1)S(1)}, bf16[1024,256]{1,0:T(8,128)(2,1)S(1)}, u32[]{:S(2)}, u32[]{:S(2)}) collective-permute-start(bf16[1024,256]{1,0:T(8,128)(2,1)S(1)} %bitcast.20), channel_id=1, source_target_pairs={{0,6},{1,3},{2,0},{3,5},{4,2},{5,7},{6,4},{7,1},{8,14},{9,11},{10,... | collective-permute-start | bytes 1572872 | tf_op jit(solution)/shard_map/ppermute | solution.py:290
  13.6 1.9 %collective-permute-start.3 = (bf16[1024,256]{1,0:T(8,128)(2,1)S(1)}, bf16[1024,256]{1,0:T(8,128)(2,1)S(1)}, u32[]{:S(2)}, u32[]{:S(2)}) collective-permute-start(bf16[1024,256]{1,0:T(8,128)(2,1)S(1)} %bitcast.21), channel_id=1, source_target_pairs={{0,1},{1,0},{2,3},{3,2},{4,5},{5,4},{6,7},{7,6},{8,9},{9,8},{10,11... | collective-permute-start | bytes 1572872 | tf_op jit(solution)/shard_map/ppermute | solution.py:268
  15.5 4.5 %collective-permute-done.refs_1_ = bf16[1024,256]{1,0:T(8,128)(2,1)S(1)} collective-permute-done((bf16[1024,256]{1,0:T(8,128)(2,1)}, bf16[1024,256]{1,0:T(8,128)(2,1)S(1)}, u32[]{:S(2)}, u32[]{:S(2)}) %collective-permute-start) | collective-permute-done | bytes 524320 | tf_op jit(solution)/shard_map/ppermute | solution.py:290
  20.1 5.5 %collective-permute-start.1 = (bf16[1024,256]{1,0:T(8,128)(2,1)S(1)}, bf16[1024,256]{1,0:T(8,128)(2,1)S(1)}, u32[]{:S(2)}, u32[]{:S(2)}) collective-permute-start(bf16[1024,256]{1,0:T(8,128)(2,1)S(1)} %collective-permute-done.refs_1_), channel_id=1, source_target_pairs={{0,2},{1,7},{2,4},{3,1},{4,6},{5,3},{6,0},{7,5},{8,10},{9,15},{10,... | collective-permute-start | bytes 1572872 | tf_op jit(solution)/shard_map/ppermute | solution.py:290
  25.5 1.9 %collective-permute-start.2 = (bf16[1024,256]{1,0:T(8,128)(2,1)S(1)}, bf16[1024,256]{1,0:T(8,128)(2,1)S(1)}, u32[]{:S(2)}, u32[]{:S(2)}) collective-permute-start(bf16[1024,256]{1,0:T(8,128)(2,1)S(1)} %collective-permute-done.refs_1_), channel_id=1, source_target_pairs={{0,1},{1,0},{2,3},{3,2},{4,5},{5,4},{6,7},{7,6},{8,9},{9,8},{10,11... | collective-permute-start | bytes 1572872 | tf_op jit(solution)/shard_map/ppermute | solution.py:268
  27.5 0.0 collective-permute-done.4.refs_4_
  27.5 2.4 %collective-permute-start.5 = (bf16[1024,256]{1,0:T(8,128)(2,1)S(1)}, bf16[1024,256]{1,0:T(8,128)(2,1)S(1)}, u32[]{:S(2)}, u32[]{:S(2)}) collective-permute-start(bf16[1024,256]{1,0:T(8,128)(2,1)S(1)} %collective-permute-done.4.refs_4_), channel_id=1, source_target_pairs={{0,1},{1,0},{2,3},{3,2},{4,5},{5,4},{6,7},{7,6},{8,9},{9,8},{10,11... | collective-permute-start | bytes 1572872 | tf_op jit(solution)/shard_map/ppermute | solution.py:268
  29.9 0.0 collective-permute-done.3.refs_0_
  29.9 0.0 copy-start.2
  29.9 0.9 copy-done.2
  30.9 1.4 %early_blocks.1 = (f32[1024,512]{1,0:T(8,128)S(1)}, bf16[1792,256]{1,0:T(8,128)(2,1)S(1)}, f32[8,256]{1,0:T(8,128)S(1)}) custom-call(s32[9]{0:T(128)S(1)} %stack.39.block_ref, f32[1024,256]{1,0:T(8,128)S(1)} %get-tuple-element.16.keys_ref, bf16[1792,256]{1,0:T(8,128)(2,1)S(1)} %get-tuple-element.17.rest_key_ref.refs_1_, bf16[1024,256]{1,0:T(8,128)(2,1)S(1)} %bitcast.22, ...), custom_call_target="tpu_custom_call" | custom-call | tf_op jit(solution)/shard_map/early_blocks/pallas_call | solution.py:353
  32.3 0.0 collective-permute-done.1.refs_6_
  32.3 0.0 collective-permute-done.2.refs_3_
  32.3 0.0 copy-start.3
  32.3 0.0 copy-start.5
  32.4 0.0 copy-start.6
  32.4 2.1 %collective-permute-start.6 = (bf16[1024,256]{1,0:T(8,128)(2,1)S(1)}, bf16[1024,256]{1,0:T(8,128)(2,1)S(1)}, u32[]{:S(2)}, u32[]{:S(2)}) collective-permute-start(bf16[1024,256]{1,0:T(8,128)(2,1)S(1)} %collective-permute-done.1.refs_6_), channel_id=1, source_target_pairs={{0,1},{1,0},{2,3},{3,2},{4,5},{5,4},{6,7},{7,6},{8,9},{9,8},{10,11... | collective-permute-start | bytes 1572872 | tf_op jit(solution)/shard_map/ppermute | solution.py:268
  34.4 0.0 collective-permute-done.5.refs_5_
  34.4 1.3 %late_blocks.1.acc_ref = f32[1024,512]{1,0:T(8,128)S(1)} custom-call(f32[1024,512]{1,0:T(8,128)S(1)} %get-tuple-element.21.refs_0_, bf16[1792,256]{1,0:T(8,128)(2,1)S(1)} %get-tuple-element.17.rest_key_ref.refs_1_, bf16[1792,256]{1,0:T(8,128)(2,1)S(1)} %get-tuple-element.22.refs_2_, bf16[1024,256]{1,0:T(8,128)(2,1)S(1)} %collective-permute-done.2.refs_3_, ...), custom_call_target="tpu_custom_call" | custom-call | tf_op jit(solution)/shard_map/late_blocks/pallas_call | solution.py:364
  35.7 0.6 collective-permute-done.6.refs_0_
  36.3 4.0 %local_sums.1 = bf16[3200,128]{1,0:T(8,128)(2,1)S(1)} custom-call(s32[32]{0:T(128)S(1)} %copy-done.6, f32[1024,512]{1,0:T(8,128)S(1)} %late_blocks.1.acc_ref, bf16[1024,256]{1,0:T(8,128)(2,1)S(1)} %collective-permute-done.6.refs_0_, bf16[1792,256]{1,0:T(8,128)(2,1)S(1)} %get-tuple-element.17.rest_key_ref.refs_1_, ...), custom_call_target="tpu_custom_call" | custom-call | tf_op jit(solution)/shard_map/local_sums/pallas_call | solution.py:372
  40.3 18.8 %all_to_all.34 = bf16[8,400,128]{2,1,0:T(8,128)(2,1)S(1)} all-to-all(bf16[8,400,128]{2,1,0:T(8,128)(2,1)S(1)} %bitcast.17), channel_id=1, replica_groups={{0,8,16,24,32,40,48,56},{2,10,18,26,34,42,50,58},{4,12,20,28,36,44,52,6..., dimensions={0} | all-to-all | bytes 1638400 | tf_op jit(solution)/shard_map/all_to_all | solution.py:319
  59.1 0.8 line_sums.1
  59.9 15.3 %all_to_all.35 = bf16[8,8,896]{2,1,0:T(8,128)(2,1)S(1)} all-to-all(bf16[8,8,896]{2,1,0:T(8,128)(2,1)S(1)} %bitcast.25), channel_id=1, replica_groups={{0,64,128,192,256,320,384,448},{2,66,130,194,258,322,386,450},{4,68,132..., dimensions={0} | all-to-all | bytes 229376 | tf_op jit(solution)/shard_map/all_to_all | solution.py:319
  75.2 0.3 final_sums.1
  75.6 21.2 %all_to_all.36 = bf16[64,8,512]{2,1,0:T(8,128)(2,1)S(1)} all-to-all(bf16[64,8,512]{2,1,0:T(8,128)(2,1)S(1)} %bitcast.23), channel_id=1, replica_groups={{0,64,128,192,256,320,384,448,8,72,136,200,264,328,392,456,16,80,144,20..., dimensions={0} | all-to-all | bytes 1048576 | tf_op jit(solution)/shard_map/all_to_all | solution.py:319
  96.7 0.8 fusion
  (7 shorter events, 0.0 us)
Async XLA Ops:
  0.6 19.4 %collective-permute-start = (bf16[1024,256]{1,0:T(8,128)(2,1)}, bf16[1024,256]{1,0:T(8,128)(2,1)S(1)}, u32[]{:S(2)}, u32[]{:S(2)}) collective-permute-start(bf16[1024,256]{1,0:T(8,128)(2,1)} %bitcast.18), channel_id=1, source_target_pairs={{0,2},{1,7},{2,4},{3,1},{4,6},{5,3},{6,0},{7,5},{8,10},{9,15},{10,... | collective-permute-start | bytes 1572872 | tf_op jit(solution)/shard_map/ppermute | solution.py:290
  8.6 1.0 %copy-start = (bf16[32,32,256]{2,1,0:T(8,128)(2,1)S(1)}, bf16[32,32,256]{2,1,0:T(8,128)(2,1)}, u32[]{:S(2)}) copy-start(bf16[32,32,256]{2,1,0:T(8,128)(2,1)} %param.7) | copy-start | bytes 1572868
  9.6 1.2 %copy-start.4 = (bf16[2048,256]{1,0:T(8,128)(2,1)S(1)}, bf16[2048,256]{1,0:T(8,128)(2,1)}, u32[]{:S(2)}) copy-start(bf16[2048,256]{1,0:T(8,128)(2,1)} %wk_ref.1) | copy-start | bytes 3145732
  10.8 19.1 %copy-start.1 = (bf16[2048,256]{1,0:T(8,128)(2,1)S(1)}, bf16[2048,256]{1,0:T(8,128)(2,1)}, u32[]{:S(2)}) copy-start(bf16[2048,256]{1,0:T(8,128)(2,1)} %wv_ref.1) | copy-start | bytes 3145732
  11.7 15.8 %collective-permute-start.4 = (bf16[1024,256]{1,0:T(8,128)(2,1)S(1)}, bf16[1024,256]{1,0:T(8,128)(2,1)S(1)}, u32[]{:S(2)}, u32[]{:S(2)}) collective-permute-start(bf16[1024,256]{1,0:T(8,128)(2,1)S(1)} %bitcast.20), channel_id=1, source_target_pairs={{0,6},{1,3},{2,0},{3,5},{4,2},{5,7},{6,4},{7,1},{8,14},{9,11},{10,... | collective-permute-start | bytes 1572872 | tf_op jit(solution)/shard_map/ppermute | solution.py:290
  13.6 16.3 %collective-permute-start.3 = (bf16[1024,256]{1,0:T(8,128)(2,1)S(1)}, bf16[1024,256]{1,0:T(8,128)(2,1)S(1)}, u32[]{:S(2)}, u32[]{:S(2)}) collective-permute-start(bf16[1024,256]{1,0:T(8,128)(2,1)S(1)} %bitcast.21), channel_id=1, source_target_pairs={{0,1},{1,0},{2,3},{3,2},{4,5},{5,4},{6,7},{7,6},{8,9},{9,8},{10,11... | collective-permute-start | bytes 1572872 | tf_op jit(solution)/shard_map/ppermute | solution.py:268
  20.1 12.3 %collective-permute-start.1 = (bf16[1024,256]{1,0:T(8,128)(2,1)S(1)}, bf16[1024,256]{1,0:T(8,128)(2,1)S(1)}, u32[]{:S(2)}, u32[]{:S(2)}) collective-permute-start(bf16[1024,256]{1,0:T(8,128)(2,1)S(1)} %collective-permute-done.refs_1_), channel_id=1, source_target_pairs={{0,2},{1,7},{2,4},{3,1},{4,6},{5,3},{6,0},{7,5},{8,10},{9,15},{10,... | collective-permute-start | bytes 1572872 | tf_op jit(solution)/shard_map/ppermute | solution.py:290
  25.5 6.8 %collective-permute-start.2 = (bf16[1024,256]{1,0:T(8,128)(2,1)S(1)}, bf16[1024,256]{1,0:T(8,128)(2,1)S(1)}, u32[]{:S(2)}, u32[]{:S(2)}) collective-permute-start(bf16[1024,256]{1,0:T(8,128)(2,1)S(1)} %collective-permute-done.refs_1_), channel_id=1, source_target_pairs={{0,1},{1,0},{2,3},{3,2},{4,5},{5,4},{6,7},{7,6},{8,9},{9,8},{10,11... | collective-permute-start | bytes 1572872 | tf_op jit(solution)/shard_map/ppermute | solution.py:268
  27.5 6.9 %collective-permute-start.5 = (bf16[1024,256]{1,0:T(8,128)(2,1)S(1)}, bf16[1024,256]{1,0:T(8,128)(2,1)S(1)}, u32[]{:S(2)}, u32[]{:S(2)}) collective-permute-start(bf16[1024,256]{1,0:T(8,128)(2,1)S(1)} %collective-permute-done.4.refs_4_), channel_id=1, source_target_pairs={{0,1},{1,0},{2,3},{3,2},{4,5},{5,4},{6,7},{7,6},{8,9},{9,8},{10,11... | collective-permute-start | bytes 1572872 | tf_op jit(solution)/shard_map/ppermute | solution.py:268
  29.9 1.0 copy-start.2
  32.3 4.0 %copy-start.3 = (bf16[512,256]{1,0:T(8,128)(2,1)S(1)}, bf16[512,256]{1,0:T(8,128)(2,1)}, u32[]{:S(2)}) copy-start(bf16[512,256]{1,0:T(8,128)(2,1)} %refs_4_.1) | copy-start | bytes 786436
  32.3 4.0 %copy-start.5 = (bf16[512,256]{1,0:T(8,128)(2,1)S(1)}, bf16[512,256]{1,0:T(8,128)(2,1)}, u32[]{:S(2)}) copy-start(bf16[512,256]{1,0:T(8,128)(2,1)} %refs_3_.1) | copy-start | bytes 786436
  32.4 4.0 %copy-start.6 = (s32[32]{0:T(128)S(1)}, s32[32]{0:T(128)}, u32[]{:S(2)}) copy-start(s32[32]{0:T(128)} %owner_ref.1) | copy-start | bytes 388
  32.4 3.9 %collective-permute-start.6 = (bf16[1024,256]{1,0:T(8,128)(2,1)S(1)}, bf16[1024,256]{1,0:T(8,128)(2,1)S(1)}, u32[]{:S(2)}, u32[]{:S(2)}) collective-permute-start(bf16[1024,256]{1,0:T(8,128)(2,1)S(1)} %collective-permute-done.1.refs_6_), channel_id=1, source_target_pairs={{0,1},{1,0},{2,3},{3,2},{4,5},{5,4},{6,7},{7,6},{8,9},{9,8},{10,11... | collective-permute-start | bytes 1572872 | tf_op jit(solution)/shard_map/ppermute | solution.py:268
